TPU v7x, 32 devices: a whole 2x2x4 slice. The times are simulated.
32 devices in a mesh: row: 8 (over y, x, core), col: 4 (over z).
Axes of the slice: x: 2, y: 2, z: 4, core: 2. Of those that a mesh axis runs over, the one named last changes fastest.
Arguments:
- inputs: bfloat16 [8192, 1536], P(('row', 'col')), may hold values from -6 to 6
- text_states: bfloat16 [8, 64, 1536], P('row', 'col'), may hold values from -6 to 6
- cotangent: float32 [8192, 1536], P(('row', 'col')), may hold values from -6 to 6
- norm_gains: float32 [2, 3, 1536], replicated, may hold values from 0.25 to 1.75
- norm_shifts: float32 [2, 3, 1536], replicated, may hold values from -3 to 3
- self_query: bfloat16 [2, 1536, 1536], P(None, 'row', 'col'), may hold values from -0.15625 to 0.15625
- self_key: bfloat16 [2, 1536, 1536], P(None, 'row', 'col'), may hold values from -0.15625 to 0.15625
- self_value: bfloat16 [2, 1536, 1536], P(None, 'row', 'col'), may hold values from -0.15625 to 0.15625
- self_out: bfloat16 [2, 1536, 1536], P(None, 'row', 'col'), may hold values from -1.75 to 1.75
- cross_query: bfloat16 [2, 1536, 1536], P(None, 'row', 'col'), may hold values from -0.15625 to 0.15625
- cross_key: bfloat16 [2, 1536, 1536], P(None, 'row', 'col'), may hold values from -0.15625 to 0.15625
- cross_value: bfloat16 [2, 1536, 1536], P(None, 'row', 'col'), may hold values from -0.15625 to 0.15625
- cross_out: bfloat16 [2, 1536, 1536], P(None, 'row', 'col'), may hold values from -0.4375 to 0.4375
- mlp_up: bfloat16 [2, 1536, 6144], P(None, 'row', 'col'), may hold values from -0.15625 to 0.15625
- mlp_down: bfloat16 [2, 1536, 6144], P(None, 'row', 'col'), may hold values from -0.078125 to 0.078125
Outputs:
- output: float32 [8192, 1536], P(('row', 'col'))
- input_grad: float32 [8192, 1536], P(('row', 'col'))
- text_grad: float32 [8, 64, 1536], P('row', 'col')
- norm_gains_grad: float32 [2, 3, 1536], replicated
- norm_shifts_grad: float32 [2, 2, 1536], replicated
- self_norm_shift_grad: float32 [2, 1536], replicated
- self_query_grad: float32 [2, 1536, 1536], P(None, 'row', 'col')
- self_key_grad: float32 [2, 1536, 1536], P(None, 'row', 'col')
- self_value_grad: float32 [2, 1536, 1536], P(None, 'row', 'col')
- self_out_grad: float32 [2, 1536, 1536], P(None, 'row', 'col')
- cross_query_grad: float32 [2, 1536, 1536], P(None, 'row', 'col')
- cross_key_grad: float32 [2, 1536, 1536], P(None, 'row', 'col')
- cross_value_grad: float32 [2, 1536, 1536], P(None, 'row', 'col')
- cross_out_grad: float32 [2, 1536, 1536], P(None, 'row', 'col')
- mlp_up_grad: float32 [2, 1536, 6144], P(None, 'row', 'col')
- mlp_down_grad: float32 [2, 1536, 6144], P(None, 'row', 'col')
All inputs are finite; a program needn't handle non-finite values.
Results may differ from a plain program's by a relative error of at most 0.024.
Values may be sent and summed in bfloat16 or wider, within the bound.
No kernel may reach another device: no remote copies, remote signals or barrier semaphores. Data moves between devices by JAX's collectives and lax.ppermute only.
A program may use at most 320 MiB of HBM per device.

v0:
```python
import jax
import jax.numpy as jnp
from jax import lax
from jax.sharding import PartitionSpec as P

HEAD = 64
CLIP_LEN = 1024
LAYERS = 2


SCALE = 0.125
EPS = 1e-05
NEG = -1e30


def as_sent(array):
    return jax.tree.map(lambda a: a.astype(jnp.bfloat16) if a.dtype == jnp.float32 else a, array)


def product(left, right):
    return jnp.dot(left, right, preferred_element_type=jnp.float32)


def product_tn(left, right):
    return lax.dot_general(
        left, right, (((0,), (0,)), ((), ())), preferred_element_type=jnp.float32
    )


def product_nt(left, right):
    return lax.dot_general(
        left, right, (((1,), (1,)), ((), ())), preferred_element_type=jnp.float32
    )


def gelu_exact(value_in):
    return jax.nn.gelu(value_in, approximate=False)


def norm_forward(residual, gain, shift):
    row_mean = jnp.mean(residual, axis=1, keepdims=True)
    centered = residual - row_mean
    variance = jnp.mean(centered * centered, axis=1, keepdims=True)
    inv_std = lax.rsqrt(variance + EPS)
    normed = centered * inv_std
    return (normed, inv_std, (normed * gain + shift).astype(jnp.bfloat16))


def norm_backward(grad_out, normed, inv_std, gain):
    scaled = grad_out * gain
    row_mean = jnp.mean(scaled, axis=1, keepdims=True)
    row_along = jnp.mean(scaled * normed, axis=1, keepdims=True)
    grad_in = inv_std * (scaled - row_mean - normed * row_along)
    return (grad_in, jnp.sum(grad_out * normed, axis=0), jnp.sum(grad_out, axis=0))


def full_rows(local_part):
    return jax.tree.map(
        lambda part, own: part.astype(own.dtype),
        lax.all_gather(as_sent(local_part), "col", axis=0, tiled=True),
        local_part,
    )


def split_sum(partial_value):
    return lax.psum_scatter(
        partial_value.astype(jnp.bfloat16), "col", scatter_dimension=0, tiled=True
    ).astype(jnp.float32)


def text_split(partial_value):
    return lax.psum_scatter(
        partial_value.astype(jnp.bfloat16), "col", scatter_dimension=1, tiled=True
    ).astype(jnp.float32)


def inner_weights(w_query, w_key, w_value, w_cross_query, w_cross_key, w_cross_value, w_up):
    return (
        lax.all_gather(w_query, "row", axis=0, tiled=True),
        lax.all_gather(w_key, "row", axis=0, tiled=True),
        lax.all_gather(w_value, "row", axis=0, tiled=True),
        lax.all_gather(w_cross_query, "row", axis=0, tiled=True),
        lax.all_gather(w_cross_key, "row", axis=0, tiled=True),
        lax.all_gather(w_cross_value, "row", axis=0, tiled=True),
        lax.all_gather(w_up, "row", axis=0, tiled=True),
    )


def outer_weights(w_self_out, w_cross_out, w_down):
    return (
        lax.all_gather(w_self_out, "row", axis=0, tiled=True),
        lax.all_gather(w_cross_out, "row", axis=0, tiled=True),
        lax.all_gather(w_down, "row", axis=0, tiled=True),
    )


def block_scores(row_block, keys_all, row_start, causal):
    scores = (
        jnp.einsum("qhd,khd->hqk", row_block, keys_all, preferred_element_type=jnp.float32) * SCALE
    )
    if causal:
        shape_pair = (row_block.shape[0], keys_all.shape[0])
        row_ids = row_start + lax.broadcasted_iota(jnp.int32, shape_pair, 0)
        key_ids = lax.broadcasted_iota(jnp.int32, shape_pair, 1)
        scores = jnp.where((key_ids <= row_ids)[None], scores, NEG)
    return scores


def attend_forward(queries, keys_all, values_all, causal):
    block_rows = min(512, queries.shape[0])
    outputs = []
    log_sums = []
    for row_start in range(0, queries.shape[0], block_rows):
        row_block = queries[row_start : row_start + block_rows]
        scores = block_scores(row_block, keys_all, row_start, causal)
        row_max = jnp.max(scores, axis=2, keepdims=True)
        shifted_exp = jnp.exp(scores - row_max)
        row_sum = jnp.sum(shifted_exp, axis=2, keepdims=True)
        attn_probs = (shifted_exp / row_sum).astype(jnp.bfloat16)
        outputs.append(
            jnp.einsum("hqk,khd->qhd", attn_probs, values_all, preferred_element_type=jnp.float32)
        )
        log_sums.append(row_max + jnp.log(row_sum))
    return (jnp.concatenate(outputs, axis=0), jnp.concatenate(log_sums, axis=1))


def attend_backward(queries, keys_all, values_all, log_sums, grad_out, causal):
    block_rows = min(512, queries.shape[0])
    grad_queries = []
    grad_keys = jnp.zeros(keys_all.shape, jnp.float32)
    grad_values = jnp.zeros(values_all.shape, jnp.float32)
    for row_start in range(0, queries.shape[0], block_rows):
        row_block = queries[row_start : row_start + block_rows]
        grad_block = grad_out[row_start : row_start + block_rows]
        scores = block_scores(row_block, keys_all, row_start, causal)
        attn_probs = jnp.exp(scores - log_sums[:, row_start : row_start + block_rows])
        grad_probs = jnp.einsum(
            "qhd,khd->hqk", grad_block, values_all, preferred_element_type=jnp.float32
        )
        row_inner = jnp.sum(attn_probs * grad_probs, axis=2, keepdims=True)
        grad_scores = (attn_probs * (grad_probs - row_inner)).astype(jnp.bfloat16)
        grad_queries.append(
            jnp.einsum("hqk,khd->qhd", grad_scores, keys_all, preferred_element_type=jnp.float32)
            * SCALE
        )
        grad_keys = (
            grad_keys
            + jnp.einsum("hqk,qhd->khd", grad_scores, row_block, preferred_element_type=jnp.float32)
            * SCALE
        )
        grad_values = grad_values + jnp.einsum(
            "hqk,qhd->khd",
            attn_probs.astype(jnp.bfloat16),
            grad_block,
            preferred_element_type=jnp.float32,
        )
    return (jnp.concatenate(grad_queries, axis=0), grad_keys, grad_values)


def clip_shapes(queries, keys_all):
    clip_count = queries.shape[0] // CLIP_LEN
    head_count = queries.shape[1] // HEAD
    return (
        (clip_count, CLIP_LEN, head_count, HEAD),
        (clip_count, keys_all.shape[0] // clip_count, head_count, HEAD),
    )


def attention(queries, keys_all, values_all, causal):
    query_shape, key_shape = clip_shapes(queries, keys_all)

    def one_clip(clip_args):
        return attend_forward(clip_args[0], clip_args[1], clip_args[2], causal)

    outputs, log_sums = lax.map(
        one_clip,
        (queries.reshape(query_shape), keys_all.reshape(key_shape), values_all.reshape(key_shape)),
    )
    return (outputs.reshape(queries.shape), log_sums)


def attention_grad(queries, keys_all, values_all, log_sums, grad_out, causal):
    query_shape, key_shape = clip_shapes(queries, keys_all)

    def one_clip(clip_args):
        return attend_backward(
            clip_args[0], clip_args[1], clip_args[2], clip_args[3], clip_args[4], causal
        )

    grad_queries, grad_keys, grad_values = lax.map(
        one_clip,
        (
            queries.reshape(query_shape),
            keys_all.reshape(key_shape),
            values_all.reshape(key_shape),
            log_sums,
            grad_out.reshape(query_shape),
        ),
    )
    return (
        grad_queries.reshape(queries.shape).astype(jnp.bfloat16),
        grad_keys.reshape(keys_all.shape).astype(jnp.bfloat16),
        grad_values.reshape(values_all.shape).astype(jnp.bfloat16),
    )


def layer_forward(residual, text_full, inner_set, outer_set, gains, shifts):
    w_query, w_key, w_value, w_cross_query, w_cross_key, w_cross_value, w_up = inner_set
    w_self_out, w_cross_out, w_down = outer_set
    normed_one, inv_one, low_one = norm_forward(residual, gains[0], shifts[0])
    full_one = full_rows(low_one)
    queries = product(full_one, w_query).astype(jnp.bfloat16)
    keys_self = product(full_one, w_key).astype(jnp.bfloat16)
    values_self = product(full_one, w_value).astype(jnp.bfloat16)
    attn_out, sums_self = attention(queries, keys_self, values_self, True)
    attn_low = attn_out.astype(jnp.bfloat16)
    residual = residual + split_sum(product_nt(attn_low, w_self_out))
    normed_two, inv_two, low_two = norm_forward(residual, gains[1], shifts[1])
    full_two = full_rows(low_two)
    cross_queries = product(full_two, w_cross_query).astype(jnp.bfloat16)
    cross_keys = product(text_full, w_cross_key).astype(jnp.bfloat16)
    cross_values = product(text_full, w_cross_value).astype(jnp.bfloat16)
    cross_att, sums_cross = attention(cross_queries, cross_keys, cross_values, False)
    cross_low = cross_att.astype(jnp.bfloat16)
    residual = residual + split_sum(product_nt(cross_low, w_cross_out))
    normed_three, inv_three, low_three = norm_forward(residual, gains[2], shifts[2])
    full_three = full_rows(low_three)
    hidden_pre = product(full_three, w_up)
    hidden_low = gelu_exact(hidden_pre).astype(jnp.bfloat16)
    residual = residual + split_sum(product_nt(hidden_low, w_down))
    stored = dict(
        normed_one=normed_one,
        inv_one=inv_one,
        low_one=low_one,
        full_one=full_one,
        queries=queries,
        keys_self=keys_self,
        values_self=values_self,
        attn_low=attn_low,
        sums_self=sums_self,
        normed_two=normed_two,
        inv_two=inv_two,
        low_two=low_two,
        full_two=full_two,
        cross_queries=cross_queries,
        cross_keys=cross_keys,
        cross_values=cross_values,
        cross_low=cross_low,
        sums_cross=sums_cross,
        normed_three=normed_three,
        inv_three=inv_three,
        low_three=low_three,
        full_three=full_three,
        hidden_pre=hidden_pre,
    )
    return (residual, stored)


def layer_backward(gradient, text_full, inner_set, outer_set, gains, stored):
    w_query, w_key, w_value, w_cross_query, w_cross_key, w_cross_value, w_up = inner_set
    w_self_out, w_cross_out, w_down = outer_set
    full_one = full_rows(stored["low_one"])
    full_two = full_rows(stored["low_two"])
    full_three = full_rows(stored["low_three"])
    hidden_val, gelu_pull = jax.vjp(gelu_exact, stored["hidden_pre"])
    hidden_low = hidden_val.astype(jnp.bfloat16)
    grad_full_three = full_rows(gradient.astype(jnp.bfloat16))
    grad_hidden = product(grad_full_three, w_down)
    grad_pre = gelu_pull(grad_hidden)[0].astype(jnp.bfloat16)
    grad_normed = split_sum(product_nt(grad_pre, w_up))
    grad_res, gain_three, shift_three = norm_backward(
        grad_normed, stored["normed_three"], stored["inv_three"], gains[2]
    )
    gradient = gradient + grad_res
    grad_full_two = full_rows(gradient.astype(jnp.bfloat16))
    grad_cross = product(grad_full_two, w_cross_out).astype(jnp.bfloat16)
    grad_cquery, grad_ckeys, grad_cvalues = attention_grad(
        stored["cross_queries"],
        stored["cross_keys"],
        stored["cross_values"],
        stored["sums_cross"],
        grad_cross,
        False,
    )
    grad_normed = split_sum(product_nt(grad_cquery, w_cross_query))
    text_term = product_nt(grad_ckeys, w_cross_key) + product_nt(grad_cvalues, w_cross_value)
    grad_res, gain_two, shift_two = norm_backward(
        grad_normed, stored["normed_two"], stored["inv_two"], gains[1]
    )
    gradient = gradient + grad_res
    grad_full_one = full_rows(gradient.astype(jnp.bfloat16))
    grad_attn = product(grad_full_one, w_self_out).astype(jnp.bfloat16)
    grad_query, grad_keys, grad_values = attention_grad(
        stored["queries"],
        stored["keys_self"],
        stored["values_self"],
        stored["sums_self"],
        grad_attn,
        True,
    )
    grad_normed = split_sum(
        product_nt(grad_query, w_query)
        + product_nt(grad_keys, w_key)
        + product_nt(grad_values, w_value)
    )
    grad_res, gain_one, shift_one = norm_backward(
        grad_normed, stored["normed_one"], stored["inv_one"], gains[0]
    )
    gradient = gradient + grad_res
    attn_low = stored["attn_low"]
    cross_low = stored["cross_low"]
    row_count = full_one.shape[1] // lax.axis_size("row") * lax.axis_size("row")

    def columns(full_array):
        return lax.slice_in_dim(full_array, 0, row_count, axis=1)

    slice_one = columns(full_one)
    slice_two = columns(full_two)
    slice_text = columns(text_full)
    summed = lax.psum_scatter(
        jnp.concatenate(
            [
                product_tn(slice_one, grad_query),
                product_tn(slice_one, grad_keys),
                product_tn(slice_one, grad_values),
                product_tn(columns(grad_full_one), attn_low),
                product_tn(slice_two, grad_cquery),
                product_tn(slice_text, grad_ckeys),
                product_tn(slice_text, grad_cvalues),
                product_tn(columns(grad_full_two), cross_low),
                product_tn(columns(full_three), grad_pre),
                product_tn(columns(grad_full_three), hidden_low),
            ],
            axis=1,
        ).astype(jnp.bfloat16),
        "row",
        scatter_dimension=0,
        tiled=True,
    ).astype(jnp.float32)
    head_width = grad_query.shape[1]
    hidden_width = grad_pre.shape[1]
    weight_list = []
    position = 0
    for piece_width in [head_width] * 8 + [hidden_width] * 2:
        weight_list.append(summed[:, position : position + piece_width])
        position = position + piece_width
    gain_stack = jnp.stack([gain_one, gain_two, gain_three])
    shift_stack = jnp.stack([shift_one, shift_two, shift_three])
    return (gradient, text_term, weight_list, gain_stack, shift_stack)


def shards(
    inputs,
    text_states,
    cotangent,
    norm_gains,
    norm_shifts,
    self_query,
    self_key,
    self_value,
    self_out,
    cross_query,
    cross_key,
    cross_value,
    cross_out,
    mlp_up,
    mlp_down,
):
    text_gathered = lax.all_gather(text_states, "col", axis=1, tiled=True)
    text_full = text_gathered.reshape(-1, text_gathered.shape[2])
    residual = inputs.astype(jnp.float32)
    stored_list = []
    gathered = []
    for layer_index in range(LAYERS):
        inner_set = inner_weights(
            self_query[layer_index],
            self_key[layer_index],
            self_value[layer_index],
            cross_query[layer_index],
            cross_key[layer_index],
            cross_value[layer_index],
            mlp_up[layer_index],
        )
        outer_set = outer_weights(
            self_out[layer_index], cross_out[layer_index], mlp_down[layer_index]
        )
        residual, stored = layer_forward(
            residual,
            text_full,
            inner_set,
            outer_set,
            norm_gains[layer_index],
            norm_shifts[layer_index],
        )
        stored_list.append(stored)
        gathered.append((inner_set, outer_set))
    gradient = cotangent
    text_grad = jnp.zeros(text_states.shape, jnp.float32)
    weight_grads = [None] * LAYERS
    gain_grads = [None] * LAYERS
    shift_grads = [None] * LAYERS
    for layer_index in range(LAYERS - 1, -1, -1):
        inner_set = inner_weights(
            self_query[layer_index],
            self_key[layer_index],
            self_value[layer_index],
            cross_query[layer_index],
            cross_key[layer_index],
            cross_value[layer_index],
            mlp_up[layer_index],
        )
        outer_set = outer_weights(
            self_out[layer_index], cross_out[layer_index], mlp_down[layer_index]
        )
        gradient, text_term, weight_list, gain_stack, shift_stack = layer_backward(
            gradient,
            text_full,
            inner_set,
            outer_set,
            norm_gains[layer_index],
            stored_list[layer_index],
        )
        text_grad = text_grad + text_split(text_term.reshape(text_gathered.shape))
        weight_grads[layer_index] = weight_list
        gain_grads[layer_index] = gain_stack
        shift_grads[layer_index] = shift_stack
    gains_sum, shifts_sum = lax.psum(
        (jnp.stack(gain_grads), jnp.stack(shift_grads)), ("row", "col")
    )
    stacked = [
        jnp.stack([weight_grads[layer_index][slot] for layer_index in range(LAYERS)])
        for slot in range(10)
    ]
    return (
        residual,
        gradient,
        text_grad,
        gains_sum,
        shifts_sum[:, 1:],
        shifts_sum[:, 0],
        stacked[0],
        stacked[1],
        stacked[2],
        stacked[3],
        stacked[4],
        stacked[5],
        stacked[6],
        stacked[7],
        stacked[8],
        stacked[9],
    )


def solution(mesh):
    in_specs = (
        P(("row", "col"), None),
        P("row", "col", None),
        P(("row", "col"), None),
        P(),
        P(),
        P(None, "row", "col"),
        P(None, "row", "col"),
        P(None, "row", "col"),
        P(None, "row", "col"),
        P(None, "row", "col"),
        P(None, "row", "col"),
        P(None, "row", "col"),
        P(None, "row", "col"),
        P(None, "row", "col"),
        P(None, "row", "col"),
    )
    out_specs = (
        P(("row", "col"), None),
        P(("row", "col"), None),
        P("row", "col", None),
        P(),
        P(),
        P(),
        P(None, "row", "col"),
        P(None, "row", "col"),
        P(None, "row", "col"),
        P(None, "row", "col"),
        P(None, "row", "col"),
        P(None, "row", "col"),
        P(None, "row", "col"),
        P(None, "row", "col"),
        P(None, "row", "col"),
        P(None, "row", "col"),
    )
    return jax.shard_map(shards, mesh=mesh, in_specs=in_specs, out_specs=out_specs, check_vma=False)
```

profile of v0, /device:TPU:0, one launch (start us, length us, event | category | flops | bytes accessed | tf_op | source)
XLA Modules:
  0.0 2804.8 jit_solution(4538265825561260005)
XLA Ops:
  20.5 16.8 all-gather.79.cloned.1.call-done
  37.3 65.7 %all-gather.53.cloned.1.call-done = bf16[1024,1536]{1,0:T(8,128)(2,1)} async-done(((bf16[256,1536]{1,0:T(8,128)(2,1)}), bf16[1024,1536]{1,0:T(8,128)(2,1)}) %all-gather.53.cloned.1.call-update) | async-done | bytes 3145744 | tf_op jit(solution)/shard_map/all_gather | solution.py:60
  106.7 21.5 all-gather.81.cloned.1.call-done
  141.9 12.7 all-gather.77.cloned.1.call-done
  189.3 57.0 %reduce-scatter.21.cloned.1.call-done = bf16[256,1536]{1,0:T(8,128)(2,1)} async-done(((bf16[1024,1536]{1,0:T(8,128)(2,1)}), bf16[256,1536]{1,0:T(8,128)(2,1)}) %reduce-scatter.21.cloned.1.call-update) | async-done | bytes 786448 | tf_op jit(solution)/shard_map/reduce_scatter | solution.py:66
  251.6 13.9 all_gather.130
  274.6 24.8 all-gather.85.cloned.1.call-done
  301.8 24.2 all-gather.87.cloned.1.call-done
  326.0 65.5 %all-gather.55.cloned.1.call-done = bf16[1024,1536]{1,0:T(8,128)(2,1)} async-done(((bf16[256,1536]{1,0:T(8,128)(2,1)}), bf16[1024,1536]{1,0:T(8,128)(2,1)}) %all-gather.55.cloned.1.call-update) | async-done | bytes 3145744 | tf_op jit(solution)/shard_map/all_gather | solution.py:60
  398.3 18.4 all-gather.91.cloned.1.call-done
  424.2 58.0 %reduce-scatter.23.cloned.1.call-done = bf16[256,1536]{1,0:T(8,128)(2,1)} async-done(((bf16[1024,1536]{1,0:T(8,128)(2,1)}), bf16[256,1536]{1,0:T(8,128)(2,1)}) %reduce-scatter.23.cloned.1.call-update) | async-done | bytes 786448 | tf_op jit(solution)/shard_map/reduce_scatter | solution.py:66
  488.2 35.4 %all-gather.93.cloned.1.call-done = bf16[1,1536,1536]{2,1,0:T(8,128)(2,1)} async-done(((bf16[1,192,1536]{2,1,0:T(8,128)(2,1)}), bf16[1,1536,1536]{2,1,0:T(8,128)(2,1)}) %all-gather.93.cloned.1.call-update) | async-done | bytes 4718608 | tf_op jit(solution)/shard_map/all_gather | solution.py:85
  523.6 65.5 %all-gather.57.cloned.1.call-done = bf16[1024,1536]{1,0:T(8,128)(2,1)} async-done(((bf16[256,1536]{1,0:T(8,128)(2,1)}), bf16[1024,1536]{1,0:T(8,128)(2,1)}) %all-gather.57.cloned.1.call-update) | async-done | bytes 3145744 | tf_op jit(solution)/shard_map/all_gather | solution.py:60
  589.1 23.6 multiply_convert_fusion.5
  612.7 16.3 all-gather.95.cloned.1.call-done
  638.9 59.8 %reduce-scatter.25.cloned.1.call-done = bf16[256,1536]{1,0:T(8,128)(2,1)} async-done(((bf16[1024,1536]{1,0:T(8,128)(2,1)}), bf16[256,1536]{1,0:T(8,128)(2,1)}) %reduce-scatter.25.cloned.1.call-update) | async-done | bytes 786448 | tf_op jit(solution)/shard_map/reduce_scatter | solution.py:66
  704.8 19.8 all-gather.99.cloned.1.call-done
  724.5 65.5 %all-gather.59.cloned.1.call-done = bf16[1024,1536]{1,0:T(8,128)(2,1)} async-done(((bf16[256,1536]{1,0:T(8,128)(2,1)}), bf16[1024,1536]{1,0:T(8,128)(2,1)}) %all-gather.59.cloned.1.call-update) | async-done | bytes 3145744 | tf_op jit(solution)/shard_map/all_gather | solution.py:60
  793.9 20.9 all-gather.101.cloned.1.call-done
  874.1 58.3 %reduce-scatter.27.cloned.1.call-done = bf16[256,1536]{1,0:T(8,128)(2,1)} async-done(((bf16[1024,1536]{1,0:T(8,128)(2,1)}), bf16[256,1536]{1,0:T(8,128)(2,1)}) %reduce-scatter.27.cloned.1.call-update) | async-done | bytes 786448 | tf_op jit(solution)/shard_map/reduce_scatter | solution.py:66
  936.2 22.7 all-gather.109.cloned.1.call-done
  960.7 24.1 all-gather.105.cloned.1.call-done
  986.5 24.2 all-gather.107.cloned.1.call-done
  1010.8 65.5 %all-gather.61.cloned.1.call-done = bf16[1024,1536]{1,0:T(8,128)(2,1)} async-done(((bf16[256,1536]{1,0:T(8,128)(2,1)}), bf16[1024,1536]{1,0:T(8,128)(2,1)}) %all-gather.61.cloned.1.call-update) | async-done | bytes 3145744 | tf_op jit(solution)/shard_map/all_gather | solution.py:60
  1082.2 18.6 all-gather.111.cloned.1.call-done
  1106.4 59.6 %reduce-scatter.29.cloned.1.call-done = bf16[256,1536]{1,0:T(8,128)(2,1)} async-done(((bf16[1024,1536]{1,0:T(8,128)(2,1)}), bf16[256,1536]{1,0:T(8,128)(2,1)}) %reduce-scatter.29.cloned.1.call-update) | async-done | bytes 786448 | tf_op jit(solution)/shard_map/reduce_scatter | solution.py:66
  1172.6 34.8 %all-gather.113.cloned.1.call-done = bf16[1,1536,1536]{2,1,0:T(8,128)(2,1)} async-done(((bf16[1,192,1536]{2,1,0:T(8,128)(2,1)}), bf16[1,1536,1536]{2,1,0:T(8,128)(2,1)}) %all-gather.113.cloned.1.call-update) | async-done | bytes 4718608 | tf_op jit(solution)/shard_map/all_gather | solution.py:85
  1207.4 65.5 %all-gather.63.cloned.1.call-done = bf16[1024,1536]{1,0:T(8,128)(2,1)} async-done(((bf16[256,1536]{1,0:T(8,128)(2,1)}), bf16[1024,1536]{1,0:T(8,128)(2,1)}) %all-gather.63.cloned.1.call-update) | async-done | bytes 3145744 | tf_op jit(solution)/shard_map/all_gather | solution.py:60
  1272.9 23.6 multiply_convert_fusion.4
  1296.6 40.7 %all-gather.65.cloned.1.call-done = bf16[1024,1536]{1,0:T(8,128)(2,1)} async-done(((bf16[256,1536]{1,0:T(8,128)(2,1)}), bf16[1024,1536]{1,0:T(8,128)(2,1)}) %all-gather.65.cloned.1.call-update) | async-done | bytes 3145744 | tf_op jit(solution)/shard_map/all_gather | solution.py:60
  1337.3 40.1 %all-gather.115.cloned.1.call-done = bf16[1,1536,1536]{2,1,0:T(8,128)(2,1)} async-done(((bf16[1,192,1536]{2,1,0:T(8,128)(2,1)}), bf16[1,1536,1536]{2,1,0:T(8,128)(2,1)}) %all-gather.115.cloned.1.call-update) | async-done | bytes 4718608 | tf_op jit(solution)/shard_map/all_gather | solution.py:93
  1407.3 51.0 %reduce-scatter.33.cloned.1.call-done = bf16[256,1536]{1,0:T(8,128)(2,1)} async-done(((bf16[1024,1536]{1,0:T(8,128)(2,1)}), bf16[256,1536]{1,0:T(8,128)(2,1)}) %reduce-scatter.33.cloned.1.call-update) | async-done | bytes 786448 | tf_op jit(solution)/shard_map/reduce_scatter | solution.py:66
  1460.7 60.2 %reduce-scatter.31.cloned.1.call-done = bf16[256,1536]{1,0:T(8,128)(2,1)} async-done(((bf16[1024,1536]{1,0:T(8,128)(2,1)}), bf16[256,1536]{1,0:T(8,128)(2,1)}) %reduce-scatter.31.cloned.1.call-update) | async-done | bytes 786448 | tf_op jit(solution)/shard_map/reduce_scatter | solution.py:66
  1525.7 63.4 %all-gather.67.cloned.1.call-done = bf16[1024,1536]{1,0:T(8,128)(2,1)} async-done(((bf16[256,1536]{1,0:T(8,128)(2,1)}), bf16[1024,1536]{1,0:T(8,128)(2,1)}) %all-gather.67.cloned.1.call-update) | async-done | bytes 3145744 | tf_op jit(solution)/shard_map/all_gather | solution.py:60
  1600.5 59.0 %reduce-scatter.35.cloned.1.call-done = bf16[256,1536]{1,0:T(8,128)(2,1)} async-done(((bf16[1024,1536]{1,0:T(8,128)(2,1)}), bf16[256,1536]{1,0:T(8,128)(2,1)}) %reduce-scatter.35.cloned.1.call-update) | async-done | bytes 786448 | tf_op jit(solution)/shard_map/reduce_scatter | solution.py:66
  1665.3 63.6 %all-gather.69.cloned.1.call-done = bf16[1024,1536]{1,0:T(8,128)(2,1)} async-done(((bf16[256,1536]{1,0:T(8,128)(2,1)}), bf16[1024,1536]{1,0:T(8,128)(2,1)}) %all-gather.69.cloned.1.call-update) | async-done | bytes 3145744 | tf_op jit(solution)/shard_map/all_gather | solution.py:60
  1796.5 59.0 %reduce-scatter.37.cloned.1.call-done = bf16[256,1536]{1,0:T(8,128)(2,1)} async-done(((bf16[1024,1536]{1,0:T(8,128)(2,1)}), bf16[256,1536]{1,0:T(8,128)(2,1)}) %reduce-scatter.37.cloned.1.call-update) | async-done | bytes 786448 | tf_op jit(solution)/shard_map/reduce_scatter | solution.py:66
  1861.2 63.6 %all-gather.71.cloned.1.call-done = bf16[1024,1536]{1,0:T(8,128)(2,1)} async-done(((bf16[256,1536]{1,0:T(8,128)(2,1)}), bf16[1024,1536]{1,0:T(8,128)(2,1)}) %all-gather.71.cloned.1.call-update) | async-done | bytes 3145744 | tf_op jit(solution)/shard_map/all_gather | solution.py:60
  1924.9 12.3 add_convert_fusion.1
  1947.8 59.0 %reduce-scatter.39.cloned.1.call-done = bf16[256,1536]{1,0:T(8,128)(2,1)} async-done(((bf16[1024,1536]{1,0:T(8,128)(2,1)}), bf16[256,1536]{1,0:T(8,128)(2,1)}) %reduce-scatter.39.cloned.1.call-update) | async-done | bytes 786448 | tf_op jit(solution)/shard_map/reduce_scatter | solution.py:66
  2012.7 63.5 %all-gather.73.cloned.1.call-done = bf16[1024,1536]{1,0:T(8,128)(2,1)} async-done(((bf16[256,1536]{1,0:T(8,128)(2,1)}), bf16[1024,1536]{1,0:T(8,128)(2,1)}) %all-gather.73.cloned.1.call-update) | async-done | bytes 3145744 | tf_op jit(solution)/shard_map/all_gather | solution.py:60
  2087.6 59.0 %reduce-scatter.41.cloned.1.call-done = bf16[256,1536]{1,0:T(8,128)(2,1)} async-done(((bf16[1024,1536]{1,0:T(8,128)(2,1)}), bf16[256,1536]{1,0:T(8,128)(2,1)}) %reduce-scatter.41.cloned.1.call-update) | async-done | bytes 786448 | tf_op jit(solution)/shard_map/reduce_scatter | solution.py:66
  2153.7 62.8 %all-gather.75.cloned.1.call-done = bf16[1024,1536]{1,0:T(8,128)(2,1)} async-done(((bf16[256,1536]{1,0:T(8,128)(2,1)}), bf16[1024,1536]{1,0:T(8,128)(2,1)}) %all-gather.75.cloned.1.call-update) | async-done | bytes 3145744 | tf_op jit(solution)/shard_map/all_gather | solution.py:60
  2331.6 24.7 copy.116
  2397.8 26.2 copy.114
  2425.6 90.2 %reduce-scatter.51.cloned.1.call-done = bf16[192,6144]{1,0:T(8,128)(2,1)} async-done(((bf16[1536,6144]{1,0:T(8,128)(2,1)}), bf16[192,6144]{1,0:T(8,128)(2,1)}) %reduce-scatter.51.cloned.1.call-update) | async-done | bytes 2359312
  2528.8 113.1 %all-reduce.3.cloned.1.call-done = (f32[2,3,1536]{2,1,0:T(4,128)}, f32[2,3,1536]{2,0,1:T(2,128)}) async-done(((f32[2,3,1536]{2,1,0:T(4,128)}, f32[2,3,1536]{2,0,1:T(2,128)}), (f32[2,3,1536]{2,1,0:T(4,128)}, f32[2,3,1536]{2,0,1:T(2,128)})) %all-reduce.3.cloned.1.call-update) | async-done | bytes 73744 | tf_op jit(solution)/shard_map/psum | solution.py:427
  2646.0 127.3 %reduce-scatter.49.cloned.1.call-done = bf16[192,6144]{1,0:T(8,128)(2,1)} async-done(((bf16[1536,6144]{1,0:T(8,128)(2,1)}), bf16[192,6144]{1,0:T(8,128)(2,1)}) %reduce-scatter.49.cloned.1.call-update) | async-done | bytes 2359312
  (847 shorter events, 565.2 us)
Async XLA Ops:
  9.1 93.9 %all-gather.53.cloned.1.call-start = ((), (), s32[]{:S(2)}) async-start(), calls=%async_computation.16 | async-start | bytes 3932160 | tf_op jit(solution)/shard_map/all_gather | solution.py:60
  17.4 110.8 %all-gather.81.cloned.1.call-start = ((), (), s32[]{:S(2)}) async-start(), calls=%async_computation.44 | async-start | bytes 1327104 | tf_op jit(solution)/shard_map/all_gather | solution.py:80
  18.2 136.4 %all-gather.77.cloned.1.call-start = ((), (), s32[]{:S(2)}) async-start(), calls=%async_computation.42 | async-start | bytes 1327104 | tf_op jit(solution)/shard_map/all_gather | solution.py:81
  19.0 161.9 %all-gather.83.cloned.1.call-start = ((), (), s32[]{:S(2)}) async-start(), calls=%async_computation.45 | async-start | bytes 1327104 | tf_op jit(solution)/shard_map/all_gather | solution.py:91
  19.9 226.4 %reduce-scatter.21.cloned.1.call-start = ((), (), s32[]{:S(2)}) async-start(), calls=%async_computation.17 | async-start | bytes 3932160 | tf_op jit(solution)/shard_map/reduce_scatter | solution.py:66
  185.9 87.0 %all-gather.89.cloned.1.call-start = ((), (), s32[]{:S(2)}) async-start(), calls=%async_computation.48 | async-start | bytes 1327104 | tf_op jit(solution)/shard_map/all_gather | solution.py:83
  187.6 111.8 %all-gather.85.cloned.1.call-start = ((), (), s32[]{:S(2)}) async-start(), calls=%async_computation.46 | async-start | bytes 1327104 | tf_op jit(solution)/shard_map/all_gather | solution.py:84
  188.4 137.6 %all-gather.87.cloned.1.call-start = ((), (), s32[]{:S(2)}) async-start(), calls=%async_computation.47 | async-start | bytes 1327104 | tf_op jit(solution)/shard_map/all_gather | solution.py:82
  189.2 202.3 %all-gather.55.cloned.1.call-start = ((), (), s32[]{:S(2)}) async-start(), calls=%async_computation.18 | async-start | bytes 3932160 | tf_op jit(solution)/shard_map/all_gather | solution.py:60
  250.7 166.0 %all-gather.91.cloned.1.call-start = ((), (), s32[]{:S(2)}) async-start(), calls=%async_computation.49 | async-start | bytes 1327104 | tf_op jit(solution)/shard_map/all_gather | solution.py:92
  251.5 230.6 %reduce-scatter.23.cloned.1.call-start = ((), (), s32[]{:S(2)}) async-start(), calls=%async_computation.19 | async-start | bytes 3932160 | tf_op jit(solution)/shard_map/reduce_scatter | solution.py:66
  421.7 101.8 %all-gather.93.cloned.1.call-start = ((), (), s32[]{:S(2)}) async-start(), calls=%async_computation.50 | async-start | bytes 5308416 | tf_op jit(solution)/shard_map/all_gather | solution.py:85
  424.1 165.0 %all-gather.57.cloned.1.call-start = ((), (), s32[]{:S(2)}) async-start(), calls=%async_computation.20 | async-start | bytes 3932160 | tf_op jit(solution)/shard_map/all_gather | solution.py:60
  485.3 143.8 %all-gather.95.cloned.1.call-start = ((), (), s32[]{:S(2)}) async-start(), calls=%async_computation.51 | async-start | bytes 5308416 | tf_op jit(solution)/shard_map/all_gather | solution.py:93
  487.7 211.0 %reduce-scatter.25.cloned.1.call-start = ((), (), s32[]{:S(2)}) async-start(), calls=%async_computation.21 | async-start | bytes 3932160 | tf_op jit(solution)/shard_map/reduce_scatter | solution.py:66
  638.3 86.2 %all-gather.99.cloned.1.call-start = ((), (), s32[]{:S(2)}) async-start(), calls=%async_computation.53 | async-start | bytes 1327104 | tf_op jit(solution)/shard_map/all_gather | solution.py:79
  638.9 151.2 %all-gather.59.cloned.1.call-start = ((), (), s32[]{:S(2)}) async-start(), calls=%async_computation.22 | async-start | bytes 3932160 | tf_op jit(solution)/shard_map/all_gather | solution.py:60
  702.5 112.2 %all-gather.101.cloned.1.call-start = ((), (), s32[]{:S(2)}) async-start(), calls=%async_computation.54 | async-start | bytes 1327104 | tf_op jit(solution)/shard_map/all_gather | solution.py:80
  703.2 137.9 %all-gather.97.cloned.1.call-start = ((), (), s32[]{:S(2)}) async-start(), calls=%async_computation.52 | async-start | bytes 1327104 | tf_op jit(solution)/shard_map/all_gather | solution.py:81
  703.8 163.4 %all-gather.103.cloned.1.call-start = ((), (), s32[]{:S(2)}) async-start(), calls=%async_computation.55 | async-start | bytes 1327104 | tf_op jit(solution)/shard_map/all_gather | solution.py:91
  704.5 227.8 %reduce-scatter.27.cloned.1.call-start = ((), (), s32[]{:S(2)}) async-start(), calls=%async_computation.23 | async-start | bytes 3932160 | tf_op jit(solution)/shard_map/reduce_scatter | solution.py:66
  872.0 87.0 %all-gather.109.cloned.1.call-start = ((), (), s32[]{:S(2)}) async-start(), calls=%async_computation.58 | async-start | bytes 1327104 | tf_op jit(solution)/shard_map/all_gather | solution.py:83
  872.7 112.1 %all-gather.105.cloned.1.call-start = ((), (), s32[]{:S(2)}) async-start(), calls=%async_computation.56 | async-start | bytes 1327104 | tf_op jit(solution)/shard_map/all_gather | solution.py:84
  873.3 137.5 %all-gather.107.cloned.1.call-start = ((), (), s32[]{:S(2)}) async-start(), calls=%async_computation.57 | async-start | bytes 1327104 | tf_op jit(solution)/shard_map/all_gather | solution.py:82
  874.1 202.3 %all-gather.61.cloned.1.call-start = ((), (), s32[]{:S(2)}) async-start(), calls=%async_computation.24 | async-start | bytes 3932160 | tf_op jit(solution)/shard_map/all_gather | solution.py:60
  935.3 165.4 %all-gather.111.cloned.1.call-start = ((), (), s32[]{:S(2)}) async-start(), calls=%async_computation.59 | async-start | bytes 1327104 | tf_op jit(solution)/shard_map/all_gather | solution.py:92
  935.9 230.1 %reduce-scatter.29.cloned.1.call-start = ((), (), s32[]{:S(2)}) async-start(), calls=%async_computation.25 | async-start | bytes 3932160 | tf_op jit(solution)/shard_map/reduce_scatter | solution.py:66
  1105.6 101.8 %all-gather.113.cloned.1.call-start = ((), (), s32[]{:S(2)}) async-start(), calls=%async_computation.60 | async-start | bytes 5308416 | tf_op jit(solution)/shard_map/all_gather | solution.py:85
  1106.3 166.6 %all-gather.63.cloned.1.call-start = ((), (), s32[]{:S(2)}) async-start(), calls=%async_computation.26 | async-start | bytes 3932160 | tf_op jit(solution)/shard_map/all_gather | solution.py:60
  1168.9 168.3 %all-gather.65.cloned.1.call-start = ((), (), s32[]{:S(2)}) async-start(), calls=%async_computation.28 | async-start | bytes 3932160 | tf_op jit(solution)/shard_map/all_gather | solution.py:60
  1171.4 206.0 %all-gather.115.cloned.1.call-start = ((), (), s32[]{:S(2)}) async-start(), calls=%async_computation.61 | async-start | bytes 5308416 | tf_op jit(solution)/shard_map/all_gather | solution.py:93
  1172.1 286.2 %reduce-scatter.33.cloned.1.call-start = ((), (), s32[]{:S(2)}) async-start(), calls=%async_computation.29 | async-start | bytes 3932160 | tf_op jit(solution)/shard_map/reduce_scatter | solution.py:66
  1397.9 123.0 %reduce-scatter.31.cloned.1.call-start = ((), (), s32[]{:S(2)}) async-start(), calls=%async_computation.27 | async-start | bytes 3932160 | tf_op jit(solution)/shard_map/reduce_scatter | solution.py:66
  1407.2 181.9 %all-gather.67.cloned.1.call-start = ((), (), s32[]{:S(2)}) async-start(), calls=%async_computation.30 | async-start | bytes 3932160 | tf_op jit(solution)/shard_map/all_gather | solution.py:60
  1525.4 134.1 %reduce-scatter.35.cloned.1.call-start = ((), (), s32[]{:S(2)}) async-start(), calls=%async_computation.31 | async-start | bytes 3932160 | tf_op jit(solution)/shard_map/reduce_scatter | solution.py:66
  1600.5 128.4 %all-gather.69.cloned.1.call-start = ((), (), s32[]{:S(2)}) async-start(), calls=%async_computation.32 | async-start | bytes 3932160 | tf_op jit(solution)/shard_map/all_gather | solution.py:60
  1665.2 190.4 %reduce-scatter.37.cloned.1.call-start = ((), (), s32[]{:S(2)}) async-start(), calls=%async_computation.33 | async-start | bytes 3932160 | tf_op jit(solution)/shard_map/reduce_scatter | solution.py:66
  1796.5 128.4 %all-gather.71.cloned.1.call-start = ((), (), s32[]{:S(2)}) async-start(), calls=%async_computation.34 | async-start | bytes 3932160 | tf_op jit(solution)/shard_map/all_gather | solution.py:60
  1861.2 145.6 %reduce-scatter.39.cloned.1.call-start = ((), (), s32[]{:S(2)}) async-start(), calls=%async_computation.35 | async-start | bytes 3932160 | tf_op jit(solution)/shard_map/reduce_scatter | solution.py:66
  1947.8 128.4 %all-gather.73.cloned.1.call-start = ((), (), s32[]{:S(2)}) async-start(), calls=%async_computation.36 | async-start | bytes 3932160 | tf_op jit(solution)/shard_map/all_gather | solution.py:60
  2012.5 134.1 %reduce-scatter.41.cloned.1.call-start = ((), (), s32[]{:S(2)}) async-start(), calls=%async_computation.37 | async-start | bytes 3932160 | tf_op jit(solution)/shard_map/reduce_scatter | solution.py:66
  2087.5 128.9 %all-gather.75.cloned.1.call-start = ((), (), s32[]{:S(2)}) async-start(), calls=%async_computation.38 | async-start | bytes 3932160 | tf_op jit(solution)/shard_map/all_gather | solution.py:60
  2152.7 232.3 %reduce-scatter.43.cloned.1.call-start = ((), (), s32[]{:S(2)}) async-start(), calls=%async_computation.39 | async-start | bytes 3932160 | tf_op jit(solution)/shard_map/reduce_scatter | solution.py:66
  2286.4 137.7 %reduce-scatter.45.cloned.1.call-start = ((), (), s32[]{:S(2)}) async-start(), calls=%async_computation.40 | async-start | bytes 245760 | tf_op jit(solution)/shard_map/reduce_scatter | solution.py:72
  2293.1 131.1 %reduce-scatter.47.cloned.1.call-start = ((), (), s32[]{:S(2)}) async-start(), calls=%async_computation.41 | async-start | bytes 245760 | tf_op jit(solution)/shard_map/reduce_scatter | solution.py:72
  2322.1 193.7 %reduce-scatter.51.cloned.1.call-start = ((), (), s32[]{:S(2)}) async-start(), calls=%async_computation.63 | async-start | bytes 21233664
  2356.4 285.5 %all-reduce.3.cloned.1.call-start = ((), (), s32[]{:S(2)}) async-start(), calls=%async_computation.64 | async-start | bytes 172032 | tf_op jit(solution)/shard_map/psum | solution.py:427
  2388.4 385.0 %reduce-scatter.49.cloned.1.call-start = ((), (), s32[]{:S(2)}) async-start(), calls=%async_computation.62 | async-start | bytes 21233664
  (234 other events, 6254.5 us)
Sparse Core Ops, SparseCore 0:
  10.5 26.7 all-gather.78
  39.4 63.4 all-gather.52
  105.4 22.6 all-gather.80
  130.5 24.0 all-gather.76
  156.9 24.0 all-gather.82
  186.0 60.2 reduce-scatter.20
  248.7 24.0 all-gather.88
  275.3 24.0 all-gather.84
  301.9 24.0 all-gather.86
  328.0 63.4 all-gather.54
  394.0 22.6 all-gather.90
  421.9 60.2 reduce-scatter.22
  484.6 38.9 all-gather.92
  525.6 63.4 all-gather.56
  591.4 37.5 all-gather.94
  638.4 60.2 reduce-scatter.24
  700.4 24.0 all-gather.98
  726.5 63.4 all-gather.58
  792.0 22.6 all-gather.100
  817.0 24.0 all-gather.96
  843.0 24.1 all-gather.102
  872.1 60.2 reduce-scatter.26
  934.8 24.0 all-gather.108
  960.7 24.0 all-gather.104
  986.7 24.0 all-gather.106
  1012.8 63.4 all-gather.60
  1078.0 22.6 all-gather.110
  1105.7 60.2 reduce-scatter.28
  1168.4 38.9 all-gather.112
  1209.4 63.4 all-gather.62
  1275.1 62.1 all-gather.64
  1339.7 37.5 all-gather.114
  1398.0 60.2 reduce-scatter.32
  1460.6 60.2 reduce-scatter.30
  1525.6 63.5 all-gather.66
  1600.6 58.8 reduce-scatter.34
  1665.3 63.5 all-gather.68
  1796.6 58.8 reduce-scatter.36
  1861.3 63.5 all-gather.70
  1947.9 58.8 reduce-scatter.38
  2012.6 63.5 all-gather.72
  2087.6 58.8 reduce-scatter.40
  2152.9 63.5 all-gather.74
  2286.5 58.9 reduce-scatter.42
  2348.2 19.3 reduce-scatter.44
  2391.5 124.3 reduce-scatter.50
  2521.9 119.9 all-reduce.2
  2645.4 127.9 reduce-scatter.48
  (1 shorter events, 17.5 us)
where the time goes:
time: 2810 us; the launch traced here: 2800 us
  waiting for transfers between devices  2140 us (76%)
  matrix products  379 us (13%)
  local copies, waits for them, and re-layouts  135 us (5%)
  other arithmetic  116 us (4%)
    all_gather x12, waiting for transfers between devices, full_rows(): lax.all_gather(as_sent(local_part), 'col', axis=0, tiled=True)  751 us
    reduce_scatter x12, waiting for transfers between devices, split_sum(): lax.psum_scatter(partial_value.astype(jnp.bfloat16), 'col', scatter_dimen...  640 us
    unnamed x51, waiting for transfers between devices  224 us
    dot_general x20, matrix products, product(): return jnp.dot(left, right, preferred_element_type=jnp.float32)  121 us
    psum x1, waiting for transfers between devices, shards(): lax.psum((jnp.stack(gain_grads), jnp.stack(shift_grads)), ('row', 'col'))  113 us
    unnamed x482, local copies, waits for them, and re-layouts  111 us
    dot_general x20, matrix products, product_nt(): lax.dot_general(left, right, (((1,), (1,)), ((), ())), preferred_element_...  78.3 us
    all_gather x2, waiting for transfers between devices, inner_weights(): lax.all_gather(w_up, 'row', axis=0, tiled=True)  70.2 us
  transfers between devices with their start and end apart: 49, of which 46 were waited for; matrix products, arithmetic and copies ran while one was open for 11% of the time, Pallas kernels for 0%

commit v1 on v0

v1 whole, which is shorter than its diff:
```python
import functools

import jax
import jax.numpy as jnp
from jax import lax
from jax.experimental import pallas as pl
from jax.experimental.pallas import tpu as pltpu
from jax.sharding import PartitionSpec as P

HEAD = 64
CLIP_LEN = 1024
LAYERS = 2
SCALE = 0.125
EPS = 1e-05
NEG = -1e30
BF = jnp.bfloat16
F32 = jnp.float32
VMEM_LIMIT = 48 * 2**20
COST = CLIP_LEN * CLIP_LEN * 8


def product(left, right):
    return jnp.dot(left, right, preferred_element_type=F32)


def product_tn(left, right):
    return lax.dot_general(left, right, (((0,), (0,)), ((), ())), preferred_element_type=F32)


def product_nt(left, right):
    return lax.dot_general(left, right, (((1,), (1,)), ((), ())), preferred_element_type=F32)


def after(value, token):
    return lax.optimization_barrier((value, token))[0]


class Grid:
    def __init__(self, mesh):
        self.R = mesh.shape["row"]
        self.C = mesh.shape["col"]
        self.T = self.R // 2
        assert self.T == self.C
        self.groups = [[2 * i + core for i in range(self.T)] for core in range(2)]

    def at(self):
        row = lax.axis_index("row")
        self.i = row // 2
        self.core = row % 2
        self.z = lax.axis_index("col")

    def swap(self, value, d):
        return lax.ppermute(value, "row", [(r, r ^ (2 * d)) for r in range(self.R)])

    def core_swap(self, value):
        return lax.ppermute(value, "row", [(r, r ^ 1) for r in range(self.R)])

    def plane_a2a(self, value):
        return lax.all_to_all(value, "row", 0, 0, tiled=True, axis_index_groups=self.groups)

    def row_a2a(self, value):
        return lax.all_to_all(value, "row", 0, 0, tiled=True)

    def col_a2a(self, value):
        return lax.all_to_all(value, "col", 0, 0, tiled=True)

    def distances(self):
        return sorted(range(1, self.T), key=lambda d: (bin(d).count("1"), d))

    def gather(self, own):
        half = own.shape[0] // 2
        pieces = {0: own}
        for d in self.distances():
            high = 1 << (d.bit_length() - 1)
            low = d & -d
            if high == low:
                pieces[d] = self.swap(own, d)
            else:
                pieces[d] = jnp.concatenate(
                    [self.swap(pieces[d ^ high][:half], high), self.swap(pieces[d ^ low][half:], low)], axis=0
                )
        return [pieces[d] for d in range(self.T)]

    def scatter(self, terms):
        held = {}
        extra = {}
        half = None
        for d in reversed(self.distances()):
            term = terms[d]()
            half = term.shape[0] // 2
            for lower, upper in extra.get(d, []):
                term = term + jnp.concatenate([lower, upper], axis=0)
            sent = term.astype(BF)
            high = 1 << (d.bit_length() - 1)
            low = d & -d
            if high == low:
                held[d] = self.swap(sent, d).astype(F32)
            else:
                first = self.swap(sent[:half], high).astype(F32)
                second = self.swap(sent[half:], low).astype(F32)
                extra.setdefault(d ^ high, []).append((first, jnp.zeros_like(second)))
                extra.setdefault(d ^ low, []).append((jnp.zeros_like(first), second))
        total = terms[0]()
        for d in held:
            total = total + held[d]
        return total

    def natural(self, pieces):
        stacked = jnp.stack(pieces)
        return [lax.dynamic_index_in_dim(stacked, self.i ^ m, 0, keepdims=False) for m in range(self.T)]

    def tokens_in(self, block):
        rows, width = block.shape
        spread = self.plane_a2a(block.reshape(self.T, rows // self.T, width))
        return self.col_a2a(spread).reshape(rows, width)

    def tokens_out(self, block):
        rows, width = block.shape
        spread = self.col_a2a(block.reshape(self.C, rows // self.C, width))
        return self.plane_a2a(spread).reshape(rows, width)

    def total(self, value):
        for d in range(self.R.bit_length() - 1):
            value = value + lax.ppermute(value, "row", [(r, r ^ (1 << d)) for r in range(self.R)])
        for d in range(self.C.bit_length() - 1):
            value = value + lax.ppermute(value, "col", [(c, c ^ (1 << d)) for c in range(self.C)])
        return value

    def own_first(self, value):
        width = value.shape[-1]
        parts = value.reshape(value.shape[:-1] + (self.T, 2, width // self.R))
        even, odd = parts[..., 0, :], parts[..., 1, :]
        first = self.core == 0
        pair = [jnp.where(first, even, odd), jnp.where(first, odd, even)]
        return jnp.stack(pair, axis=-3).reshape(value.shape)

    def own_last(self, value):
        width = value.shape[-1]
        parts = value.reshape(value.shape[:-1] + (2, self.T, width // self.R))
        own, other = parts[..., 0, :, :], parts[..., 1, :, :]
        first = self.core == 0
        pair = [jnp.where(first, own, other), jnp.where(first, other, own)]
        return jnp.stack(pair, axis=-2).reshape(value.shape)


def gelu_parts(u):
    cdf = 0.5 * (1.0 + lax.erf(u * (0.5**0.5)))
    pdf = jnp.exp(-0.5 * u * u) * (0.5 / jnp.pi) ** 0.5
    return u * cdf, cdf + u * pdf


def norm_forward(residual, gain, shift):
    row_mean = jnp.mean(residual, axis=1, keepdims=True)
    centered = residual - row_mean
    variance = jnp.mean(centered * centered, axis=1, keepdims=True)
    inv_std = lax.rsqrt(variance + EPS)
    normed = centered * inv_std
    return (normed, inv_std, (normed * gain + shift).astype(BF))


def norm_backward(grad_out, normed, inv_std, gain):
    scaled = grad_out * gain
    row_mean = jnp.mean(scaled, axis=1, keepdims=True)
    row_along = jnp.mean(scaled * normed, axis=1, keepdims=True)
    grad_in = inv_std * (scaled - row_mean - normed * row_along)
    return (grad_in, jnp.sum(grad_out * normed, axis=0), jnp.sum(grad_out, axis=0))


def to_clip(grid, i, source, target):
    rows = CLIP_LEN // grid.T
    small = rows // grid.C
    for d in range(grid.T):
        for k in range(grid.C):
            start = pl.multiple_of((i ^ d) * small + k * rows, small)
            target[pl.ds(start, small), :] = source[d * rows + k * small : d * rows + (k + 1) * small, :]


def from_clip(grid, i, block, k, target, lanes):
    rows = CLIP_LEN // grid.T
    small = rows // grid.C
    for d in range(grid.T):
        start = pl.multiple_of((i ^ d) * small, small)
        target[d * rows + k * small : d * rows + (k + 1) * small, lanes] = block[pl.ds(start, small), :]


def causal_block(scores_t, size):
    keys = lax.broadcasted_iota(jnp.int32, (size, size), 0)
    asks = lax.broadcasted_iota(jnp.int32, (size, size), 1)
    last = scores_t.shape[0] - size
    edge = jnp.where(keys <= asks, scores_t[last:], NEG)
    return edge if last == 0 else jnp.concatenate([scores_t[:last], edge], axis=0)


def dot_nt(left, right):
    return lax.dot_general(left, right, (((1,), (1,)), ((), ())), preferred_element_type=F32)


def dot_nn(left, right):
    return lax.dot_general(left, right, (((1,), (0,)), ((), ())), preferred_element_type=F32)


def flip(value):
    return value.astype(F32).T


def self_forward_kernel(grid, units, width, i_ref, x_ref, out_ref, sums_ref, clip, block):
    i = i_ref[0]
    size = CLIP_LEN // grid.C
    to_clip(grid, i, x_ref, clip)
    for u in range(units):
        base = u * 3 * width
        heads = range(width // HEAD)
        keys = [clip[:, base + width + h * HEAD : base + width + (h + 1) * HEAD] for h in heads]
        values_t = [
            flip(clip[:, base + 2 * width + h * HEAD : base + 2 * width + (h + 1) * HEAD]).astype(BF) for h in heads
        ]
        for k in range(grid.C):
            low, high = k * size, (k + 1) * size
            outs = []
            for h in heads:
                asks = clip[low:high, base + h * HEAD : base + (h + 1) * HEAD] * BF(SCALE)
                scores = causal_block(dot_nt(keys[h][:high], asks), size)
                top = jnp.max(scores, axis=0, keepdims=True)
                weight = jnp.exp(scores - top)
                total = jnp.sum(weight, axis=0, keepdims=True)
                outs.append(dot_nn(values_t[h][:, :high], weight.astype(BF)) / total)
                sums_ref[u, h : h + 1, low:high] = top + jnp.log(total)
            both = outs[0] if len(outs) == 1 else jnp.concatenate(outs, axis=0)
            block[...] = both.T.astype(BF)
            from_clip(grid, i, block, k, out_ref, slice(u * width, (u + 1) * width))


def self_backward_kernel(grid, units, width, i_ref, x_ref, da_ref, sums_ref, out_ref, clip, da_clip, block, acc):
    i = i_ref[0]
    size = CLIP_LEN // grid.C
    to_clip(grid, i, x_ref, clip)
    to_clip(grid, i, da_ref, da_clip)
    for u in range(units):
        base = u * 3 * width
        heads = range(width // HEAD)
        lanes = lambda which, h: slice(base + which * width + h * HEAD, base + which * width + (h + 1) * HEAD)
        keys = [clip[:, lanes(1, h)] for h in heads]
        values = [clip[:, lanes(2, h)] for h in heads]
        keys_t = [flip(keys[h]).astype(BF) for h in heads]
        for k in reversed(range(grid.C)):
            low, high = k * size, (k + 1) * size
            dq = []
            for h in heads:
                asks = clip[low:high, lanes(0, h)] * BF(SCALE)
                da = da_clip[low:high, u * width + h * HEAD : u * width + (h + 1) * HEAD]
                scores = causal_block(dot_nt(keys[h][:high], asks), size)
                probs = jnp.exp(scores - sums_ref[u, h : h + 1, low:high])
                d_probs = dot_nt(values[h][:high], da)
                inner = jnp.sum(probs * d_probs, axis=0, keepdims=True)
                d_scores = (probs * (d_probs - inner)).astype(BF)
                dk = dot_nn(d_scores, asks)
                dv = dot_nn(probs.astype(BF), da)
                at_k, at_v = slice(h * HEAD, (h + 1) * HEAD), slice(width + h * HEAD, width + (h + 1) * HEAD)
                if k == grid.C - 1:
                    acc[:, at_k] = dk
                    acc[:, at_v] = dv
                else:
                    acc[:high, at_k] += dk
                    acc[:high, at_v] += dv
                dq.append(dot_nn(keys_t[h][:, :high], d_scores) * SCALE)
            both = dq[0] if len(dq) == 1 else jnp.concatenate(dq, axis=0)
            block[:, :width] = both.T.astype(BF)
            block[:, width:] = acc[low:high, :].astype(BF)
            from_clip(grid, i, block, k, out_ref, slice(base, base + 3 * width))


def self_specs(grid, units, width):
    per_step = 1 if width % 128 == 0 else units
    steps = units // per_step

    def spec(lanes):
        return pl.BlockSpec((CLIP_LEN, per_step * lanes), lambda n, i: (0, n))

    sums = pl.BlockSpec((per_step, 8, CLIP_LEN), lambda n, i: (n, 0, 0))
    return steps, per_step, spec, sums


def self_attention(grid, x, units, width):
    steps, per_step, spec, sums = self_specs(grid, units, width)
    size = CLIP_LEN // grid.C
    return pl.pallas_call(
        functools.partial(self_forward_kernel, grid, per_step, width),
        grid_spec=pltpu.PrefetchScalarGridSpec(
            num_scalar_prefetch=1,
            grid=(steps,),
            in_specs=[spec(3 * width)],
            out_specs=[spec(width), sums],
            scratch_shapes=[
                pltpu.VMEM((CLIP_LEN, per_step * 3 * width), BF),
                pltpu.VMEM((size, width), BF),
            ],
        ),
        out_shape=[
            jax.ShapeDtypeStruct((CLIP_LEN, units * width), BF),
            jax.ShapeDtypeStruct((units, 8, CLIP_LEN), F32),
        ],
        compiler_params=pltpu.CompilerParams(vmem_limit_bytes=VMEM_LIMIT),
        cost_estimate=pl.CostEstimate(
            flops=COST * units * width, bytes_accessed=CLIP_LEN * units * width * 8, transcendentals=0
        ),
        name="self_attention",
    )(grid.i.reshape(1), x)


def self_attention_grad(grid, x, da, sums_in, units, width):
    steps, per_step, spec, sums = self_specs(grid, units, width)
    size = CLIP_LEN // grid.C
    return pl.pallas_call(
        functools.partial(self_backward_kernel, grid, per_step, width),
        grid_spec=pltpu.PrefetchScalarGridSpec(
            num_scalar_prefetch=1,
            grid=(steps,),
            in_specs=[spec(3 * width), spec(width), sums],
            out_specs=spec(3 * width),
            scratch_shapes=[
                pltpu.VMEM((CLIP_LEN, per_step * 3 * width), BF),
                pltpu.VMEM((CLIP_LEN, per_step * width), BF),
                pltpu.VMEM((size, 3 * width), BF),
                pltpu.VMEM((CLIP_LEN, 2 * width), F32),
            ],
        ),
        out_shape=jax.ShapeDtypeStruct((CLIP_LEN, units * 3 * width), BF),
        compiler_params=pltpu.CompilerParams(vmem_limit_bytes=VMEM_LIMIT),
        cost_estimate=pl.CostEstimate(
            flops=3 * COST * units * width, bytes_accessed=CLIP_LEN * units * width * 16, transcendentals=0
        ),
        name="self_attention_grad",
    )(grid.i.reshape(1), x, da, sums_in)


def cross_scores(keys, asks):
    scores = dot_nt(keys, asks)
    top = jnp.max(scores, axis=0, keepdims=True)
    weight = jnp.exp(scores - top)
    return weight / jnp.sum(weight, axis=0, keepdims=True)


def cross_forward_kernel(q_ref, k_ref, v_ref, out_ref):
    for low in range(0, q_ref.shape[1], 2 * HEAD):
        pair = []
        for at in (slice(low, low + HEAD), slice(low + HEAD, low + 2 * HEAD)):
            probs = cross_scores(k_ref[:, at], q_ref[:, at] * BF(SCALE)).astype(BF)
            pair.append(dot_nn(flip(v_ref[:, at]).astype(BF), probs))
        out_ref[:, low : low + 2 * HEAD] = jnp.concatenate(pair, axis=0).T.astype(BF)


def cross_backward_kernel(q_ref, k_ref, v_ref, dc_ref, dq_ref, dk_ref, dv_ref):
    for low in range(0, q_ref.shape[1], 2 * HEAD):
        pair, dk, dv = [], [], []
        for at in (slice(low, low + HEAD), slice(low + HEAD, low + 2 * HEAD)):
            asks = q_ref[:, at] * BF(SCALE)
            probs = cross_scores(k_ref[:, at], asks)
            d_probs = dot_nt(v_ref[:, at], dc_ref[:, at])
            inner = jnp.sum(probs * d_probs, axis=0, keepdims=True)
            d_scores = (probs * (d_probs - inner)).astype(BF)
            dk.append(dot_nn(d_scores, asks))
            dv.append(dot_nn(probs.astype(BF), dc_ref[:, at]))
            pair.append(dot_nn(flip(k_ref[:, at]).astype(BF), d_scores) * SCALE)
        at = slice(low, low + 2 * HEAD)
        dq_ref[:, at] = jnp.concatenate(pair, axis=0).T.astype(BF)
        dk_ref[:, at] = jnp.concatenate(dk, axis=1)
        dv_ref[:, at] = jnp.concatenate(dv, axis=1)


def cross_call(kernel, name, arrays, outs):
    width = arrays[0].shape[1]
    lanes = 512 if width % 512 == 0 else width

    def spec(rows):
        return pl.BlockSpec((rows, lanes), lambda n: (0, n))

    return pl.pallas_call(
        kernel,
        grid=(width // lanes,),
        in_specs=[spec(a.shape[0]) for a in arrays],
        out_specs=[spec(rows) for rows, _ in outs],
        out_shape=[jax.ShapeDtypeStruct((rows, width), kind) for rows, kind in outs],
        compiler_params=pltpu.CompilerParams(vmem_limit_bytes=VMEM_LIMIT),
        cost_estimate=pl.CostEstimate(
            flops=arrays[0].shape[0] * arrays[1].shape[0] * width * 20, bytes_accessed=2**22, transcendentals=0
        ),
        name=name,
    )(*arrays)


def cross_attention(queries, keys, values):
    return cross_call(cross_forward_kernel, "cross_attention", [queries, keys, values], [(queries.shape[0], BF)])[0]


def cross_attention_grad(queries, keys, values, grad_out):
    outs = [(queries.shape[0], BF), (keys.shape[0], F32), (keys.shape[0], F32)]
    return cross_call(cross_backward_kernel, "cross_attention_grad", [queries, keys, values, grad_out], outs)


def head_units(grid, width):
    heads = width // HEAD
    per_unit = -(-heads // grid.T)
    assert heads % per_unit == 0
    return heads // per_unit, per_unit * HEAD


def self_weights(grid, mats, token):
    rows, width = mats[0].shape
    count = len(mats)
    units, wide = head_units(grid, width)
    slots = jnp.stack(mats).reshape(count, rows, units, wide).transpose(2, 0, 1, 3)
    slots = jnp.concatenate([slots, jnp.zeros((grid.T - units, count, rows, wide), BF)], axis=0)
    order = [lax.dynamic_index_in_dim(slots, (s - grid.z - 1) % grid.T, 0, keepdims=False) for s in range(grid.T)]
    moved = grid.plane_a2a(jnp.stack(order))
    moved = after(moved.transpose(1, 0, 2, 3).reshape(count, grid.T * rows, wide), token)
    token = lax.all_gather(moved, "col", axis=0)
    half = jnp.stack(
        [lax.dynamic_index_in_dim(token, (grid.i - 1 - m) % grid.T, 0, keepdims=False) for m in range(units)]
    )
    other = grid.core_swap(half)

    def columns(part):
        low = part[:, :3].transpose(2, 0, 1, 3).reshape(grid.T * rows, units * 3 * wide)
        return low, part[:, 3].transpose(1, 0, 2).reshape(grid.T * rows, units * wide)

    own_in, own_out = columns(half)
    other_in, other_out = columns(other)
    return (joined([own_in, other_in]), joined([own_out, other_out])), token


def core_sum(grid, low, axis=0):
    half = low.shape[axis] // 2
    keep = lax.slice_in_dim(low, 0, half, axis=axis)
    send = lax.slice_in_dim(low, half, 2 * half, axis=axis)
    return (keep.astype(F32) + grid.core_swap(send).astype(F32)).astype(BF)


def self_weights_grad(grid, low, rows, width):
    units, wide = head_units(grid, width)
    half = core_sum(grid, low, 1)
    half = jnp.concatenate([half, jnp.zeros((grid.C - units,) + half.shape[1:], BF)], axis=0)
    slots = jnp.stack(
        [lax.dynamic_index_in_dim(half, (grid.i - c - 1) % grid.T, 0, keepdims=False) for c in range(grid.C)]
    )
    summed = lax.psum_scatter(slots, "col", scatter_dimension=0)
    moved = grid.plane_a2a(summed.reshape(grid.T, rows, 4 * wide))
    mine = [
        lax.dynamic_index_in_dim(moved, (grid.z + 1 + m) % grid.T, 0, keepdims=False) for m in range(units)
    ]
    return [
        jnp.concatenate([part[:, n * wide : (n + 1) * wide] for part in mine], axis=1).astype(F32) for n in range(4)
    ]


def hidden_weights(grid, mats, token):
    rows, width = mats[0].shape
    count = len(mats)
    wide = width // grid.T
    slots = jnp.stack(mats).reshape(count, rows, grid.T, wide).transpose(2, 0, 1, 3)
    moved = grid.plane_a2a(after(slots, token))
    moved = moved.transpose(1, 0, 2, 3).reshape(count, grid.T * rows, wide)
    token = lax.all_gather(moved, "col", axis=0)
    other = grid.core_swap(token)

    def columns(part, n):
        return part[:, n].transpose(1, 0, 2).reshape(grid.T * rows, grid.C * wide)

    return [joined([columns(token, n), columns(other, n)]) for n in range(count)], token


def hidden_weights_grad(grid, low, rows, width):
    half = core_sum(grid, low, 1)
    summed = lax.psum_scatter(half, "col", scatter_dimension=0)
    moved = grid.plane_a2a(summed.reshape(grid.T, rows, width // grid.T))
    return moved.transpose(1, 0, 2).reshape(rows, width).astype(F32)


def cross_weights(grid, mats, token):
    rows, width = mats[0].shape
    count = len(mats)
    token = lax.all_gather(after(jnp.stack(mats), token), "col", axis=0)
    own = token.transpose(1, 2, 0, 3).reshape(count * rows, grid.C * width)
    half = jnp.stack(grid.natural(grid.gather(own)))
    half = half.reshape(grid.T, count, rows, grid.C * width).transpose(1, 0, 2, 3)
    half = half.reshape(count, grid.T * rows, grid.C * width)
    other = grid.core_swap(half)
    return [joined([half[n], other[n]]) for n in range(count)], token


def cross_weights_grad(grid, lows, rows, width):
    count = len(lows)
    halves = [core_sum(grid, low).reshape(grid.T, rows, grid.C * width) for low in lows]

    def term(d):
        parts = [lax.dynamic_index_in_dim(half, grid.i ^ d, 0, keepdims=False) for half in halves]
        return lambda: joined(parts).astype(F32)

    own = grid.scatter([term(d) for d in range(grid.T)]).astype(BF)
    own = own.reshape(count, rows, grid.C, width).transpose(2, 0, 1, 3)
    summed = lax.psum_scatter(own, "col", scatter_dimension=0).astype(F32)
    return [summed[n] for n in range(count)]


def text_columns(grid, text):
    _, own, width = text.shape
    parts = text.reshape(own, grid.R, width // grid.R).transpose(1, 0, 2)
    parts = grid.row_a2a(parts)
    pieces = [parts] + [
        lax.ppermute(parts, "col", [(c, c ^ d) for c in range(grid.C)]) for d in range(1, grid.C)
    ]
    stacked = jnp.stack(pieces)
    order = [lax.dynamic_index_in_dim(stacked, grid.z ^ c, 0, keepdims=False) for c in range(grid.C)]
    return jnp.stack(order, axis=1).reshape(-1, width // grid.R)


def text_forward(grid, columns, mats):
    count, rows, width = mats.shape
    own = columns.shape[0] // (grid.R * grid.C)
    part = product(columns, mats.transpose(1, 0, 2).reshape(rows, count * width)).astype(BF)
    part = part.reshape(grid.T, 2, grid.C, own, count * width).transpose(2, 1, 0, 3, 4)
    part = part.reshape(grid.R, grid.T * own, count * width)
    moved = grid.row_a2a(part).astype(F32)
    summed = jnp.sum(moved, axis=0).astype(BF).reshape(grid.T, own, count * width)
    moved = grid.col_a2a(summed)
    mine = moved.reshape(grid.C, own, count, width).transpose(1, 2, 0, 3)
    mine = mine.reshape(own, count * grid.C * width)
    full = jnp.concatenate(grid.gather(mine), axis=0)
    return full.reshape(-1, count, grid.C * width)


def text_backward(grid, grads, width):
    states = grads.shape[0]
    own = states // grid.T
    pieces = grads.reshape(grid.T, own, -1)
    mine = grid.scatter([lambda d=d: pieces[d] for d in range(grid.T)]).astype(BF)
    mine = mine.reshape(own, -1, grid.C, width).transpose(2, 0, 1, 3)
    moved = grid.col_a2a(mine)
    other = grid.core_swap(moved)
    pair = jnp.stack(
        [jnp.where(grid.core == 0, moved, other), jnp.where(grid.core == 0, other, moved)], axis=1
    )
    shape = pair.shape
    flat = pair.reshape(shape[0] * 2, -1)
    full = jnp.stack(grid.natural(grid.gather(flat)), axis=1)
    return full.reshape(-1, shape[3], width)


def text_out(grid, part):
    own = part.shape[0] // (grid.R * grid.C)
    cols = part.shape[1]
    parts = part.astype(BF).reshape(grid.R, grid.C, own, cols).transpose(1, 0, 2, 3)
    moved = grid.col_a2a(parts).astype(F32)
    summed = jnp.sum(moved, axis=0).astype(BF)
    moved = grid.row_a2a(summed)
    return moved.transpose(1, 0, 2).reshape(1, own, grid.R * cols).astype(F32)


def joined(pieces):
    return jnp.concatenate(pieces, axis=0)


def rows_of(grid, value, d):
    count = value.shape[0] // grid.T
    return value[d * count : (d + 1) * count]


def layer_forward(grid, residual, weights, text_pair, gains, shifts, units, wide):
    (w_qkv, w_out), w_cross, w_hidden = weights
    normed_one, inv_one, low_one = norm_forward(residual, gains[0], shifts[0])
    full_one = joined(grid.gather(low_one))
    qkv = product(full_one, w_qkv).astype(BF)
    attn_low, sums_self = self_attention(grid, qkv, units, wide)
    residual = residual + grid.scatter(
        [lambda d=d: product_nt(rows_of(grid, attn_low, d), w_out) for d in range(grid.T)]
    )
    normed_two, inv_two, low_two = norm_forward(residual, gains[1], shifts[1])
    cross_queries = product(low_two, w_cross[0]).astype(BF)
    cross_low = cross_attention(cross_queries, text_pair[0], text_pair[1])
    residual = residual + product_nt(cross_low, w_cross[1])
    normed_three, inv_three, low_three = norm_forward(residual, gains[2], shifts[2])
    full_three = joined(grid.gather(low_three))
    hidden, slope = gelu_parts(product(full_three, w_hidden[0]))
    hidden_low = hidden.astype(BF)
    hidden_slope = slope.astype(BF)
    residual = residual + grid.scatter(
        [lambda d=d: product_nt(rows_of(grid, hidden_low, d), w_hidden[1]) for d in range(grid.T)]
    )
    stored = dict(
        normed_one=normed_one,
        inv_one=inv_one,
        full_one=full_one,
        qkv=qkv,
        attn_low=attn_low,
        sums_self=sums_self,
        normed_two=normed_two,
        inv_two=inv_two,
        low_two=low_two,
        cross_queries=cross_queries,
        cross_low=cross_low,
        normed_three=normed_three,
        inv_three=inv_three,
        full_three=full_three,
        hidden_low=hidden_low,
        hidden_slope=hidden_slope,
    )
    return residual, stored


def weight_product(left, right, blocks):
    parts = right.reshape(right.shape[0], blocks, -1)
    return lax.dot_general(left, parts, (((0,), (0,)), ((), ())), preferred_element_type=F32).astype(BF).transpose(1, 0, 2)


def layer_backward(grid, gradient, weights, text_pair, gains, stored, units, wide):
    (w_qkv, w_out), w_cross, w_hidden = weights
    dy_three = joined(grid.gather(gradient.astype(BF)))
    d_pre = (product(dy_three, w_hidden[1]) * stored["hidden_slope"].astype(F32)).astype(BF)
    grad_normed = grid.scatter(
        [lambda d=d: product_nt(rows_of(grid, d_pre, d), w_hidden[0]) for d in range(grid.T)]
    )
    hidden_grads = [
        weight_product(stored["full_three"], d_pre, grid.C),
        weight_product(dy_three, stored["hidden_low"], grid.C),
    ]
    grad_res, gain_three, shift_three = norm_backward(
        grad_normed, stored["normed_three"], stored["inv_three"], gains[2]
    )
    gradient = gradient + grad_res
    dy_two = gradient.astype(BF)
    d_cross = product(dy_two, w_cross[1]).astype(BF)
    d_cquery, d_ckey, d_cvalue = cross_attention_grad(
        stored["cross_queries"], text_pair[0], text_pair[1], d_cross
    )
    grad_normed = product_nt(d_cquery, w_cross[0])
    cross_grads = [
        product_tn(stored["low_two"], d_cquery).astype(BF),
        product_tn(dy_two, stored["cross_low"]).astype(BF),
    ]
    text_grads = jnp.concatenate([d_ckey, d_cvalue], axis=1)
    grad_res, gain_two, shift_two = norm_backward(
        grad_normed, stored["normed_two"], stored["inv_two"], gains[1]
    )
    gradient = gradient + grad_res
    dy_one = joined(grid.gather(gradient.astype(BF)))
    d_attn = product(dy_one, w_out).astype(BF)
    d_qkv = self_attention_grad(grid, stored["qkv"], d_attn, stored["sums_self"], units, wide)
    grad_normed = grid.scatter(
        [lambda d=d: product_nt(rows_of(grid, d_qkv, d), w_qkv) for d in range(grid.T)]
    )
    self_grads = jnp.concatenate(
        [
            weight_product(stored["full_one"], d_qkv, units),
            weight_product(dy_one, stored["attn_low"], units),
        ],
        axis=2,
    )
    grad_res, gain_one, shift_one = norm_backward(
        grad_normed, stored["normed_one"], stored["inv_one"], gains[0]
    )
    gradient = gradient + grad_res
    norms = jnp.stack([gain_one, gain_two, gain_three, shift_one, shift_two, shift_three])
    return gradient, hidden_grads, cross_grads, self_grads, text_grads, norms


def shards(
    grid,
    inputs,
    text_states,
    cotangent,
    norm_gains,
    norm_shifts,
    self_query,
    self_key,
    self_value,
    self_out,
    cross_query,
    cross_key,
    cross_value,
    cross_out,
    mlp_up,
    mlp_down,
):
    grid.at()
    rows, width = self_query.shape[1:]
    hidden_width = mlp_up.shape[2]
    units, wide = head_units(grid, width)
    weights = []
    token = jnp.zeros((), BF)
    gains, shifts = grid.own_first(norm_gains), grid.own_first(norm_shifts)
    residual = grid.own_first(grid.tokens_in(inputs)).astype(F32)
    for n in range(LAYERS):
        w_self, token = self_weights(grid, [self_query[n], self_key[n], self_value[n], self_out[n]], token)
        w_cross, token = cross_weights(grid, [cross_query[n], cross_out[n]], token)
        w_hidden, token = hidden_weights(grid, [mlp_up[n], mlp_down[n]], token)
        weights.append((w_self, w_cross, w_hidden))
    text_cols = text_columns(grid, text_states)
    text_mats = jnp.stack([mat for n in range(LAYERS) for mat in (cross_key[n], cross_value[n])])
    text_all = text_forward(grid, text_cols, text_mats)
    text_pairs = [(text_all[:, 2 * n], text_all[:, 2 * n + 1]) for n in range(LAYERS)]
    stored = []
    for n in range(LAYERS):
        residual, kept = layer_forward(
            grid, residual, weights[n], text_pairs[n], gains[n], shifts[n], units, wide
        )
        stored.append(kept)
    output = grid.tokens_out(grid.own_last(residual.astype(BF))).astype(F32)
    gradient = grid.own_first(grid.tokens_in(cotangent.astype(BF))).astype(F32)
    hidden_out = [None] * LAYERS
    cross_out_grads = [None] * LAYERS
    self_out_grads = [None] * LAYERS
    text_weights = [None] * LAYERS
    norms = [None] * LAYERS
    text_part = 0.0
    for n in range(LAYERS - 1, -1, -1):
        gradient, hidden_grads, cross_grads, self_grads, text_grads, norms[n] = layer_backward(
            grid, gradient, weights[n], text_pairs[n], gains[n], stored[n], units, wide
        )
        hidden_out[n] = [hidden_weights_grad(grid, low, rows, hidden_width) for low in hidden_grads]
        cross_out_grads[n] = cross_weights_grad(grid, cross_grads, rows, width)
        self_out_grads[n] = self_weights_grad(grid, self_grads, rows, width)
        text_full = text_backward(grid, text_grads, width)
        text_weights[n] = [product_tn(text_cols, text_full[:, side]) for side in range(2)]
        text_part = (
            text_part
            + product_nt(text_full[:, 0], cross_key[n])
            + product_nt(text_full[:, 1], cross_value[n])
        )
    input_grad = grid.tokens_out(grid.own_last(gradient.astype(BF))).astype(F32)
    text_grad = text_out(grid, text_part)
    totals = grid.total(grid.own_last(jnp.stack(norms)))
    gains_sum, shifts_sum = totals[:, :3], totals[:, 3:]

    def both(values, slot):
        return jnp.stack([values[n][slot] for n in range(LAYERS)])

    return (
        output,
        input_grad,
        text_grad,
        gains_sum,
        shifts_sum[:, 1:],
        shifts_sum[:, 0],
        both(self_out_grads, 0),
        both(self_out_grads, 1),
        both(self_out_grads, 2),
        both(self_out_grads, 3),
        both(cross_out_grads, 0),
        both(text_weights, 0),
        both(text_weights, 1),
        both(cross_out_grads, 1),
        both(hidden_out, 0),
        both(hidden_out, 1),
    )


def solution(mesh):
    grid = Grid(mesh)
    tokens = P(("row", "col"), None)
    text = P("row", "col", None)
    block = P(None, "row", "col")
    in_specs = (tokens, text, tokens, P(), P()) + (block,) * 10
    out_specs = (tokens, tokens, text, P(), P(), P()) + (block,) * 10

    def run(*args):
        return shards(grid, *args)

    return jax.shard_map(run, mesh=mesh, in_specs=in_specs, out_specs=out_specs, check_vma=False)
```

time: 2810 us -> 1540 us (0.55)
  waiting for transfers between devices: 2140 us -> 522 us
  starting transfers between devices: 4.39 us -> 219 us
  local copies, waits for them, and re-layouts: 135 us -> 307 us
  matrix products: 379 us -> 219 us
  Pallas kernels: 0 us -> 83.2 us
    all_gather x32 -> x6, waiting for transfers between devices: 1160 us -> 74.8 us  [the longest x2 32.6 us: cross_weights(): token = lax.all_gather(after(jnp.stack(mats), token), 'col', axis=0)]
    reduce_scatter x14 -> x8, waiting for transfers between devices: 640 us -> 0.05 us  [the longest x4 0.04 us: hidden_weights_grad(): summed = lax.psum_scatter(half, 'col', scatter_dimension=0)]
    ppermute x0 -> x126, waiting for transfers between devices: none -> 309 us  [the longest x100 281 us: swap(): return lax.ppermute(value, 'row', [(r, r ^ 2 * d) for r in range(self.R)])]
    unnamed x51 -> x14, waiting for transfers between devices: 224 us -> 0.23 us
    dot_general x68 -> x19, matrix products: 239 us -> 101 us  [the longest x13 60.7 us: product(): return jnp.dot(left, right, preferred_element_type=F32)]
    all_to_all x0 -> x24, waiting for transfers between devices: none -> 137 us  [the longest x8 62.7 us: col_a2a(): return lax.all_to_all(value, 'col', 0, 0, tiled=True)]
    ppermute x0 -> x126, starting transfers between devices: none -> 122 us  [the longest x100 114 us: swap(): return lax.ppermute(value, 'row', [(r, r ^ 2 * d) for r in range(self.R)])]
    psum x1 -> x0, waiting for transfers between devices: 113 us -> none  [shards(): lax.psum((jnp.stack(gain_grads), jnp.stack(shift_grads)), ('row', 'col'))]
  transfers between devices with their start and end apart: 49 -> 164, of which waited for: 46 -> 64; matrix products, arithmetic and copies ran while one was open for 11% -> 40% of each run, Pallas kernels for 0% -> 5%
where the time goes in v1:
time: 1540 us; the launch traced here: 1520 us
  waiting for transfers between devices  522 us (34%)
  local copies, waits for them, and re-layouts  307 us (20%)
  starting transfers between devices  219 us (14%)
  matrix products  219 us (14%)
  other arithmetic  129 us (8%)
  Pallas kernels  83.2 us (5%)
  blocking collectives  24.4 us (2%)
  between operations  18.5 us (1%)
    ppermute x100, waiting for transfers between devices, swap(): return lax.ppermute(value, 'row', [(r, r ^ 2 * d) for r in range(self.R)])  281 us
    ppermute x100, starting transfers between devices, swap(): return lax.ppermute(value, 'row', [(r, r ^ 2 * d) for r in range(self.R)])  114 us
    dot_general x40, matrix products, product_nt(): lax.dot_general(left, right, (((1,), (1,)), ((), ())), preferred_element_...  93.1 us
    all_to_all x8, waiting for transfers between devices, col_a2a(): return lax.all_to_all(value, 'col', 0, 0, tiled=True)  62.7 us
    unnamed x551, local copies, waits for them, and re-layouts  62.5 us
    dot_general x13, matrix products, product(): return jnp.dot(left, right, preferred_element_type=F32)  60.7 us
    all_to_all x13, waiting for transfers between devices, plane_a2a(): lax.all_to_all(value, 'row', 0, 0, tiled=True, axis_index_groups=self.gro...  57 us
    all_to_all x13, starting transfers between devices, plane_a2a(): lax.all_to_all(value, 'row', 0, 0, tiled=True, axis_index_groups=self.gro...  49.8 us
  transfers between devices with their start and end apart: 164, of which 64 were waited for; matrix products, arithmetic and copies ran while one was open for 40% of the time, Pallas kernels for 5%

profile of v1, /device:TPU:0, one launch (start us, length us, event | category | flops | bytes accessed | tf_op | source)
XLA Modules:
  0.0 1522.6 jit_solution(3154711533301454374)
XLA Ops:
  43.3 7.6 all-to-all-done.2
  57.9 17.6 %all-to-all-done.4 = bf16[8,64,1536]{2,1,0:T(8,128)(2,1)S(1)} async-done(((bf16[8,64,1536]{2,1,0:T(8,128)(2,1)}), bf16[8,64,1536]{2,1,0:T(8,128)(2,1)S(1)}, u32[]{:S(2)}, u32[]{:S(2)}) %all-to-all-start.4) | async-done | bytes 1572896 | tf_op jit(solution)/shard_map/all_to_all | solution.py:62
  79.9 9.2 all-to-all-done.11
  94.2 13.1 all-to-all-done.5
  116.5 26.5 %all-to-all-done.1 = bf16[4,64,1536]{2,1,0:T(8,128)(2,1)S(1)} async-done(((bf16[4,64,1536]{2,1,0:T(8,128)(2,1)}), bf16[4,64,1536]{2,1,0:T(8,128)(2,1)S(1)}, u32[]{:S(2)}, u32[]{:S(2)}) %all-to-all-start.1) | async-done | bytes 786464 | tf_op jit(solution)/shard_map/all_to_all | solution.py:65
  158.6 8.4 all-to-all-done.12
  189.4 11.6 all-gather.17.cloned.1.call-done
  221.6 33.6 %collective-permute-done.1 = bf16[256,1536]{1,0:T(8,128)(2,1)S(1)} collective-permute-done((bf16[256,1536]{1,0:T(8,128)(2,1)}, bf16[256,1536]{1,0:T(8,128)(2,1)S(1)}, u32[]{:S(2)}, u32[]{:S(2)}) %collective-permute-start.1) | collective-permute-done | bytes 786464 | tf_op jit(solution)/shard_map/ppermute | solution.py:53
  299.1 12.4 self_attention.2
  315.6 6.9 collective-permute-done.7
  333.9 7.1 collective-permute-done.8
  343.4 14.0 all-gather.11.cloned.1.call-done
  357.4 6.7 copy.485
  382.0 24.4 %all_to_all.125 = bf16[4,4,192,128]{3,2,1,0:T(8,128)(2,1)S(1)} all-to-all(bf16[4,4,192,128]{3,2,1,0:T(8,128)(2,1)S(1)} %copy.488), channel_id=1, replica_groups={{0,8,16,24},{4,12,20,28},{1,9,17,25},{5,13,21,29},{2,10,18,26},{6,14,22..., dimensions={0} | all-to-all | bytes 1572864 | tf_op jit(solution)/shard_map/all_to_all | solution.py:59
  410.6 8.3 collective-permute-done.23
  427.6 7.2 multiply_convert_fusion.3
  438.0 7.1 collective-permute-done.28
  452.2 28.2 %all-gather.19.cloned.1.call-done = bf16[16,768,128]{2,1,0:T(8,128)(2,1)} async-done(((bf16[4,768,128]{2,1,0:T(8,128)(2,1)}), bf16[16,768,128]{2,1,0:T(8,128)(2,1)}) %all-gather.19.cloned.1.call-update) | async-done | bytes 3145744 | tf_op jit(solution)/shard_map/all_gather | solution.py:416
  491.9 21.0 %all-gather.21.cloned.1.call-done = bf16[8,192,384]{2,1,0:T(8,128)(2,1)} async-done(((bf16[2,192,384]{2,1,0:T(8,128)(2,1)}), bf16[8,192,384]{2,1,0:T(8,128)(2,1)}) %all-gather.21.cloned.1.call-update) | async-done | bytes 1179664 | tf_op jit(solution)/shard_map/all_gather | solution.py:481
  539.8 27.4 %collective-permute-done.31 = bf16[256,1536]{1,0:T(8,128)(2,1)S(1)} collective-permute-done((bf16[256,1536]{1,0:T(8,128)(2,1)}, bf16[256,1536]{1,0:T(8,128)(2,1)S(1)}, u32[]{:S(2)}, u32[]{:S(2)}) %collective-permute-start.31) | collective-permute-done | bytes 786464 | tf_op jit(solution)/shard_map/ppermute | solution.py:53
  588.3 7.4 collective-permute-done.42
  610.5 12.5 self_attention.3
  669.5 8.7 collective-permute-done.38
  681.9 6.7 copy.495
  712.7 12.0 collective-permute-done.45
  729.7 6.9 collective-permute-done.46
  738.9 10.4 multiply_convert_fusion.2
  749.3 9.8 multiply_convert_fusion.1
  766.5 7.3 convert_bitcast_fusion
  773.8 9.0 convert_bitcast_fusion.2
  798.8 10.9 collective-permute-done.52
  816.6 8.2 collective-permute-done.60
  918.3 8.6 collective-permute-done.61
  949.6 17.2 %self_attention_grad.2 = bf16[1024,1152]{1,0:T(8,128)(2,1)S(1)} custom-call(s32[1]{0:T(128)} %bitcast.4.i_ref, bf16[1024,1152]{1,0:T(8,128)(2,1)S(1)} %copy-done.13, bf16[1024,384]{1,0:T(8,128)(2,1)S(1)} %convolution_convert_fusion.18.da_ref, f32[3,8,1024]{2,1,0:T(8,128)S(1)} %copy-done.17), custom_call_target="tpu_custom_call" | custom-call | flops 9663676416 | bytes 6291456 | tf_op jit(solution)/shard_map/self_attention_grad/pallas_call | solution.py:313
  973.3 6.5 fusion.11
  1005.1 10.4 collective-permute-done.68
  1034.6 22.6 %collective-permute-done.118 = bf16[192,1536]{1,0:T(8,128)(2,1)S(1)} collective-permute-done((bf16[192,1536]{1,0:T(8,128)(2,1)S(1)}, bf16[192,1536]{1,0:T(8,128)(2,1)S(1)}, u32[]{:S(2)}, u32[]{:S(2)}) %collective-permute-start.118) | collective-permute-done | bytes 589856 | tf_op jit(solution)/shard_map/ppermute | solution.py:53
  1066.7 25.2 %collective-permute-done.71 = bf16[128,1536]{1,0:T(8,128)(2,1)S(1)} collective-permute-done((bf16[128,1536]{1,0:T(8,128)(2,1)S(1)}, bf16[128,1536]{1,0:T(8,128)(2,1)S(1)}, u32[]{:S(2)}, u32[]{:S(2)}) %collective-permute-start.71) | collective-permute-done | bytes 393248 | tf_op jit(solution)/shard_map/ppermute | solution.py:53
  1092.5 8.7 multiply_convert_fusion
  1134.2 9.4 collective-permute-done.76
  1183.1 7.6 all-to-all-done.16
  1220.0 6.9 collective-permute-done.78
  1231.3 6.6 collective-permute-done.79
  1243.4 17.3 %self_attention_grad.3 = bf16[1024,1152]{1,0:T(8,128)(2,1)S(1)} custom-call(s32[1]{0:T(128)} %bitcast.4.i_ref, bf16[1024,1152]{1,0:T(8,128)(2,1)S(1)} %copy-done.11, bf16[1024,384]{1,0:T(8,128)(2,1)S(1)} %convolution_convert_fusion.17.da_ref, f32[3,8,1024]{2,1,0:T(8,128)S(1)} %copy-done.15), custom_call_target="tpu_custom_call" | custom-call | flops 9663676416 | bytes 6291456 | tf_op jit(solution)/shard_map/self_attention_grad/pallas_call | solution.py:313
  1288.8 7.4 collective-permute-done.81
  1365.1 13.7 all-to-all-done.24
  1414.2 21.6 %collective-permute-done.104 = f32[2,6,1536]{2,0,1:T(2,128)S(1)} collective-permute-done((f32[2,6,1536]{2,0,1:T(2,128)S(1)}, f32[2,6,1536]{2,0,1:T(2,128)S(1)}, u32[]{:S(2)}, u32[]{:S(2)}) %collective-permute-start.104) | collective-permute-done | bytes 73760 | tf_op jit(solution)/shard_map/ppermute | solution.py:124
  1478.3 7.3 all-to-all-done.23
  (1280 shorter events, 899.1 us)
Async XLA Ops:
  54.5 113.4 %all-gather.15.cloned.1.call-start = ((), (), s32[]{:S(2)}) async-start(), calls=%async_computation.43 | async-start | bytes 3932160 | tf_op jit(solution)/shard_map/all_gather | solution.py:416
  146.6 54.4 %all-gather.17.cloned.1.call-start = ((), (), s32[]{:S(2)}) async-start(), calls=%async_computation.44 | async-start | bytes 1474560 | tf_op jit(solution)/shard_map/all_gather | solution.py:481
  154.0 55.3 %collective-permute-start.18 = (bf16[16,6144]{1,0:T(8,128)(2,1)}, bf16[16,6144]{1,0:T(8,128)(2,1)}, u32[]{:S(2)}, u32[]{:S(2)}) collective-permute-start(bf16[16,6144]{1,0:T(8,128)(2,1)} %reshape.1170), channel_id=1, source_target_pairs={{0,16},{4,20},{8,24},{12,28},{16,0},{20,4},{24,8},{28,12},{1,17},{... | collective-permute-start | bytes 589832 | tf_op jit(solution)/shard_map/ppermute | solution.py:53
  155.4 56.0 %collective-permute-start.17 = (bf16[16,6144]{1,0:T(8,128)(2,1)}, bf16[16,6144]{1,0:T(8,128)(2,1)}, u32[]{:S(2)}, u32[]{:S(2)}) collective-permute-start(bf16[16,6144]{1,0:T(8,128)(2,1)} %reshape.1170), channel_id=1, source_target_pairs={{0,8},{4,12},{8,0},{12,4},{16,24},{20,28},{24,16},{28,20},{1,9},{5... | collective-permute-start | bytes 589832 | tf_op jit(solution)/shard_map/ppermute | solution.py:53
  189.4 93.1 %collective-permute-start.4 = (bf16[3,4,768,128]{2,3,1,0:T(8,128)(2,1)}, bf16[3,4,768,128]{2,3,1,0:T(8,128)(2,1)}, u32[]{:S(2)}, u32[]{:S(2)}) collective-permute-start(bf16[3,4,768,128]{2,3,1,0:T(8,128)(2,1)} %pad_maximum_fusion.38), channel_id=1, source_target_pairs={{0,4},{4,0},{8,12},{12,8},{16,20},{20,16},{24,28},{28,24},{1,5},{5... | collective-permute-start | bytes 7077896 | tf_op jit(solution)/shard_map/ppermute | solution.py:56
  204.4 57.2 %collective-permute-start.10 = (bf16[384,1536]{1,0:T(8,128)(2,1)}, bf16[384,1536]{1,0:T(8,128)(2,1)}, u32[]{:S(2)}, u32[]{:S(2)}) collective-permute-start(bf16[384,1536]{1,0:T(8,128)(2,1)} %bitcast.314), channel_id=1, source_target_pairs={{0,16},{4,20},{8,24},{12,28},{16,0},{20,4},{24,8},{28,12},{1,17},{... | collective-permute-start | bytes 3538952 | tf_op jit(solution)/shard_map/ppermute | solution.py:53
  206.3 59.3 %collective-permute-start.9 = (bf16[384,1536]{1,0:T(8,128)(2,1)}, bf16[384,1536]{1,0:T(8,128)(2,1)}, u32[]{:S(2)}, u32[]{:S(2)}) collective-permute-start(bf16[384,1536]{1,0:T(8,128)(2,1)} %bitcast.314), channel_id=1, source_target_pairs={{0,8},{4,12},{8,0},{12,4},{16,24},{20,28},{24,16},{28,20},{1,9},{5... | collective-permute-start | bytes 3538952 | tf_op jit(solution)/shard_map/ppermute | solution.py:53
  209.3 45.8 %collective-permute-start.1 = (bf16[256,1536]{1,0:T(8,128)(2,1)}, bf16[256,1536]{1,0:T(8,128)(2,1)S(1)}, u32[]{:S(2)}, u32[]{:S(2)}) collective-permute-start(bf16[256,1536]{1,0:T(8,128)(2,1)} %get-tuple-element.200), channel_id=1, source_target_pairs={{0,16},{4,20},{8,24},{12,28},{16,0},{20,4},{24,8},{28,12},{1,17},{... | collective-permute-start | bytes 2359304 | tf_op jit(solution)/shard_map/ppermute | solution.py:53
  211.4 44.5 %collective-permute-start = (bf16[256,1536]{1,0:T(8,128)(2,1)}, bf16[256,1536]{1,0:T(8,128)(2,1)}, u32[]{:S(2)}, u32[]{:S(2)}) collective-permute-start(bf16[256,1536]{1,0:T(8,128)(2,1)} %get-tuple-element.200), channel_id=1, source_target_pairs={{0,8},{4,12},{8,0},{12,4},{16,24},{20,28},{24,16},{28,20},{1,9},{5... | collective-permute-start | bytes 2359304 | tf_op jit(solution)/shard_map/ppermute | solution.py:53
  215.9 52.7 %all-to-all-start.6 = ((bf16[4,2,192,384]{3,2,1,0:T(8,128)(2,1)}), bf16[4,2,192,384]{3,2,1,0:T(8,128)(2,1)S(1)}, u32[]{:S(2)}, u32[]{:S(2)}) async-start(bf16[4,2,192,384]{3,2,1,0:T(8,128)(2,1)} %copy.483), calls=%async_computation.6 | async-start | bytes 2359296 | tf_op jit(solution)/shard_map/all_to_all | solution.py:59
  219.9 137.4 %all-gather.11.cloned.1.call-start = ((), (), s32[]{:S(2)}) async-start(), calls=%async_computation.33 | async-start | bytes 5898240 | tf_op jit(solution)/shard_map/all_gather | solution.py:462
  269.7 210.7 %all-gather.19.cloned.1.call-start = ((), (), s32[]{:S(2)}) async-start(), calls=%async_computation.45 | async-start | bytes 3932160 | tf_op jit(solution)/shard_map/all_gather | solution.py:416
  293.2 70.8 %collective-permute-start.13 = (bf16[2,768,1536]{2,1,0:T(8,128)(2,1)}, bf16[2,768,1536]{2,1,0:T(8,128)(2,1)}, u32[]{:S(2)}, u32[]{:S(2)}) collective-permute-start(bf16[2,768,1536]{2,1,0:T(8,128)(2,1)} %bitcast.30), channel_id=1, source_target_pairs={{0,4},{4,0},{8,12},{12,8},{16,20},{20,16},{24,28},{28,24},{1,5},{5... | collective-permute-start | bytes 14155784 | tf_op jit(solution)/shard_map/ppermute | solution.py:56
  364.0 58.8 %collective-permute-start.25 = (bf16[4,2,768,384]{2,3,0,1:T(8,128)(2,1)}, bf16[4,2,768,384]{2,3,0,1:T(8,128)(2,1)}, u32[]{:S(2)}, u32[]{:S(2)}) collective-permute-start(bf16[4,2,768,384]{2,3,0,1:T(8,128)(2,1)} %copy.485), channel_id=1, source_target_pairs={{0,4},{4,0},{8,12},{12,8},{16,20},{20,16},{24,28},{28,24},{1,5},{5... | collective-permute-start | bytes 14155784 | tf_op jit(solution)/shard_map/ppermute | solution.py:56
  419.0 93.9 %all-gather.21.cloned.1.call-start = ((), (), s32[]{:S(2)}) async-start(), calls=%async_computation.46 | async-start | bytes 1474560 | tf_op jit(solution)/shard_map/all_gather | solution.py:481
  486.3 96.8 %collective-permute-start.34 = (bf16[3,4,768,128]{2,3,1,0:T(8,128)(2,1)}, bf16[3,4,768,128]{2,3,1,0:T(8,128)(2,1)}, u32[]{:S(2)}, u32[]{:S(2)}) collective-permute-start(bf16[3,4,768,128]{2,3,1,0:T(8,128)(2,1)} %pad_maximum_fusion.39), channel_id=1, source_target_pairs={{0,4},{4,0},{8,12},{12,8},{16,20},{20,16},{24,28},{28,24},{1,5},{5... | collective-permute-start | bytes 7077896 | tf_op jit(solution)/shard_map/ppermute | solution.py:56
  516.4 54.8 %collective-permute-start.40 = (bf16[384,1536]{1,0:T(8,128)(2,1)}, bf16[384,1536]{1,0:T(8,128)(2,1)}, u32[]{:S(2)}, u32[]{:S(2)}) collective-permute-start(bf16[384,1536]{1,0:T(8,128)(2,1)} %bitcast.324), channel_id=1, source_target_pairs={{0,16},{4,20},{8,24},{12,28},{16,0},{20,4},{24,8},{28,12},{1,17},{... | collective-permute-start | bytes 3538952 | tf_op jit(solution)/shard_map/ppermute | solution.py:53
  517.9 57.3 %collective-permute-start.39 = (bf16[384,1536]{1,0:T(8,128)(2,1)}, bf16[384,1536]{1,0:T(8,128)(2,1)}, u32[]{:S(2)}, u32[]{:S(2)}) collective-permute-start(bf16[384,1536]{1,0:T(8,128)(2,1)} %bitcast.324), channel_id=1, source_target_pairs={{0,8},{4,12},{8,0},{12,4},{16,24},{20,28},{24,16},{28,20},{1,9},{5... | collective-permute-start | bytes 3538952 | tf_op jit(solution)/shard_map/ppermute | solution.py:53
  520.9 46.2 %collective-permute-start.31 = (bf16[256,1536]{1,0:T(8,128)(2,1)}, bf16[256,1536]{1,0:T(8,128)(2,1)S(1)}, u32[]{:S(2)}, u32[]{:S(2)}) collective-permute-start(bf16[256,1536]{1,0:T(8,128)(2,1)} %get-tuple-element.196), channel_id=1, source_target_pairs={{0,16},{4,20},{8,24},{12,28},{16,0},{20,4},{24,8},{28,12},{1,17},{... | collective-permute-start | bytes 2359304 | tf_op jit(solution)/shard_map/ppermute | solution.py:53
  521.5 46.5 %collective-permute-start.30 = (bf16[256,1536]{1,0:T(8,128)(2,1)}, bf16[256,1536]{1,0:T(8,128)(2,1)}, u32[]{:S(2)}, u32[]{:S(2)}) collective-permute-start(bf16[256,1536]{1,0:T(8,128)(2,1)} %get-tuple-element.196), channel_id=1, source_target_pairs={{0,8},{4,12},{8,0},{12,4},{16,24},{20,28},{24,16},{28,20},{1,9},{5... | collective-permute-start | bytes 2359304 | tf_op jit(solution)/shard_map/ppermute | solution.py:53
  527.7 51.9 %all-to-all-start.8 = ((bf16[4,2,192,384]{3,2,1,0:T(8,128)(2,1)}), bf16[4,2,192,384]{3,2,1,0:T(8,128)(2,1)}, u32[]{:S(2)}, u32[]{:S(2)}) async-start(bf16[4,2,192,384]{3,2,1,0:T(8,128)(2,1)} %copy.493), calls=%async_computation.8 | async-start | bytes 2359296 | tf_op jit(solution)/shard_map/all_to_all | solution.py:59
  532.0 149.9 %all-gather.13.cloned.1.call-start = ((), (), s32[]{:S(2)}) async-start(), calls=%async_computation.34 | async-start | bytes 5898240 | tf_op jit(solution)/shard_map/all_gather | solution.py:462
  602.6 86.0 %collective-permute-start.43 = (bf16[2,768,1536]{2,1,0:T(8,128)(2,1)}, bf16[2,768,1536]{2,1,0:T(8,128)(2,1)}, u32[]{:S(2)}, u32[]{:S(2)}) collective-permute-start(bf16[2,768,1536]{2,1,0:T(8,128)(2,1)} %bitcast.91), channel_id=1, source_target_pairs={{0,4},{4,0},{8,12},{12,8},{16,20},{20,16},{24,28},{28,24},{1,5},{5... | collective-permute-start | bytes 14155784 | tf_op jit(solution)/shard_map/ppermute | solution.py:56
  658.3 53.2 %collective-permute-start.56 = (bf16[128,1536]{0,1:T(8,128)(2,1)}, bf16[128,1536]{0,1:T(8,128)(2,1)}, u32[]{:S(2)}, u32[]{:S(2)}) collective-permute-start(bf16[128,1536]{0,1:T(8,128)(2,1)} %slice.1032), channel_id=1, source_target_pairs={{0,8},{4,12},{8,0},{12,4},{16,24},{20,28},{24,16},{28,20},{1,9},{5... | collective-permute-start | bytes 1179656 | tf_op jit(solution)/shard_map/ppermute | solution.py:53
  663.1 47.2 %collective-permute-start.55 = (bf16[128,1536]{0,1:T(8,128)(2,1)}, bf16[128,1536]{0,1:T(8,128)(2,1)}, u32[]{:S(2)}, u32[]{:S(2)}) collective-permute-start(bf16[128,1536]{0,1:T(8,128)(2,1)} %slice.1031), channel_id=1, source_target_pairs={{0,16},{4,20},{8,24},{12,28},{16,0},{20,4},{24,8},{28,12},{1,17},{... | collective-permute-start | bytes 1179656 | tf_op jit(solution)/shard_map/ppermute | solution.py:53
  688.6 50.0 %collective-permute-start.48 = (bf16[4,2,768,384]{2,3,0,1:T(8,128)(2,1)}, bf16[4,2,768,384]{2,3,0,1:T(8,128)(2,1)S(1)}, u32[]{:S(2)}, u32[]{:S(2)}) collective-permute-start(bf16[4,2,768,384]{2,3,0,1:T(8,128)(2,1)} %copy.495), channel_id=1, source_target_pairs={{0,4},{4,0},{8,12},{12,8},{16,20},{20,16},{24,28},{28,24},{1,5},{5... | collective-permute-start | bytes 14155784 | tf_op jit(solution)/shard_map/ppermute | solution.py:56
  786.4 152.3 %collective-permute-start.125 = (bf16[4,768,384]{2,1,0:T(8,128)(2,1)}, bf16[4,768,384]{2,1,0:T(8,128)(2,1)}, u32[]{:S(2)}, u32[]{:S(2)}) collective-permute-start(bf16[4,768,384]{2,1,0:T(8,128)(2,1)} %slice.1135), channel_id=1, source_target_pairs={{0,4},{4,0},{8,12},{12,8},{16,20},{20,16},{24,28},{28,24},{1,5},{5... | collective-permute-start | bytes 7077896 | tf_op jit(solution)/shard_map/ppermute | solution.py:56
  786.4 210.9 %collective-permute-start.123 = (bf16[4,768,384]{2,1,0:T(8,128)(2,1)}, bf16[4,768,384]{2,1,0:T(8,128)(2,1)}, u32[]{:S(2)}, u32[]{:S(2)}) collective-permute-start(bf16[4,768,384]{2,1,0:T(8,128)(2,1)} %slice.1131), channel_id=1, source_target_pairs={{0,4},{4,0},{8,12},{12,8},{16,20},{20,16},{24,28},{28,24},{1,5},{5... | collective-permute-start | bytes 7077896 | tf_op jit(solution)/shard_map/ppermute | solution.py:56
  872.5 110.7 %all-to-all-start.9 = ((bf16[4,64,1536]{2,1,0:T(8,128)(2,1)}), bf16[4,64,1536]{2,1,0:T(8,128)(2,1)}, u32[]{:S(2)}, u32[]{:S(2)}) async-start(bf16[4,64,1536]{2,1,0:T(8,128)(2,1)} %reshape_reshape.13), calls=%async_computation.9 | async-start | bytes 1572864 | tf_op jit(solution)/shard_map/all_to_all | solution.py:65
  876.7 481.8 %reduce-scatter.23.cloned.1.call-start = ((), (), s32[]{:S(2)}) async-start(), calls=%async_computation.42 | async-start | bytes 2949120 | tf_op jit(solution)/shard_map/reduce_scatter | solution.py:473
  906.7 124.8 %collective-permute-start.116 = (bf16[768,1536]{1,0:T(8,128)(2,1)}, bf16[768,1536]{1,0:T(8,128)(2,1)}, u32[]{:S(2)}, u32[]{:S(2)}) collective-permute-start(bf16[768,1536]{1,0:T(8,128)(2,1)} %slice.1122), channel_id=1, source_target_pairs={{0,4},{4,0},{8,12},{12,8},{16,20},{20,16},{24,28},{28,24},{1,5},{5... | collective-permute-start | bytes 7077896 | tf_op jit(solution)/shard_map/ppermute | solution.py:56
  935.8 90.7 %collective-permute-start.117 = (bf16[768,1536]{1,0:T(8,128)(2,1)}, bf16[768,1536]{1,0:T(8,128)(2,1)}, u32[]{:S(2)}, u32[]{:S(2)}) collective-permute-start(bf16[768,1536]{1,0:T(8,128)(2,1)} %slice.1124), channel_id=1, source_target_pairs={{0,4},{4,0},{8,12},{12,8},{16,20},{20,16},{24,28},{28,24},{1,5},{5... | collective-permute-start | bytes 7077896 | tf_op jit(solution)/shard_map/ppermute | solution.py:56
  987.4 377.7 %reduce-scatter.19.cloned.1.call-start = ((), (), s32[]{:S(2)}) async-start(), calls=%async_computation.40 | async-start | bytes 2949120 | tf_op jit(solution)/shard_map/reduce_scatter | solution.py:473
  987.9 139.3 %collective-permute-start.109 = (bf16[3,768,512]{1,2,0:T(8,128)(2,1)}, bf16[3,768,512]{1,2,0:T(8,128)(2,1)}, u32[]{:S(2)}, u32[]{:S(2)}) collective-permute-start(bf16[3,768,512]{1,2,0:T(8,128)(2,1)} %pad_maximum_fusion.36), channel_id=1, source_target_pairs={{0,4},{4,0},{8,12},{12,8},{16,20},{20,16},{24,28},{28,24},{1,5},{5... | collective-permute-start | bytes 7077896 | tf_op jit(solution)/shard_map/ppermute | solution.py:56
  1002.4 445.4 %reduce-scatter.15.cloned.1.call-start = ((), (), s32[]{:S(2)}) async-start(), calls=%async_computation.38 | async-start | bytes 1474560 | tf_op jit(solution)/shard_map/reduce_scatter | solution.py:500
  1057.4 74.6 %collective-permute-start.119 = (bf16[384,1536]{1,0:T(8,128)(2,1)S(1)}, bf16[384,1536]{1,0:T(8,128)(2,1)S(1)}, u32[]{:S(2)}, u32[]{:S(2)}) collective-permute-start(bf16[384,1536]{1,0:T(8,128)(2,1)S(1)} %add_convert_fusion.12), channel_id=1, source_target_pairs={{0,16},{4,20},{8,24},{12,28},{16,0},{20,4},{24,8},{28,12},{1,17},{... | collective-permute-start | bytes 3538952 | tf_op jit(solution)/shard_map/ppermute | solution.py:53
  1058.2 73.8 %collective-permute-start.121 = (bf16[384,1536]{1,0:T(8,128)(2,1)S(1)}, bf16[384,1536]{1,0:T(8,128)(2,1)S(1)}, u32[]{:S(2)}, u32[]{:S(2)}) collective-permute-start(bf16[384,1536]{1,0:T(8,128)(2,1)S(1)} %add_convert_fusion.11), channel_id=1, source_target_pairs={{0,8},{4,12},{8,0},{12,4},{16,24},{20,28},{24,16},{28,20},{1,9},{5... | collective-permute-start | bytes 3538952 | tf_op jit(solution)/shard_map/ppermute | solution.py:53
  1121.1 91.7 %collective-permute-start.124 = (bf16[4,768,384]{2,1,0:T(8,128)(2,1)}, bf16[4,768,384]{2,1,0:T(8,128)(2,1)}, u32[]{:S(2)}, u32[]{:S(2)}) collective-permute-start(bf16[4,768,384]{2,1,0:T(8,128)(2,1)} %slice.1133), channel_id=1, source_target_pairs={{0,4},{4,0},{8,12},{12,8},{16,20},{20,16},{24,28},{28,24},{1,5},{5... | collective-permute-start | bytes 7077896 | tf_op jit(solution)/shard_map/ppermute | solution.py:56
  1131.9 132.5 %collective-permute-start.122 = (bf16[4,768,384]{2,1,0:T(8,128)(2,1)}, bf16[4,768,384]{2,1,0:T(8,128)(2,1)}, u32[]{:S(2)}, u32[]{:S(2)}) collective-permute-start(bf16[4,768,384]{2,1,0:T(8,128)(2,1)} %slice.1129), channel_id=1, source_target_pairs={{0,4},{4,0},{8,12},{12,8},{16,20},{20,16},{24,28},{28,24},{1,5},{5... | collective-permute-start | bytes 7077896 | tf_op jit(solution)/shard_map/ppermute | solution.py:56
  1134.2 321.4 %reduce-scatter.11.cloned.1.call-start = ((), (), s32[]{:S(2)}) async-start(), calls=%async_computation.36 | async-start | bytes 3932160 | tf_op jit(solution)/shard_map/reduce_scatter | solution.py:445
  1181.8 290.4 %reduce-scatter.21.cloned.1.call-start = ((), (), s32[]{:S(2)}) async-start(), calls=%async_computation.41 | async-start | bytes 2949120 | tf_op jit(solution)/shard_map/reduce_scatter | solution.py:473
  1217.3 261.0 %reduce-scatter.17.cloned.1.call-start = ((), (), s32[]{:S(2)}) async-start(), calls=%async_computation.39 | async-start | bytes 2949120 | tf_op jit(solution)/shard_map/reduce_scatter | solution.py:473
  1283.0 52.7 %collective-permute-start.108 = (bf16[3,768,512]{1,2,0:T(8,128)(2,1)}, bf16[3,768,512]{1,2,0:T(8,128)(2,1)}, u32[]{:S(2)}, u32[]{:S(2)}) collective-permute-start(bf16[3,768,512]{1,2,0:T(8,128)(2,1)} %pad_maximum_fusion.37), channel_id=1, source_target_pairs={{0,4},{4,0},{8,12},{12,8},{16,20},{20,16},{24,28},{28,24},{1,5},{5... | collective-permute-start | bytes 7077896 | tf_op jit(solution)/shard_map/ppermute | solution.py:56
  1327.8 170.5 %reduce-scatter.9.cloned.1.call-start = ((), (), s32[]{:S(2)}) async-start(), calls=%async_computation.35 | async-start | bytes 3932160 | tf_op jit(solution)/shard_map/reduce_scatter | solution.py:445
  1392.3 44.1 %all-to-all-start.13 = ((bf16[4,64,1536]{2,1,0:T(8,128)(2,1)}), bf16[4,64,1536]{2,1,0:T(8,128)(2,1)}, u32[]{:S(2)}, u32[]{:S(2)}) async-start(bf16[4,64,1536]{2,1,0:T(8,128)(2,1)} %reshape_reshape.15), calls=%async_computation.13 | async-start | bytes 1572864 | tf_op jit(solution)/shard_map/all_to_all | solution.py:65
  1399.7 62.6 %collective-permute-start.113 = (bf16[384,1536]{1,0:T(8,128)(2,1)}, bf16[384,1536]{1,0:T(8,128)(2,1)}, u32[]{:S(2)}, u32[]{:S(2)}) collective-permute-start(bf16[384,1536]{1,0:T(8,128)(2,1)} %add_convert_fusion.15), channel_id=1, source_target_pairs={{0,16},{4,20},{8,24},{12,28},{16,0},{20,4},{24,8},{28,12},{1,17},{... | collective-permute-start | bytes 3538952 | tf_op jit(solution)/shard_map/ppermute | solution.py:53
  1408.0 54.3 %collective-permute-start.115 = (bf16[384,1536]{1,0:T(8,128)(2,1)}, bf16[384,1536]{1,0:T(8,128)(2,1)}, u32[]{:S(2)}, u32[]{:S(2)}) collective-permute-start(bf16[384,1536]{1,0:T(8,128)(2,1)} %add_convert_fusion.14), channel_id=1, source_target_pairs={{0,8},{4,12},{8,0},{12,4},{16,24},{20,28},{24,16},{28,20},{1,9},{5... | collective-permute-start | bytes 3538952 | tf_op jit(solution)/shard_map/ppermute | solution.py:53
  1462.0 43.7 %reduce-scatter.13.cloned.1.call-start = ((), (), s32[]{:S(2)}) async-start(), calls=%async_computation.37 | async-start | bytes 1474560 | tf_op jit(solution)/shard_map/reduce_scatter | solution.py:500
  (369 other events, 5725.9 us)
Sparse Core Ops, SparseCore 0:
  57.5 84.7 all-gather.14
  172.8 28.1 all-gather.16
  269.9 87.4 all-gather.10
  419.1 61.2 all-gather.18
  483.7 29.0 all-gather.20
  582.3 87.0 all-gather.12
  942.5 48.5 reduce-scatter.22
  1002.5 47.5 reduce-scatter.18
  1134.3 29.7 reduce-scatter.14
  1167.5 62.2 reduce-scatter.10
  1232.1 48.0 reduce-scatter.20
  1282.4 51.6 reduce-scatter.16
  1341.2 60.5 reduce-scatter.8
  1466.1 29.6 reduce-scatter.12

commit v2 on v1

v2 whole, which is shorter than its diff:
```python
import functools

import jax
import jax.numpy as jnp
from jax import lax
from jax.experimental import pallas as pl
from jax.experimental.pallas import tpu as pltpu
from jax.sharding import PartitionSpec as P

HEAD = 64
CLIP_LEN = 1024
LAYERS = 2
SCALE = 0.125
EPS = 1e-05
NEG = -1e30
BF = jnp.bfloat16
F32 = jnp.float32
VMEM_LIMIT = 48 * 2**20
COST = CLIP_LEN * CLIP_LEN * 8


def product(left, right):
    return jnp.dot(left, right, preferred_element_type=F32)


def product_tn(left, right):
    return lax.dot_general(left, right, (((0,), (0,)), ((), ())), preferred_element_type=F32)


def product_nt(left, right):
    return lax.dot_general(left, right, (((1,), (1,)), ((), ())), preferred_element_type=F32)


def after(value, token):
    return lax.optimization_barrier((value, token))[0]


def tied(values, others):
    leaves, tree = jax.tree.flatten(values)
    arrays = [leaf for leaf in leaves if not isinstance(leaf, int)]
    others = [leaf for leaf in jax.tree.leaves(others) if not isinstance(leaf, int)]
    done = iter(lax.optimization_barrier((arrays, others))[0])
    return jax.tree.unflatten(tree, [leaf if isinstance(leaf, int) else next(done) for leaf in leaves])


def meet(values, fill):
    return tied((values, fill), [])


def joined(pieces):
    return pieces[0] if len(pieces) == 1 else jnp.concatenate(pieces, axis=0)


def flat(pieces):
    return [array for piece in pieces for array in piece]


class Grid:
    def __init__(self, mesh):
        self.R = mesh.shape["row"]
        self.C = mesh.shape["col"]
        self.T = self.R // 2
        assert self.T == self.C
        self.groups = [[2 * i + core for i in range(self.T)] for core in range(2)]

    def at(self):
        row = lax.axis_index("row")
        self.i = row // 2
        self.core = row % 2
        self.z = lax.axis_index("col")

    def swap(self, value, d):
        return lax.ppermute(value, "row", [(r, r ^ (2 * d)) for r in range(self.R)])

    def core_swap(self, value):
        return lax.ppermute(value, "row", [(r, r ^ 1) for r in range(self.R)])

    def plane_a2a(self, value):
        return lax.all_to_all(value, "row", 0, 0, tiled=True, axis_index_groups=self.groups)

    def row_a2a(self, value):
        return lax.all_to_all(value, "row", 0, 0, tiled=True)

    def col_a2a(self, value):
        return lax.all_to_all(value, "col", 0, 0, tiled=True)

    def distances(self):
        return sorted(range(1, self.T), key=lambda d: (bin(d).count("1"), d))

    def order(self):
        return [0] + self.distances()

    def gather_begin(self, own):
        return [own] + [self.swap(own, d) for d in self.distances() if d & (d - 1) == 0]

    def gather_end(self, near):
        half = near[0].shape[0] // 2
        pieces = {d: [piece] for d, piece in zip([0] + [d for d in self.distances() if d & (d - 1) == 0], near)}

        def part(d, upper):
            if len(pieces[d]) == 2:
                return pieces[d][upper]
            return pieces[d][0][half:] if upper else pieces[d][0][:half]

        for d in self.distances():
            high = 1 << (d.bit_length() - 1)
            low = d & -d
            if high != low:
                pieces[d] = [self.swap(part(d ^ high, 0), high), self.swap(part(d ^ low, 1), low)]
        return [pieces[d] for d in self.order()]

    def gather(self, own):
        return self.gather_end(self.gather_begin(own))

    def scatter_begin(self, top):
        d = self.order()[-1]
        high = 1 << (d.bit_length() - 1)
        low = d & -d
        return [(d ^ high, 0, self.swap(top[0], high)), (d ^ low, 1, self.swap(top[1], low))]

    def scatter_end(self, state, rest, fill=()):
        held = []
        order = self.order()
        state = list(state)
        for n in reversed(range(1, self.T - 1)):
            d = order[n]
            high = 1 << (d.bit_length() - 1)
            low = d & -d
            half = rest[n].shape[0] // 2
            parts = [rest[n][:half], rest[n][half:]]
            for goal, upper, value in state:
                if goal == d:
                    parts[upper] = parts[upper] + value.astype(F32)
            parts = [part.astype(BF) for part in parts]
            if high == low:
                held.append(self.swap(joined(parts), d))
            else:
                state += [(d ^ high, 0, self.swap(parts[0], high)), (d ^ low, 1, self.swap(parts[1], low))]
        total = rest[0]
        held, fill = meet(held, fill)
        for value in held:
            total = total + value.astype(F32)
        return total, fill

    def scatter(self, top, rest, fill=()):
        return self.scatter_end(self.scatter_begin(top), rest, fill)

    def natural(self, pieces):
        by_distance = [None] * self.T
        for d, piece in zip(self.order(), pieces):
            by_distance[d] = joined(piece)
        return self.picked(by_distance, [self.i ^ m for m in range(self.T)])

    def picked(self, parts, indices):
        stacked = jnp.stack(parts)
        return [lax.dynamic_index_in_dim(stacked, index, 0, keepdims=False) for index in indices]

    def col_swap(self, value, d):
        if d == 0:
            return value
        return lax.ppermute(value, "col", [(c, c ^ d) for c in range(self.C)])

    def plane_swap(self, value, d):
        return self.swap(value, d) if d else value

    def tokens_in(self, block, mid=None):
        rows, width = block.shape
        parts = block.reshape(self.T, rows // self.T, width)
        sent = [lax.dynamic_index_in_dim(parts, self.i ^ d, 0, keepdims=False) for d in range(self.T)]
        got = [self.plane_swap(sent[d], d) for d in range(self.T)]
        got = got if mid is None else tied(got, mid)
        sent = self.picked(got, [self.i ^ self.z ^ e for e in range(self.C)])
        return joined([self.col_swap(sent[e], e) for e in range(self.C)])

    def tokens_out_begin(self, block):
        small = block.shape[0] // self.C
        return [self.col_swap(block[e * small : (e + 1) * small], e) for e in range(self.C)]

    def tokens_out_end(self, got):
        sent = self.picked(got, [self.i ^ self.z ^ d for d in range(self.T)])
        got = [self.plane_swap(sent[d], d) for d in range(self.T)]
        return joined(self.picked(got, [self.i ^ m for m in range(self.T)]))

    def tokens_out(self, block):
        return self.tokens_out_end(self.tokens_out_begin(block))

    def total(self, value):
        for d in range(self.R.bit_length() - 1):
            value = value + lax.ppermute(value, "row", [(r, r ^ (1 << d)) for r in range(self.R)])
        for d in range(self.C.bit_length() - 1):
            value = value + lax.ppermute(value, "col", [(c, c ^ (1 << d)) for c in range(self.C)])
        return value


def gelu_parts(u):
    cdf = 0.5 * (1.0 + lax.erf(u * (0.5**0.5)))
    pdf = jnp.exp(-0.5 * u * u) * (0.5 / jnp.pi) ** 0.5
    return u * cdf, cdf + u * pdf


def norm_forward(residual, gain, shift):
    row_mean = jnp.mean(residual, axis=1, keepdims=True)
    centered = residual - row_mean
    variance = jnp.mean(centered * centered, axis=1, keepdims=True)
    inv_std = lax.rsqrt(variance + EPS)
    normed = centered * inv_std
    return (normed, inv_std, (normed * gain + shift).astype(BF))


def norm_backward(grad_out, normed, inv_std, gain):
    scaled = grad_out * gain
    row_mean = jnp.mean(scaled, axis=1, keepdims=True)
    row_along = jnp.mean(scaled * normed, axis=1, keepdims=True)
    grad_in = inv_std * (scaled - row_mean - normed * row_along)
    return (grad_in, jnp.sum(grad_out * normed, axis=0), jnp.sum(grad_out, axis=0))


def to_clip(grid, at_ref, source, target):
    rows = CLIP_LEN // grid.T
    small = rows // grid.C
    for n, d in enumerate(grid.order()):
        for e in range(grid.C):
            start = pl.multiple_of((at_ref[0] ^ d) * small + (at_ref[1] ^ e) * rows, small)
            low = n * rows + e * small
            target[pl.ds(start, small), :] = source[low : low + small, :]


def from_clip(grid, at_ref, block, k, target):
    rows = CLIP_LEN // grid.T
    small = rows // grid.C
    for n, d in enumerate(grid.order()):
        start = pl.multiple_of((at_ref[0] ^ d) * small, small)
        goal = pl.multiple_of(n * rows + (at_ref[1] ^ k) * small, small)
        target[pl.ds(goal, small), :] = block[pl.ds(start, small), :]


def causal_block(scores_t, size):
    keys = lax.broadcasted_iota(jnp.int32, (size, size), 0)
    asks = lax.broadcasted_iota(jnp.int32, (size, size), 1)
    last = scores_t.shape[0] - size
    edge = jnp.where(keys <= asks, scores_t[last:], NEG)
    return edge if last == 0 else jnp.concatenate([scores_t[:last], edge], axis=0)


def dot_nt(left, right):
    return lax.dot_general(left, right, (((1,), (1,)), ((), ())), preferred_element_type=F32)


def dot_nn(left, right):
    return lax.dot_general(left, right, (((1,), (0,)), ((), ())), preferred_element_type=F32)


def flip(value):
    return value.astype(F32).T


def self_forward_kernel(grid, width, at_ref, x_ref, out_ref, sums_ref, clip, block):
    size = CLIP_LEN // grid.C
    to_clip(grid, at_ref, x_ref, clip)
    heads = range(width // HEAD)

    def lanes(which, h):
        return slice(which * width + h * HEAD, which * width + (h + 1) * HEAD)

    keys = [clip[:, lanes(1, h)] for h in heads]
    values_t = [flip(clip[:, lanes(2, h)]).astype(BF) for h in heads]
    for k in range(grid.C):
        low, high = k * size, (k + 1) * size
        outs = []
        for h in heads:
            asks = clip[low:high, lanes(0, h)] * BF(SCALE)
            scores = causal_block(dot_nt(keys[h][:high], asks), size)
            top = jnp.max(scores, axis=0, keepdims=True)
            weight = jnp.exp(scores - top)
            total = jnp.sum(weight, axis=0, keepdims=True)
            outs.append(dot_nn(values_t[h][:, :high], weight.astype(BF)) / total)
            sums_ref[h : h + 1, low:high] = top + jnp.log(total)
        both = outs[0] if len(outs) == 1 else jnp.concatenate(outs, axis=0)
        block[...] = both.T.astype(BF)
        from_clip(grid, at_ref, block, k, out_ref)


def self_backward_kernel(grid, width, at_ref, x_ref, da_ref, sums_ref, out_ref, clip, da_clip, block, acc):
    size = CLIP_LEN // grid.C
    to_clip(grid, at_ref, x_ref, clip)
    to_clip(grid, at_ref, da_ref, da_clip)
    heads = range(width // HEAD)

    def lanes(which, h):
        return slice(which * width + h * HEAD, which * width + (h + 1) * HEAD)

    keys = [clip[:, lanes(1, h)] for h in heads]
    values = [clip[:, lanes(2, h)] for h in heads]
    keys_t = [flip(keys[h]).astype(BF) for h in heads]
    for k in reversed(range(grid.C)):
        low, high = k * size, (k + 1) * size
        dq = []
        for h in heads:
            asks = clip[low:high, lanes(0, h)] * BF(SCALE)
            da = da_clip[low:high, lanes(0, h)]
            scores = causal_block(dot_nt(keys[h][:high], asks), size)
            probs = jnp.exp(scores - sums_ref[h : h + 1, low:high])
            d_probs = dot_nt(values[h][:high], da)
            inner = jnp.sum(probs * d_probs, axis=0, keepdims=True)
            d_scores = (probs * (d_probs - inner)).astype(BF)
            dk = dot_nn(d_scores, asks)
            dv = dot_nn(probs.astype(BF), da)
            if k == grid.C - 1:
                acc[:, lanes(0, h)] = dk
                acc[:, lanes(1, h)] = dv
            else:
                acc[:high, lanes(0, h)] += dk
                acc[:high, lanes(1, h)] += dv
            dq.append(dot_nn(keys_t[h][:, :high], d_scores) * SCALE)
        both = dq[0] if len(dq) == 1 else jnp.concatenate(dq, axis=0)
        block[:, :width] = both.T.astype(BF)
        block[:, width:] = acc[low:high, :].astype(BF)
        from_clip(grid, at_ref, block, k, out_ref)


def unit_spec(rows, lanes):
    return pl.BlockSpec((None, rows, lanes), lambda n, *at: (n, 0, 0))


def self_attention(grid, x):
    units, _, width = x.shape
    width //= 3
    size = CLIP_LEN // grid.C
    return pl.pallas_call(
        functools.partial(self_forward_kernel, grid, width),
        grid_spec=pltpu.PrefetchScalarGridSpec(
            num_scalar_prefetch=1,
            grid=(units,),
            in_specs=[unit_spec(CLIP_LEN, 3 * width)],
            out_specs=[unit_spec(CLIP_LEN, width), unit_spec(8, CLIP_LEN)],
            scratch_shapes=[pltpu.VMEM((CLIP_LEN, 3 * width), BF), pltpu.VMEM((size, width), BF)],
        ),
        out_shape=[
            jax.ShapeDtypeStruct((units, CLIP_LEN, width), BF),
            jax.ShapeDtypeStruct((units, 8, CLIP_LEN), F32),
        ],
        compiler_params=pltpu.CompilerParams(vmem_limit_bytes=VMEM_LIMIT),
        cost_estimate=pl.CostEstimate(
            flops=COST * units * width, bytes_accessed=CLIP_LEN * units * width * 8, transcendentals=0
        ),
        name="self_attention",
    )(jnp.stack([grid.i, grid.z]), x)


def self_attention_grad(grid, x, da, sums):
    units, _, width = da.shape
    size = CLIP_LEN // grid.C
    return pl.pallas_call(
        functools.partial(self_backward_kernel, grid, width),
        grid_spec=pltpu.PrefetchScalarGridSpec(
            num_scalar_prefetch=1,
            grid=(units,),
            in_specs=[unit_spec(CLIP_LEN, 3 * width), unit_spec(CLIP_LEN, width), unit_spec(8, CLIP_LEN)],
            out_specs=unit_spec(CLIP_LEN, 3 * width),
            scratch_shapes=[
                pltpu.VMEM((CLIP_LEN, 3 * width), BF),
                pltpu.VMEM((CLIP_LEN, width), BF),
                pltpu.VMEM((size, 3 * width), BF),
                pltpu.VMEM((CLIP_LEN, 2 * width), F32),
            ],
        ),
        out_shape=jax.ShapeDtypeStruct((units, CLIP_LEN, 3 * width), BF),
        compiler_params=pltpu.CompilerParams(vmem_limit_bytes=VMEM_LIMIT),
        cost_estimate=pl.CostEstimate(
            flops=3 * COST * units * width, bytes_accessed=CLIP_LEN * units * width * 16, transcendentals=0
        ),
        name="self_attention_grad",
    )(jnp.stack([grid.i, grid.z]), x, da, sums)


def reorder_kernel(spans, core_ref, x_ref, out_ref):
    for core in range(2):

        @pl.when(core_ref[0] == core)
        def _(core=core):
            out_ref[...] = jnp.concatenate([x_ref[:, low : low + size] for low, size in spans[core]], axis=1)


def reorder(grid, x, back):
    rows, width = x.shape
    size = width // grid.R
    half = width // 2
    if back:
        spans = [[((r % 2 != core) * half + r // 2 * size, size) for r in range(grid.R)] for core in range(2)]
    else:
        spans = [[((2 * i + (core + n) % 2) * size, size) for n in range(2) for i in range(grid.T)] for core in range(2)]
    return pl.pallas_call(
        functools.partial(reorder_kernel, spans),
        grid_spec=pltpu.PrefetchScalarGridSpec(
            num_scalar_prefetch=1,
            grid=(1,),
            in_specs=[pl.BlockSpec((rows, width), lambda n, core: (0, 0))],
            out_specs=pl.BlockSpec((rows, width), lambda n, core: (0, 0)),
        ),
        out_shape=jax.ShapeDtypeStruct((rows, width), x.dtype),
        name="reorder",
    )(grid.core.reshape(1), x)


def own_first(grid, x):
    return reorder(grid, x, False)


def own_last(grid, x):
    return reorder(grid, x, True)


def lanes_of(ref, mats):
    parts = [ref[m] for m in mats]
    return parts[0] if len(parts) == 1 else jnp.concatenate(parts, axis=1)


def columns_kernel(mats, count, kind, *refs):
    pieces, (own_ref, other_ref), rest = refs[:count], refs[count : count + 2], refs[count + 2 :]
    own, other = lanes_of(own_ref, mats), lanes_of(other_ref, mats)
    half = own.shape[0]
    low = 0
    for piece in pieces:
        high = low + piece.shape[0]
        out = dot_nn(piece[:, :half], own) + dot_nn(piece[:, half:], other)
        if kind == "gelu":
            value, slope = gelu_parts(out)
            rest[0][low:high] = value.astype(BF)
            rest[1][low:high] = slope.astype(BF)
        elif kind == "slope":
            rest[1][low:high] = (out * rest[0][low:high].astype(F32)).astype(BF)
        else:
            rest[0][low:high] = out.astype(BF)
        low = high


def whole(array):
    return pl.BlockSpec(array.shape, lambda n: (0,) * array.ndim)


def act_spec(rows, lanes):
    return pl.BlockSpec((None, rows, lanes), lambda n: (n, 0, 0))


def columns_product(pieces, weights, mats, kind="plain", slope=None):
    own, other = weights
    blocks, _, half, wide = own.shape
    lanes = len(mats) * wide
    rows = sum(p.shape[0] for p in pieces)
    extra = [] if slope is None else [slope]
    outs = 2 if kind == "gelu" else 1
    shape = jax.ShapeDtypeStruct((blocks, rows, lanes), BF)
    first, picked = (mats[0], 1) if len(mats) == 1 else (0, own.shape[1])
    spec = pl.BlockSpec((None, picked) + own.shape[2:], lambda n: (n, first, 0, 0))
    result = pl.pallas_call(
        functools.partial(columns_kernel, (0,) if len(mats) == 1 else mats, len(pieces), kind),
        grid=(blocks,),
        in_specs=[whole(p) for p in pieces] + [spec, spec] + [act_spec(rows, lanes)] * len(extra),
        out_specs=[act_spec(rows, lanes)] * outs,
        out_shape=[shape] * outs,
        compiler_params=pltpu.CompilerParams(vmem_limit_bytes=VMEM_LIMIT),
        cost_estimate=pl.CostEstimate(flops=4 * half * rows * lanes * blocks, bytes_accessed=4 * half * lanes * blocks, transcendentals=0),
        name="columns_" + kind,
    )(*pieces, own, other, *extra)
    return result if outs > 1 else result[0]


def rows_kernel(mats, low, high, act_ref, own_ref, other_ref, *outs):
    blocks = act_ref.shape[0]
    acts = [act_ref[n, low:high] for n in range(blocks)]
    half = own_ref.shape[2]
    for cols, ref in ((slice(0, half), own_ref), (slice(half, 2 * half), other_ref)):
        parts = [lanes_of(ref.at[n], mats) for n in range(blocks)]
        if parts[0].shape[1] < 256:
            total = dot_nt(jnp.concatenate(acts, axis=1), jnp.concatenate(parts, axis=1))
        else:
            total = dot_nt(acts[0], parts[0])
            for act, part in zip(acts[1:], parts[1:]):
                total = total + dot_nt(act, part)
        at = 0
        for out in outs:
            out[:, cols] = total[at : at + out.shape[0]].astype(out.dtype)
            at += out.shape[0]


def rows_product(act, weights, mats, low, high, shapes):
    own, other = weights
    blocks, _, half, _ = own.shape
    lanes = act.shape[2]
    first, count = (mats[0], 1) if len(mats) == 1 else (0, own.shape[1])
    spec = pl.BlockSpec((blocks, count) + own.shape[2:], lambda n: (0, first, 0, 0))
    return pl.pallas_call(
        functools.partial(rows_kernel, (0,) if len(mats) == 1 else mats, low, high),
        grid=(1,),
        in_specs=[whole(act), spec, spec],
        out_specs=[whole(s) for s in shapes],
        out_shape=shapes,
        compiler_params=pltpu.CompilerParams(vmem_limit_bytes=VMEM_LIMIT),
        cost_estimate=pl.CostEstimate(
            flops=4 * half * (high - low) * lanes * blocks, bytes_accessed=4 * half * lanes * blocks, transcendentals=0
        ),
        name="rows",
    )(act, own, other)


def rows_top(grid, act, weights, mats):
    rows = act.shape[1] // grid.T
    shapes = [jax.ShapeDtypeStruct((rows // 2, 2 * weights[0].shape[2]), BF)] * 2
    return list(rows_product(act, weights, mats, rows * (grid.T - 1), rows * grid.T, shapes))


def rows_rest(grid, act, weights, mats):
    rows = act.shape[1] // grid.T
    shapes = [jax.ShapeDtypeStruct((rows, 2 * weights[0].shape[2]), F32)] * (grid.T - 1)
    return list(rows_product(act, weights, mats, 0, rows * (grid.T - 1), shapes))


def rows_terms(grid, act, weights, mats):
    top = rows_top(grid, act, weights, mats)
    return top, rows_rest(grid, after(act, top), weights, mats)


def grads_kernel(count, *refs):
    pieces, y_ref, keep_ref, send_ref, turned = refs[:count], refs[count], refs[count + 1], refs[count + 2], refs[count + 3]
    half = keep_ref.shape[0]

    @pl.when(pl.program_id(0) == 0)
    def _():
        low = 0
        for piece in pieces:
            high = low + piece.shape[0]
            turned[:, low:high] = piece[...].T
            low = high

    y = y_ref[...]
    keep_ref[...] = dot_nn(turned[:half], y).astype(BF)
    send_ref[...] = dot_nn(turned[half:], y).astype(BF)


def weight_grads(pieces, y):
    blocks, rows, lanes = y.shape
    width = pieces[0].shape[1]
    half = width // 2
    shape = jax.ShapeDtypeStruct((blocks, half, lanes), BF)
    return pl.pallas_call(
        functools.partial(grads_kernel, len(pieces)),
        grid=(blocks,),
        in_specs=[whole(p) for p in pieces] + [act_spec(rows, lanes)],
        out_specs=[act_spec(half, lanes)] * 2,
        out_shape=[shape] * 2,
        scratch_shapes=[pltpu.VMEM((width, rows), BF)],
        compiler_params=pltpu.CompilerParams(vmem_limit_bytes=VMEM_LIMIT),
        cost_estimate=pl.CostEstimate(flops=4 * half * rows * lanes * blocks, bytes_accessed=4 * half * lanes * blocks, transcendentals=0),
        name="weight_grads",
    )(*pieces, y)


def cross_scores(keys, asks):
    scores = dot_nt(keys, asks)
    top = jnp.max(scores, axis=0, keepdims=True)
    weight = jnp.exp(scores - top)
    return weight / jnp.sum(weight, axis=0, keepdims=True)


def cross_forward_kernel(q_ref, k_ref, v_ref, out_ref):
    for low in range(0, q_ref.shape[1], 2 * HEAD):
        pair = []
        for at in (slice(low, low + HEAD), slice(low + HEAD, low + 2 * HEAD)):
            probs = cross_scores(k_ref[:, at], q_ref[:, at] * BF(SCALE)).astype(BF)
            pair.append(dot_nn(flip(v_ref[:, at]).astype(BF), probs))
        out_ref[:, low : low + 2 * HEAD] = jnp.concatenate(pair, axis=0).T.astype(BF)


def cross_backward_kernel(q_ref, k_ref, v_ref, dc_ref, dq_ref, dk_ref, dv_ref):
    for low in range(0, q_ref.shape[1], 2 * HEAD):
        pair, dk, dv = [], [], []
        for at in (slice(low, low + HEAD), slice(low + HEAD, low + 2 * HEAD)):
            asks = q_ref[:, at] * BF(SCALE)
            probs = cross_scores(k_ref[:, at], asks)
            d_probs = dot_nt(v_ref[:, at], dc_ref[:, at])
            inner = jnp.sum(probs * d_probs, axis=0, keepdims=True)
            d_scores = (probs * (d_probs - inner)).astype(BF)
            dk.append(dot_nn(d_scores, asks))
            dv.append(dot_nn(probs.astype(BF), dc_ref[:, at]))
            pair.append(dot_nn(flip(k_ref[:, at]).astype(BF), d_scores) * SCALE)
        at = slice(low, low + 2 * HEAD)
        dq_ref[:, at] = jnp.concatenate(pair, axis=0).T.astype(BF)
        dk_ref[:, at] = jnp.concatenate(dk, axis=1)
        dv_ref[:, at] = jnp.concatenate(dv, axis=1)


def cross_call(kernel, name, arrays, outs):
    width = arrays[0].shape[1]
    lanes = 512 if width % 512 == 0 else width

    def spec(rows):
        return pl.BlockSpec((rows, lanes), lambda n: (0, n))

    return pl.pallas_call(
        kernel,
        grid=(width // lanes,),
        in_specs=[spec(a.shape[0]) for a in arrays],
        out_specs=[spec(rows) for rows, _ in outs],
        out_shape=[jax.ShapeDtypeStruct((rows, width), kind) for rows, kind in outs],
        compiler_params=pltpu.CompilerParams(vmem_limit_bytes=VMEM_LIMIT),
        cost_estimate=pl.CostEstimate(
            flops=arrays[0].shape[0] * arrays[1].shape[0] * width * 20, bytes_accessed=2**22, transcendentals=0
        ),
        name=name,
    )(*arrays)


def cross_attention(queries, keys, values):
    return cross_call(cross_forward_kernel, "cross_attention", [queries, keys, values], [(queries.shape[0], BF)])[0]


def cross_attention_grad(queries, keys, values, grad_out):
    outs = [(queries.shape[0], BF), (keys.shape[0], F32), (keys.shape[0], F32)]
    return cross_call(cross_backward_kernel, "cross_attention_grad", [queries, keys, values, grad_out], outs)


def head_units(grid, width):
    heads = width // HEAD
    per_unit = -(-heads // grid.T)
    assert heads % per_unit == 0
    return heads // per_unit, per_unit * HEAD


def self_slots(grid, mats):
    units, wide = head_units(grid, mats[0].shape[1])
    both = jnp.stack(mats)
    lows = [jnp.minimum((s - grid.z - 1) % grid.T, units - 1) * wide for s in range(grid.T)]
    return jnp.stack([lax.dynamic_slice_in_dim(both, low, wide, axis=2) for low in lows])


def by_matrix(moved):
    sources, count, rows, wide = moved.shape
    return moved.transpose(1, 0, 2, 3).reshape(count, sources * rows, wide)


def self_weights(grid, slots, units):
    half = jnp.stack(
        [lax.dynamic_index_in_dim(slots, (grid.i - 1 - m) % grid.T, 0, keepdims=False) for m in range(units)]
    )
    return half, grid.core_swap(half)


def core_sum(grid, keep, send, mid):
    got = tied(grid.core_swap(send), mid)
    return (keep.astype(F32) + got.astype(F32)).astype(BF)


def self_grad_slots(grid, pairs, mid):
    half = jnp.concatenate([core_sum(grid, *pair, mid) for pair in pairs], axis=2)
    half = jnp.concatenate([half, jnp.zeros((grid.C - half.shape[0],) + half.shape[1:], BF)], axis=0)
    return jnp.stack(
        [lax.dynamic_index_in_dim(half, (grid.i - c - 1) % grid.T, 0, keepdims=False) for c in range(grid.C)]
    )


def self_grad_blocks(grid, moved, units):
    wide = moved.shape[2] // 4
    mine = [lax.dynamic_index_in_dim(moved, (grid.z + 1 + m) % grid.T, 0, keepdims=False) for m in range(units)]
    return [
        jnp.concatenate([part[:, n * wide : (n + 1) * wide] for part in mine], axis=1).astype(F32) for n in range(4)
    ]


def hidden_slots(grid, mats):
    rows, width = mats[0].shape
    count = len(mats)
    return jnp.stack(mats).reshape(count, rows, grid.T, width // grid.T).transpose(2, 0, 1, 3)


def hidden_gathered(moved, n, token):
    sources, _, rows, wide = moved.shape
    return lax.all_gather(after(moved[:, n].reshape(1, sources * rows, wide), token), "col", axis=0)


def with_other(grid, own):
    return own, grid.core_swap(own)


def hidden_grad_slots(grid, pairs, mid):
    return jnp.concatenate([core_sum(grid, *pair, mid) for pair in pairs], axis=2)


def col_sum(slots):
    return lax.psum_scatter(slots, "col", scatter_dimension=0)


def hidden_grad_blocks(grid, moved, count):
    rows, wide = moved.shape[1], moved.shape[2] // count
    return [
        moved[:, :, n * wide : (n + 1) * wide].transpose(1, 0, 2).reshape(rows, -1).astype(F32) for n in range(count)
    ]


def cross_columns(grid, blocks):
    _, count, rows, width = blocks.shape
    return blocks.transpose(1, 2, 0, 3).reshape(count * rows, grid.C * width)


def cross_weights(grid, pieces, count):
    half = jnp.stack(grid.natural(pieces))
    width = half.shape[2]
    half = half.reshape(grid.T, count, -1, width).transpose(1, 0, 2, 3).reshape(count, -1, width)
    other = grid.core_swap(half)
    return [joined([half[n], other[n]]) for n in range(count)]


def cross_core_sum(grid, lows, mid):
    edge = lows[0].shape[0] // 2
    return [core_sum(grid, low[:edge], low[edge:], mid) for low in lows]


def cross_terms(grid, halves, rows, width):
    halves = [half.reshape(grid.T, rows, grid.C * width) for half in halves]

    def term(d):
        return joined([lax.dynamic_index_in_dim(half, grid.i ^ d, 0, keepdims=False) for half in halves])

    order = grid.order()
    top = term(order[-1])
    size = top.shape[0] // 2
    return [top[:size], top[size:]], [term(d).astype(F32) for d in order[:-1]]


def cross_blocks(grid, own, rows, width):
    return own.astype(BF).reshape(-1, rows, grid.C, width).transpose(2, 0, 1, 3)


def text_columns(grid, text):
    _, own, width = text.shape
    parts = text.reshape(own, grid.R, width // grid.R).transpose(1, 0, 2)
    parts = grid.row_a2a(parts)
    pieces = [parts] + [
        lax.ppermute(parts, "col", [(c, c ^ d) for c in range(grid.C)]) for d in range(1, grid.C)
    ]
    stacked = jnp.stack(pieces)
    order = [lax.dynamic_index_in_dim(stacked, grid.z ^ c, 0, keepdims=False) for c in range(grid.C)]
    return jnp.stack(order, axis=1).reshape(-1, width // grid.R)


def text_parts(grid, columns, mats):
    count, rows, width = mats.shape
    own = columns.shape[0] // (grid.R * grid.C)
    part = product(columns, mats.transpose(1, 0, 2).reshape(rows, count * width)).astype(BF)
    part = part.reshape(grid.T, 2, grid.C, own, count * width).transpose(2, 1, 0, 3, 4)
    return grid.row_a2a(part.reshape(grid.R, grid.T * own, count * width))


def text_shared(grid, moved):
    own = moved.shape[1] // grid.T
    summed = jnp.sum(moved.astype(F32), axis=0).astype(BF).reshape(grid.T, own, moved.shape[2])
    sent = grid.picked(list(summed), [grid.z ^ e for e in range(grid.C)])
    return [grid.col_swap(sent[e], e) for e in range(grid.C)]


def text_states_of(grid, got, count):
    own, width = got[0].shape[0], got[0].shape[1] // count
    blocks = jnp.stack(grid.picked(got, [grid.z ^ c for c in range(grid.C)]))
    mine = blocks.reshape(grid.C, own, count, width).transpose(1, 2, 0, 3)
    mine = mine.reshape(own, count * grid.C * width)
    full = joined(flat(grid.gather(mine)))
    return full.reshape(-1, count, grid.C * width)


def text_begin(grid, grads):
    own = grads.shape[0] // grid.T
    pieces = grads.reshape(grid.T, own, -1)
    top = pieces[grid.T - 1].astype(BF)
    return grid.scatter_begin([top[: own // 2], top[own // 2 :]]), [pieces[n] for n in range(grid.T - 1)]


def text_backward(grid, mine, width):
    own = mine.shape[0]
    mine = mine.reshape(own, -1, grid.C, width).transpose(2, 0, 1, 3)
    moved = grid.col_a2a(mine)
    other = grid.core_swap(moved)
    pair = jnp.stack(
        [jnp.where(grid.core == 0, moved, other), jnp.where(grid.core == 0, other, moved)], axis=1
    )
    shape = pair.shape
    flat = pair.reshape(shape[0] * 2, -1)
    full = jnp.stack(grid.natural(grid.gather(flat)), axis=1)
    return full.reshape(-1, shape[3], width)


def text_out(grid, part):
    own = part.shape[0] // (grid.R * grid.C)
    cols = part.shape[1]
    parts = part.astype(BF).reshape(grid.R, grid.C, own, cols).transpose(1, 0, 2, 3)
    moved = grid.col_a2a(parts).astype(F32)
    summed = jnp.sum(moved, axis=0).astype(BF)
    moved = grid.row_a2a(summed)
    return moved.transpose(1, 0, 2).reshape(1, own, grid.R * cols).astype(F32)


def shards(
    grid,
    inputs,
    text_states,
    cotangent,
    norm_gains,
    norm_shifts,
    self_query,
    self_key,
    self_value,
    self_out,
    cross_query,
    cross_key,
    cross_value,
    cross_out,
    mlp_up,
    mlp_down,
):
    grid.at()
    last = LAYERS - 1
    rows, width = self_query.shape[1:]
    units, _ = head_units(grid, width)

    self_parts = [self_slots(grid, [w[n] for w in (self_query, self_key, self_value, self_out)]) for n in range(LAYERS)]
    hidden_parts = [hidden_slots(grid, [mlp_up[n], mlp_down[n]]) for n in range(LAYERS)]
    self_moved = [None] * LAYERS
    hidden_moved = [None] * LAYERS
    self_full = [None] * LAYERS
    self_moved[0] = grid.plane_a2a(self_parts[0])
    sent = by_matrix(self_moved[0])
    cross_parts = [jnp.stack([cross_query[n], cross_out[n]]) for n in range(LAYERS)]
    tokens = grid.tokens_in(jnp.concatenate([inputs, cotangent.astype(BF)], axis=1))
    tokens, sent = meet(tokens, sent)
    text_cols = text_columns(grid, after(text_states, tokens))
    gradient = tokens[:, inputs.shape[1] :]
    tokens = tokens[:, : inputs.shape[1]]
    self_full[0] = lax.all_gather(sent, "col", axis=0)
    residual = own_first(grid, tokens).astype(F32)
    norm_rows = after(jnp.concatenate([norm_gains, norm_shifts], axis=1), tokens)
    norm_rows = own_first(grid, norm_rows.reshape(-1, norm_rows.shape[2])).reshape(norm_rows.shape)
    gains, shifts = norm_rows[:, :3], norm_rows[:, 3:]
    text_mats = jnp.stack([mat for n in range(LAYERS) for mat in (cross_key[n], cross_value[n])])

    kept = [dict() for _ in range(LAYERS)]
    w_self = [None] * LAYERS
    w_cross = [None] * LAYERS
    w_hidden = [None] * LAYERS
    for n in range(LAYERS):
        k = kept[n]
        k["normed_one"], k["inv_one"], low_one = norm_forward(residual, gains[n, 0], shifts[n, 0])
        near_one = grid.gather_begin(low_one)
        if n == 0:
            hidden_moved[0] = grid.plane_a2a(after(hidden_parts[0], near_one))
            text_moved = text_parts(grid, after(text_cols, near_one), text_mats)
        full_one = flat(grid.gather_end(near_one))
        if n == 0:
            (self_full[0], full_one), (text_sent, hidden_moved[0]) = meet(
                (self_full[0], full_one), (text_shared(grid, text_moved), hidden_moved[0])
            )
            cross_full = lax.all_gather(after(cross_parts[0], sent), "col", axis=0)
        else:
            self_full[n] = after(self_full[n], residual)
        k["full_one"] = full_one
        w_self[n] = self_weights(grid, self_full[n], units)
        k["qkv"] = columns_product(full_one, w_self[n], (0, 1, 2))
        k["attn_low"], k["sums_self"] = self_attention(grid, k["qkv"])
        if n > 0:
            next_near = grid.gather_begin(cross_columns(grid, after(cross_full, full_one)))
            k["attn_low"], next_near = meet(k["attn_low"], next_near)
            w_cross[n] = cross_weights(grid, grid.gather_end(next_near), 2)
        up_full = hidden_gathered(hidden_moved[n], 0, full_one)
        down_full = hidden_gathered(hidden_moved[n], 1, k["qkv"])
        top, rest = rows_terms(grid, k["attn_low"], w_self[n], (3,))
        fill = []
        if n == 0:
            next_near = grid.gather_begin(cross_columns(grid, after(cross_full, k["qkv"])))
            rest, next_near = meet(rest, next_near)
            w_cross[0] = cross_weights(grid, grid.gather_end(next_near), 2)
        if n == 0:
            text_all = text_states_of(grid, tied(text_sent, top), 2 * LAYERS)
        added, _ = grid.scatter(top, rest)
        residual = residual + added
        w_up = with_other(grid, after(up_full, residual))
        before_cross = residual
        k["text"] = [text_all[:, 2 * n + side] for side in range(2)]
        k["normed_two"], k["inv_two"], k["low_two"] = norm_forward(residual, gains[n, 1], shifts[n, 1])
        k["cross_queries"] = product(k["low_two"], w_cross[n][0]).astype(BF)
        k["cross_low"] = cross_attention(k["cross_queries"], *k["text"])
        residual = residual + product_nt(k["cross_low"], w_cross[n][1])
        k["normed_three"], k["inv_three"], low_three = norm_forward(residual, gains[n, 2], shifts[n, 2])
        if n < last:
            sent = by_matrix(grid.plane_a2a(after(self_parts[n + 1], before_cross)))
            low_three, sent = meet(low_three, sent)
            self_full[n + 1] = lax.all_gather(sent, "col", axis=0)
            cross_full = lax.all_gather(after(cross_parts[n + 1], sent), "col", axis=0)
        if n == last:
            low_three, next_near = meet(low_three, grid.gather_begin(after(gradient, before_cross)))
        k["full_three"] = flat(grid.gather(low_three))
        if n < last:
            hidden_moved[n + 1] = grid.plane_a2a(after(hidden_parts[n + 1], low_three))
            k["full_three"], hidden_moved[n + 1] = meet(k["full_three"], hidden_moved[n + 1])
        k["hidden_low"], k["hidden_slope"] = columns_product(k["full_three"], w_up, (0,), "gelu")
        w_hidden[n] = (w_up, with_other(grid, after(down_full, k["hidden_low"])))
        if n < last:
            top, rest = rows_terms(grid, k["hidden_low"], w_hidden[n][1], (0,))
            gradient = own_first(grid, after(gradient, rest)) if n == 0 else gradient
            added, gradient = grid.scatter(top, rest, gradient)
            residual = residual + added
        else:
            dy_three = flat(grid.gather_end(next_near))
            gradient = gradient.astype(F32)

    before_last = residual
    hidden_sums = [None] * LAYERS
    self_sums = [None] * LAYERS
    cross_sums = [None] * LAYERS
    text_grads = [None] * LAYERS
    norms = [None] * LAYERS
    fill = []
    for n in range(last, -1, -1):
        k = kept[n]
        w_up, w_down = w_hidden[n]
        if n < last:
            sent, slots = meet(gradient.astype(BF), self_slots_grad)
            self_sums[n + 1] = col_sum(slots)
            dy_three, hidden_sums[n + 1] = meet(flat(grid.gather(sent)), hidden_sums[n + 1])
        if n == last:
            late_top, late_rest = rows_terms(grid, k["hidden_low"], w_down, (0,))
            late_state = grid.scatter_begin(late_top)
            dy_three, late_rest = meet(dy_three, late_rest)
        d_pre = columns_product(dy_three, w_down, (0,), "slope", k["hidden_slope"])
        top, rest = rows_terms(grid, d_pre, w_up, (0,))
        state = grid.scatter_begin(top)
        if n < last:
            own, _ = grid.scatter_end(tied(cross_state, dy_three), cross_last)
            own = cross_blocks(grid, own, rows, width)
            (state, rest), own = meet((state, rest), own)
            cross_late = own
        hidden_pairs = [
            weight_grads(after(k["full_three"], state), d_pre),
            weight_grads(after(dy_three, state), k["hidden_low"]),
        ]
        if n == last:
            late_state = tied(late_state, rest)
        grad_normed, hidden_pairs = grid.scatter_end(state, rest, hidden_pairs)
        grad_res, gain_three, shift_three = norm_backward(grad_normed, k["normed_three"], k["inv_three"], gains[n, 2])
        gradient = gradient + grad_res
        before_cross = gradient
        if n == last:
            late_sum, _ = grid.scatter_end(tied(late_state, gradient), late_rest)
        dy_two = gradient.astype(BF)
        d_cross = product(dy_two, w_cross[n][1]).astype(BF)
        d_cquery, d_ckey, d_cvalue = cross_attention_grad(k["cross_queries"], *k["text"], d_cross)
        grad_normed = product_nt(d_cquery, w_cross[n][0])
        text_grads[n] = jnp.concatenate([d_ckey, d_cvalue], axis=1)
        grad_res, gain_two, shift_two = norm_backward(grad_normed, k["normed_two"], k["inv_two"], gains[n, 1])
        gradient = gradient + grad_res
        sent = gradient.astype(BF)
        cross_lows = [
            product_tn(after(k["low_two"], sent), d_cquery).astype(BF),
            product_tn(after(dy_two, sent), k["cross_low"]).astype(BF),
        ]
        cross_halves = cross_core_sum(grid, cross_lows, sent)
        cross_top, cross_rest = cross_terms(grid, cross_halves, rows, width)
        fill = [cross_top]
        if n == last:
            sent, late_sum = meet(sent, late_sum)
            output = own_last(grid, (before_last + late_sum).astype(BF))
            fill += [output, hidden_grad_slots(grid, hidden_pairs, sent)]
        else:
            sent, hidden_slots_grad = meet(sent, hidden_grad_slots(grid, hidden_pairs, grad_normed))
            hidden_sums[n] = col_sum(hidden_slots_grad)
            cross_sums[n + 1] = col_sum(after(cross_late, hidden_slots_grad))
            fill.append(self_sums[n + 1])
        dy_one, fill = meet(flat(grid.gather(sent)), fill)
        cross_top = fill[0]
        if n == last:
            output = grid.tokens_out_begin(fill[1])
            hidden_sums[n] = col_sum(fill[2])
        else:
            self_sums[n + 1] = fill[1]
        d_attn = columns_product(dy_one, w_self[n], (3,))
        d_qkv = self_attention_grad(grid, k["qkv"], d_attn, k["sums_self"])
        cross_state, cross_last = grid.scatter_begin(after(cross_top, dy_one)), cross_rest
        if n == 0:
            text_state, text_rest = text_begin(grid, after(jnp.concatenate(text_grads, axis=1), dy_one))
            d_qkv, text_state = meet(d_qkv, text_state)
        if n == last:
            d_qkv, output = meet(d_qkv, output)
            output = grid.tokens_out_end(output)
        d_qkv, cross_state = meet(d_qkv, cross_state)
        if n > 0:
            top, rest = rows_terms(grid, d_qkv, w_self[n], (0, 1, 2))
            state = grid.scatter_begin(top)
            qkv_pair = weight_grads(after(k["full_one"], state), d_qkv)
            out_pair = weight_grads(after(dy_one, state), k["attn_low"])
            fill = [qkv_pair, out_pair, output]
        else:
            qkv_pair = weight_grads(k["full_one"], d_qkv)
            out_pair = weight_grads(dy_one, after(k["attn_low"], d_qkv))
            text_mine = grid.scatter_end(text_state, text_rest)[0].astype(BF)
            out_pair, text_mine = meet(out_pair, text_mine)
            top = rows_top(grid, after(d_qkv, [qkv_pair, out_pair]), w_self[n], (0, 1, 2))
            state = grid.scatter_begin(top)
            top, slots = meet(top, self_grad_slots(grid, [qkv_pair, out_pair], out_pair))
            self_sums[0] = col_sum(slots)
            rest = rows_rest(grid, after(d_qkv, top), w_self[n], (0, 1, 2))
            own, _ = grid.scatter_end(tied(cross_state, rest), cross_last)
            cross_sums[n] = col_sum(after(cross_blocks(grid, own, rows, width), self_sums[0]))
            fill = []
        grad_normed, fill = grid.scatter_end(state, rest, fill)
        if n > 0:
            qkv_pair, out_pair, output = fill
            self_slots_grad = self_grad_slots(grid, [qkv_pair, out_pair], grad_normed)
        grad_res, gain_one, shift_one = norm_backward(grad_normed, k["normed_one"], k["inv_one"], gains[n, 0])
        gradient = gradient + grad_res
        norms[n] = jnp.stack([gain_one, gain_two, gain_three, shift_one, shift_two, shift_three])

    cross_out_grads = [value.astype(F32) for value in cross_sums]
    input_grad = grid.tokens_out_begin(own_last(grid, gradient.astype(BF)))
    text_full = text_backward(grid, after(text_mine, rest), width)
    text_weights = [[product_tn(text_cols, text_full[:, 2 * n + side]) for side in range(2)] for n in range(LAYERS)]
    text_part = 0.0
    for n in range(LAYERS):
        for side, mats in enumerate((cross_key, cross_value)):
            text_part = text_part + product_nt(text_full[:, 2 * n + side], mats[n])
    text_grad = text_out(grid, text_part)
    early = [hidden_sums[n] for n in range(1, LAYERS)] + [self_sums[n] for n in range(1, LAYERS)]
    widths = [value.shape[1] for value in early]
    moved = jnp.concatenate([value.reshape(grid.T, rows, value.shape[1]) for value in early], axis=2)
    moved = grid.plane_a2a(after(moved, grad_normed))
    input_grad, moved = meet(input_grad, moved)
    input_grad = grid.tokens_out_end(input_grad).astype(F32)
    parts = [moved[:, :, sum(widths[:m]) : sum(widths[: m + 1])] for m in range(len(early))]
    first = [grid.plane_a2a(value[0].reshape(grid.T, rows, value[0].shape[1])) for value in (hidden_sums, self_sums)]
    hidden_out = [hidden_grad_blocks(grid, part, 2) for part in [first[0]] + parts[: LAYERS - 1]]
    self_out_grads = [self_grad_blocks(grid, part, units) for part in [first[1]] + parts[LAYERS - 1 :]]
    totals = grid.total(own_last(grid, jnp.concatenate(norms, axis=0))).reshape(LAYERS, 6, -1)
    gains_sum, shifts_sum = totals[:, :3], totals[:, 3:]

    def both(values, slot):
        return jnp.stack([values[n][slot] for n in range(LAYERS)])

    return (
        output.astype(F32),
        input_grad,
        text_grad,
        gains_sum,
        shifts_sum[:, 1:],
        shifts_sum[:, 0],
        both(self_out_grads, 0),
        both(self_out_grads, 1),
        both(self_out_grads, 2),
        both(self_out_grads, 3),
        both(cross_out_grads, 0),
        both(text_weights, 0),
        both(text_weights, 1),
        both(cross_out_grads, 1),
        both(hidden_out, 0),
        both(hidden_out, 1),
    )


def solution(mesh):
    grid = Grid(mesh)
    tokens = P(("row", "col"), None)
    text = P("row", "col", None)
    block = P(None, "row", "col")
    in_specs = (tokens, text, tokens, P(), P()) + (block,) * 10
    out_specs = (tokens, tokens, text, P(), P(), P()) + (block,) * 10

    def run(*args):
        return shards(grid, *args)

    return jax.shard_map(run, mesh=mesh, in_specs=in_specs, out_specs=out_specs, check_vma=False)
```

time: 1540 us -> 1370 us (0.89)
  Pallas kernels: 83.2 us -> 312 us
  matrix products: 219 us -> 32.3 us
  local copies, waits for them, and re-layouts: 307 us -> 202 us
  waiting for transfers between devices: 522 us -> 420 us
  other arithmetic: 129 us -> 154 us
  blocking collectives: 24.4 us -> 0 us
    pallas_call x4 -> x42, Pallas kernels: 59.4 us -> 288 us  [the longest x16 82.6 us: rows_product(): pl.pallas_call(functools.partial(rows_kernel, (0,) if len(mats) == 1 else...]
    dot_general x40 -> x8, matrix products: 93.1 us -> 18.2 us  [product_nt(): lax.dot_general(left, right, (((1,), (1,)), ((), ())), preferred_element_...]
    all_to_all x8 -> x2, waiting for transfers between devices: 62.7 us -> 4.83 us  [col_a2a(): return lax.all_to_all(value, 'col', 0, 0, tiled=True)]
    dot_general x13 -> x5, matrix products: 60.7 us -> 6.1 us  [product(): return jnp.dot(left, right, preferred_element_type=F32)]
    all_gather x6 -> x8, waiting for transfers between devices: 74.8 us -> 20.7 us  [the longest x1 19.5 us: shards(): self_full[n + 1] = lax.all_gather(sent, 'col', axis=0)]
    dot_general x6 -> x0, matrix products: 40.2 us -> none  [weight_product(): lax.dot_general(left, parts, (((0,), (0,)), ((), ())), preferred_element_...]
    slice x70 -> x67, local copies, waits for them, and re-layouts: 91.5 us -> 62.2 us  [the longest x24 16.7 us: part(): return pieces[d][0][half:] if upper else pieces[d][0][:half]]
    all_gather x6 -> x0, local copies, waits for them, and re-layouts: 25.7 us -> none  [the longest x2 13.4 us: hidden_weights(): token = lax.all_gather(moved, 'col', axis=0)]
  transfers between devices with their start and end apart: 164 -> 168, of which waited for: 64 -> 63; matrix products, arithmetic and copies ran while one was open for 40% -> 24% of each run, Pallas kernels for 5% -> 23%
where the time goes in v2:
time: 1370 us; the launch traced here: 1350 us
  waiting for transfers between devices  420 us (31%)
  Pallas kernels  312 us (23%)
  starting transfers between devices  214 us (16%)
  local copies, waits for them, and re-layouts  202 us (15%)
  other arithmetic  154 us (11%)
  matrix products  32.3 us (2%)
  between operations  19 us (1%)
    ppermute x101, waiting for transfers between devices, swap(): return lax.ppermute(value, 'row', [(r, r ^ 2 * d) for r in range(self.R)])  272 us
    ppermute x101, starting transfers between devices, swap(): return lax.ppermute(value, 'row', [(r, r ^ 2 * d) for r in range(self.R)])  110 us
    pallas_call x16, Pallas kernels, rows_product(): pl.pallas_call(functools.partial(rows_kernel, (0,) if len(mats) == 1 else...  82.6 us
    pallas_call x8, Pallas kernels, weight_grads(): pl.pallas_call(functools.partial(grads_kernel, len(pieces)), grid=(blocks...  68.8 us
    pallas_call x8, Pallas kernels, columns_product(): pl.pallas_call(functools.partial(columns_kernel, (0,) if len(mats) == 1 e...  64.7 us
    unnamed x598, local copies, waits for them, and re-layouts  47.8 us
    pallas_call x2, Pallas kernels, self_attention_grad(): pl.pallas_call(functools.partial(self_backward_kernel, grid, width), grid...  34.4 us
    all_to_all x7, waiting for transfers between devices, plane_a2a(): lax.all_to_all(value, 'row', 0, 0, tiled=True, axis_index_groups=self.gro...  31.6 us
  transfers between devices with their start and end apart: 168, of which 63 were waited for; matrix products, arithmetic and copies ran while one was open for 24% of the time, Pallas kernels for 23%

profile of v2, /device:TPU:0, one launch (start us, length us, event | category | flops | bytes accessed | tf_op | source)
XLA Modules:
  0.0 1353.9 jit_solution(11312334882655802843)
XLA Ops:
  22.9 12.9 collective-permute-done.1
  42.4 8.3 collective-permute-done.3
  50.7 15.0 %collective-permute-done.4 = bf16[64,3072]{1,0:T(8,128)(2,1)S(1)} collective-permute-done((bf16[64,3072]{1,0:T(8,128)(2,1)}, bf16[64,3072]{1,0:T(8,128)(2,1)S(1)}, u32[]{:S(2)}, u32[]{:S(2)}) %collective-permute-start.4) | collective-permute-done | bytes 393248 | tf_op jit(solution)/shard_map/ppermute | solution.py:161
  85.3 6.8 all-to-all-done.1
  92.0 8.9 collective-permute-start.10
  172.1 6.8 columns_plain.4.x_ref
  186.0 12.6 self_attention.2
  229.4 8.5 collective-permute-done.23
  254.9 11.5 collective-permute-done.22
  273.7 11.0 all-to-all-done.4
  307.6 12.5 collective-permute-done.30.refs_1_
  340.9 11.3 columns_gelu.2
  365.3 8.4 rows.19
  380.9 13.7 %collective-permute-done.39 = bf16[256,1536]{1,0:T(8,128)(2,1)} collective-permute-done((bf16[256,1536]{1,0:T(8,128)(2,1)}, bf16[256,1536]{1,0:T(8,128)(2,1)}, u32[]{:S(2)}, u32[]{:S(2)}) %collective-permute-start.39) | collective-permute-done | bytes 786464 | tf_op jit(solution)/shard_map/ppermute | solution.py:73
  397.8 19.5 %all-gather.25.cloned.1.call-done = bf16[16,768,128]{2,1,0:T(8,128)(2,1)} async-done(((bf16[4,768,128]{2,1,0:T(8,128)(2,1)}), bf16[16,768,128]{2,1,0:T(8,128)(2,1)}) %all-gather.25.cloned.1.call-update) | async-done | bytes 3145744 | tf_op jit(solution)/shard_map/all_gather | solution.py:893
  424.7 16.3 %collective-permute-done.40.refs_1_ = bf16[256,1536]{1,0:T(8,128)(2,1)S(1)} collective-permute-done((bf16[256,1536]{1,0:T(8,128)(2,1)S(1)}, bf16[256,1536]{1,0:T(8,128)(2,1)S(1)}, u32[]{:S(2)}, u32[]{:S(2)}) %collective-permute-start.40) | collective-permute-done | bytes 786464 | tf_op jit(solution)/shard_map/ppermute | solution.py:73
  460.4 7.1 columns_plain.5.x_ref
  467.5 12.6 self_attention.3
  490.6 7.3 collective-permute-done.51
  526.8 10.9 collective-permute-done.50
  562.6 18.0 %collective-permute-done.58.refs_1_ = bf16[256,1536]{1,0:T(8,128)(2,1)S(1)} collective-permute-done((bf16[256,1536]{1,0:T(8,128)(2,1)S(1)}, bf16[256,1536]{1,0:T(8,128)(2,1)S(1)}, u32[]{:S(2)}, u32[]{:S(2)}) %collective-permute-start.58) | collective-permute-done | bytes 786464 | tf_op jit(solution)/shard_map/ppermute | solution.py:73
  582.4 8.7 collective-permute-done.60.refs_3_
  591.3 10.5 columns_gelu.3
  617.5 8.4 rows.23
  629.5 10.5 columns_slope.2.act_ref.refs_5_
  645.4 8.5 rows.25
  660.6 10.6 weight_grads.9
  672.7 10.6 weight_grads.8
  718.2 14.4 %collective-permute-done.72.refs_1_ = bf16[256,1536]{1,0:T(8,128)(2,1)S(1)} collective-permute-done((bf16[256,1536]{1,0:T(8,128)(2,1)S(1)}, bf16[256,1536]{1,0:T(8,128)(2,1)S(1)}, u32[]{:S(2)}, u32[]{:S(2)}) %collective-permute-start.72) | collective-permute-done | bytes 786464 | tf_op jit(solution)/shard_map/ppermute | solution.py:73
  737.5 14.2 %collective-permute-done.73.refs_2_ = bf16[256,1536]{1,0:T(8,128)(2,1)S(1)} collective-permute-done((bf16[256,1536]{1,0:T(8,128)(2,1)S(1)}, bf16[256,1536]{1,0:T(8,128)(2,1)S(1)}, u32[]{:S(2)}, u32[]{:S(2)}) %collective-permute-start.73) | collective-permute-done | bytes 786464 | tf_op jit(solution)/shard_map/ppermute | solution.py:73
  785.3 17.2 %self_attention_grad.2.act_ref.refs_5_ = bf16[3,1024,384]{2,1,0:T(8,128)(2,1)S(1)} custom-call(s32[2]{0:T(128)S(1)} %pad_add_fusion.at_ref, bf16[3,1024,384]{2,1,0:T(8,128)(2,1)S(1)} %copy-done.110, bf16[3,1024,128]{2,1,0:T(8,128)(2,1)S(1)} %columns_plain.6.da_ref, f32[3,8,1024]{2,1,0:T(8,128)S(1)} %copy-done.114), custom_call_target="tpu_custom_call" | custom-call | flops 9663676416 | bytes 6291456 | tf_op jit(solution)/shard_map/self_attention_grad/pallas_call | solution.py:353
  816.2 7.0 rows.27
  831.2 8.7 weight_grads.10
  851.1 17.2 %collective-permute-done.94.refs_1_ = bf16[256,1536]{1,0:T(8,128)(2,1)S(1)} collective-permute-done((bf16[256,1536]{1,0:T(8,128)(2,1)S(1)}, bf16[256,1536]{1,0:T(8,128)(2,1)S(1)}, u32[]{:S(2)}, u32[]{:S(2)}) %collective-permute-start.94) | collective-permute-done | bytes 786464 | tf_op jit(solution)/shard_map/ppermute | solution.py:73
  871.6 7.0 collective-permute-done.96.refs_3_
  892.3 10.0 columns_slope.3.act_ref.refs_5_
  909.5 8.4 rows.29
  931.5 10.2 weight_grads.13
  941.7 11.1 weight_grads.12
  1006.2 8.7 collective-permute-done.106.refs_1_
  1037.1 17.2 %self_attention_grad.3.act_ref.refs_5_ = bf16[3,1024,384]{2,1,0:T(8,128)(2,1)S(1)} custom-call(s32[2]{0:T(128)S(1)} %pad_add_fusion.at_ref, bf16[3,1024,384]{2,1,0:T(8,128)(2,1)S(1)} %copy-done.108, bf16[3,1024,128]{2,1,0:T(8,128)(2,1)S(1)} %columns_plain.7.da_ref, f32[3,8,1024]{2,1,0:T(8,128)S(1)} %copy-done.112), custom_call_target="tpu_custom_call" | custom-call | flops 9663676416 | bytes 6291456 | tf_op jit(solution)/shard_map/self_attention_grad/pallas_call | solution.py:353
  1062.0 8.6 weight_grads.14
  1082.0 6.9 rows.30
  1099.5 16.9 %all-to-all-start.7 = ((bf16[4,16,4,384]{3,2,1,0:T(4,128)(2,1)}), bf16[4,16,4,384]{3,2,1,0:T(4,128)(2,1)}, u32[]{:S(2)}, u32[]{:S(2)}) async-start(bf16[4,16,4,384]{3,2,1,0:T(4,128)(2,1)} %bitcast.496), calls=%async_computation.9 | async-start | bytes 393216 | tf_op jit(solution)/shard_map/all_to_all | solution.py:85
  1146.4 24.6 %collective-permute-done.131 = bf16[4,24576]{1,0:T(4,128)(2,1)S(1)} collective-permute-done((bf16[4,24576]{1,0:T(4,128)(2,1)S(1)}, bf16[4,24576]{1,0:T(4,128)(2,1)S(1)}, u32[]{:S(2)}, u32[]{:S(2)}) %collective-permute-start.131) | collective-permute-done | bytes 196640 | tf_op jit(solution)/shard_map/ppermute | solution.py:73
  1244.7 18.5 %collective-permute-done.135 = f32[12,1536]{1,0:T(8,128)S(1)} collective-permute-done((f32[12,1536]{1,0:T(8,128)S(1)}, f32[12,1536]{1,0:T(8,128)S(1)}, u32[]{:S(2)}, u32[]{:S(2)}) %collective-permute-start.135) | collective-permute-done | bytes 73760 | tf_op jit(solution)/shard_map/ppermute | solution.py:189
  1278.1 14.7 %collective-permute-done.137 = f32[12,1536]{1,0:T(8,128)S(1)} collective-permute-done((f32[12,1536]{1,0:T(8,128)S(1)}, f32[12,1536]{1,0:T(8,128)S(1)}, u32[]{:S(2)}, u32[]{:S(2)}) %collective-permute-start.137) | collective-permute-done | bytes 73760 | tf_op jit(solution)/shard_map/ppermute | solution.py:191
  1319.9 9.6 all-to-all-done.11
  (1312 shorter events, 776.0 us)
Async XLA Ops:
  22.9 141.5 %all-gather.17.cloned.1.call-start = ((), (), s32[]{:S(2)}) async-start(), calls=%async_computation.24 | async-start | bytes 3932160 | tf_op jit(solution)/shard_map/all_gather | solution.py:836
  78.2 36.0 %collective-permute-start.6 = (bf16[256,1536]{1,0:T(8,128)(2,1)S(1)}, bf16[256,1536]{1,0:T(8,128)(2,1)S(1)}, u32[]{:S(2)}, u32[]{:S(2)}) collective-permute-start(bf16[256,1536]{1,0:T(8,128)(2,1)S(1)} %fusion.27.refs_0_), channel_id=1, source_target_pairs={{0,8},{4,12},{8,0},{12,4},{16,24},{20,28},{24,16},{28,20},{1,9},{5... | collective-permute-start | bytes 2359304 | tf_op jit(solution)/shard_map/ppermute | solution.py:73
  78.9 35.3 %collective-permute-start.7 = (bf16[256,1536]{1,0:T(8,128)(2,1)S(1)}, bf16[256,1536]{1,0:T(8,128)(2,1)S(1)}, u32[]{:S(2)}, u32[]{:S(2)}) collective-permute-start(bf16[256,1536]{1,0:T(8,128)(2,1)S(1)} %fusion.27.refs_0_), channel_id=1, source_target_pairs={{0,16},{4,20},{8,24},{12,28},{16,0},{20,4},{24,8},{28,12},{1,17},{... | collective-permute-start | bytes 2359304 | tf_op jit(solution)/shard_map/ppermute | solution.py:73
  120.6 59.8 %all-gather.19.cloned.1.call-start = ((), (), s32[]{:S(2)}) async-start(), calls=%async_computation.25 | async-start | bytes 1474560 | tf_op jit(solution)/shard_map/all_gather | solution.py:859
  145.6 122.9 %all-gather.21.cloned.1.call-start = ((), (), s32[]{:S(2)}) async-start(), calls=%async_computation.26 | async-start | bytes 2949120 | tf_op jit(solution)/shard_map/all_gather | solution.py:677
  168.9 183.3 %all-gather.23.cloned.1.call-start = ((), (), s32[]{:S(2)}) async-start(), calls=%async_computation.27 | async-start | bytes 2949120 | tf_op jit(solution)/shard_map/all_gather | solution.py:677
  182.7 29.1 %collective-permute-start.17 = (bf16[384,1536]{1,0:T(8,128)(2,1)S(1)}, bf16[384,1536]{1,0:T(8,128)(2,1)}, u32[]{:S(2)}, u32[]{:S(2)}) collective-permute-start(bf16[384,1536]{1,0:T(8,128)(2,1)S(1)} %bitcast.455), channel_id=1, source_target_pairs={{0,8},{4,12},{8,0},{12,4},{16,24},{20,28},{24,16},{28,20},{1,9},{5... | collective-permute-start | bytes 3538952 | tf_op jit(solution)/shard_map/ppermute | solution.py:73
  184.6 29.0 %collective-permute-start.18 = (bf16[384,1536]{1,0:T(8,128)(2,1)S(1)}, bf16[384,1536]{1,0:T(8,128)(2,1)}, u32[]{:S(2)}, u32[]{:S(2)}) collective-permute-start(bf16[384,1536]{1,0:T(8,128)(2,1)S(1)} %bitcast.456), channel_id=1, source_target_pairs={{0,16},{4,20},{8,24},{12,28},{16,0},{20,4},{24,8},{28,12},{1,17},{... | collective-permute-start | bytes 3538952 | tf_op jit(solution)/shard_map/ppermute | solution.py:73
  201.3 43.9 %collective-permute-start.21 = (bf16[128,1536]{1,0:T(8,128)(2,1)S(1)}, bf16[128,1536]{1,0:T(8,128)(2,1)}, u32[]{:S(2)}, u32[]{:S(2)}) collective-permute-start(bf16[128,1536]{1,0:T(8,128)(2,1)S(1)} %get-tuple-element.332), channel_id=1, source_target_pairs={{0,16},{4,20},{8,24},{12,28},{16,0},{20,4},{24,8},{28,12},{1,17},{... | collective-permute-start | bytes 1179656 | tf_op jit(solution)/shard_map/ppermute | solution.py:73
  217.8 30.3 %collective-permute-start.19 = (bf16[128,1536]{1,0:T(8,128)(2,1)S(1)}, bf16[128,1536]{1,0:T(8,128)(2,1)S(1)}, u32[]{:S(2)}, u32[]{:S(2)}) collective-permute-start(bf16[128,1536]{1,0:T(8,128)(2,1)S(1)} %get-tuple-element.333), channel_id=1, source_target_pairs={{0,8},{4,12},{8,0},{12,4},{16,24},{20,28},{24,16},{28,20},{1,9},{5... | collective-permute-start | bytes 1179656 | tf_op jit(solution)/shard_map/ppermute | solution.py:73
  244.1 42.6 %collective-permute-start.25 = (bf16[2,768,1536]{2,1,0:T(8,128)(2,1)}, bf16[2,768,1536]{2,1,0:T(8,128)(2,1)}, u32[]{:S(2)}, u32[]{:S(2)}) collective-permute-start(bf16[2,768,1536]{2,1,0:T(8,128)(2,1)} %bitcast.53), channel_id=1, source_target_pairs={{0,4},{4,0},{8,12},{12,8},{16,20},{20,16},{24,28},{28,24},{1,5},{5... | collective-permute-start | bytes 14155784 | tf_op jit(solution)/shard_map/ppermute | solution.py:76
  268.6 72.3 %collective-permute-start.34 = (bf16[4,1,768,384]{3,2,1,0:T(8,128)(2,1)}, bf16[4,1,768,384]{3,2,1,0:T(8,128)(2,1)}, u32[]{:S(2)}, u32[]{:S(2)}) collective-permute-start(bf16[4,1,768,384]{3,2,1,0:T(8,128)(2,1)} %bitcast.417), channel_id=1, source_target_pairs={{0,4},{4,0},{8,12},{12,8},{16,20},{20,16},{24,28},{28,24},{1,5},{5... | collective-permute-start | bytes 7077896 | tf_op jit(solution)/shard_map/ppermute | solution.py:76
  303.1 31.1 %all-to-all-start.5 = ((bf16[4,2,192,384]{3,2,1,0:T(8,128)(2,1)}), bf16[4,2,192,384]{3,2,1,0:T(8,128)(2,1)}, u32[]{:S(2)}, u32[]{:S(2)}) async-start(bf16[4,2,192,384]{3,2,1,0:T(8,128)(2,1)} %copy.132), calls=%async_computation.5 | async-start | bytes 2359296 | tf_op jit(solution)/shard_map/all_to_all | solution.py:79
  307.6 109.7 %all-gather.25.cloned.1.call-start = ((), (), s32[]{:S(2)}) async-start(), calls=%async_computation.28 | async-start | bytes 3932160 | tf_op jit(solution)/shard_map/all_gather | solution.py:893
  352.2 96.2 %all-gather.27.cloned.1.call-start = ((), (), s32[]{:S(2)}) async-start(), calls=%async_computation.29 | async-start | bytes 1474560 | tf_op jit(solution)/shard_map/all_gather | solution.py:894
  378.4 166.2 %all-gather.29.cloned.1.call-start = ((), (), s32[]{:S(2)}) async-start(), calls=%async_computation.30 | async-start | bytes 2949120 | tf_op jit(solution)/shard_map/all_gather | solution.py:677
  419.4 41.0 %collective-permute-start.44 = (bf16[3,4,768,128]{3,2,1,0:T(8,128)(2,1)S(1)}, bf16[3,4,768,128]{3,2,1,0:T(8,128)(2,1)}, u32[]{:S(2)}, u32[]{:S(2)}) collective-permute-start(bf16[3,4,768,128]{3,2,1,0:T(8,128)(2,1)S(1)} %pad_maximum_fusion.33.refs_5_.own_ref), channel_id=1, source_target_pairs={{0,4},{4,0},{8,12},{12,8},{16,20},{20,16},{24,28},{28,24},{1,5},{5... | collective-permute-start | bytes 7077896 | tf_op jit(solution)/shard_map/ppermute | solution.py:76
  490.3 112.9 %all-gather.31.cloned.1.call-start = ((), (), s32[]{:S(2)}) async-start(), calls=%async_computation.31 | async-start | bytes 2949120 | tf_op jit(solution)/shard_map/all_gather | solution.py:677
  505.1 39.6 %collective-permute-start.53 = (bf16[2,768,1536]{2,1,0:T(8,128)(2,1)}, bf16[2,768,1536]{2,1,0:T(8,128)(2,1)}, u32[]{:S(2)}, u32[]{:S(2)}) collective-permute-start(bf16[2,768,1536]{2,1,0:T(8,128)(2,1)} %bitcast.87), channel_id=1, source_target_pairs={{0,4},{4,0},{8,12},{12,8},{16,20},{20,16},{24,28},{28,24},{1,5},{5... | collective-permute-start | bytes 14155784 | tf_op jit(solution)/shard_map/ppermute | solution.py:76
  521.7 359.4 %reduce-scatter.7.cloned.1.call-start = ((), (), s32[]{:S(2)}) async-start(), calls=%async_computation.18 | async-start | bytes 5898240 | tf_op jit(solution)/shard_map/reduce_scatter | solution.py:689
  544.6 37.8 %collective-permute-start.62 = (bf16[4,1,768,384]{3,2,1,0:T(8,128)(2,1)}, bf16[4,1,768,384]{3,2,1,0:T(8,128)(2,1)S(1)}, u32[]{:S(2)}, u32[]{:S(2)}) collective-permute-start(bf16[4,1,768,384]{3,2,1,0:T(8,128)(2,1)} %bitcast.425), channel_id=1, source_target_pairs={{0,4},{4,0},{8,12},{12,8},{16,20},{20,16},{24,28},{28,24},{1,5},{5... | collective-permute-start | bytes 7077896 | tf_op jit(solution)/shard_map/ppermute | solution.py:76
  615.0 41.2 %collective-permute-start.68 = (bf16[128,1536]{1,0:T(8,128)(2,1)}, bf16[128,1536]{1,0:T(8,128)(2,1)S(1)}, u32[]{:S(2)}, u32[]{:S(2)}) collective-permute-start(bf16[128,1536]{1,0:T(8,128)(2,1)} %get-tuple-element.408), channel_id=1, source_target_pairs={{0,16},{4,20},{8,24},{12,28},{16,0},{20,4},{24,8},{28,12},{1,17},{... | collective-permute-start | bytes 1179656 | tf_op jit(solution)/shard_map/ppermute | solution.py:73
  616.8 39.4 %collective-permute-start.69 = (bf16[128,1536]{1,0:T(8,128)(2,1)}, bf16[128,1536]{1,0:T(8,128)(2,1)S(1)}, u32[]{:S(2)}, u32[]{:S(2)}) collective-permute-start(bf16[128,1536]{1,0:T(8,128)(2,1)} %get-tuple-element.409), channel_id=1, source_target_pairs={{0,8},{4,12},{8,0},{12,4},{16,24},{20,28},{24,16},{28,20},{1,9},{5... | collective-permute-start | bytes 1179656 | tf_op jit(solution)/shard_map/ppermute | solution.py:73
  706.2 47.7 %collective-permute-start.78 = (bf16[4,768,384]{2,1,0:T(8,128)(2,1)}, bf16[4,768,384]{2,1,0:T(8,128)(2,1)}, u32[]{:S(2)}, u32[]{:S(2)}) collective-permute-start(bf16[4,768,384]{2,1,0:T(8,128)(2,1)} %get-tuple-element.459), channel_id=1, source_target_pairs={{0,4},{4,0},{8,12},{12,8},{16,20},{20,16},{24,28},{28,24},{1,5},{5... | collective-permute-start | bytes 7077896 | tf_op jit(solution)/shard_map/ppermute | solution.py:76
  706.2 48.4 %collective-permute-start.79 = (bf16[4,768,384]{2,1,0:T(8,128)(2,1)}, bf16[4,768,384]{2,1,0:T(8,128)(2,1)}, u32[]{:S(2)}, u32[]{:S(2)}) collective-permute-start(bf16[4,768,384]{2,1,0:T(8,128)(2,1)} %get-tuple-element.462), channel_id=1, source_target_pairs={{0,4},{4,0},{8,12},{12,8},{16,20},{20,16},{24,28},{28,24},{1,5},{5... | collective-permute-start | bytes 7077896 | tf_op jit(solution)/shard_map/ppermute | solution.py:76
  711.1 43.6 %collective-permute-start.77 = (bf16[768,1536]{1,0:T(8,128)(2,1)}, bf16[768,1536]{1,0:T(8,128)(2,1)}, u32[]{:S(2)}, u32[]{:S(2)}) collective-permute-start(bf16[768,1536]{1,0:T(8,128)(2,1)} %slice.849), channel_id=1, source_target_pairs={{0,4},{4,0},{8,12},{12,8},{16,20},{20,16},{24,28},{28,24},{1,5},{5... | collective-permute-start | bytes 7077896 | tf_op jit(solution)/shard_map/ppermute | solution.py:76
  718.1 41.7 %collective-permute-start.76 = (bf16[768,1536]{1,0:T(8,128)(2,1)}, bf16[768,1536]{1,0:T(8,128)(2,1)}, u32[]{:S(2)}, u32[]{:S(2)}) collective-permute-start(bf16[768,1536]{1,0:T(8,128)(2,1)} %slice.847), channel_id=1, source_target_pairs={{0,4},{4,0},{8,12},{12,8},{16,20},{20,16},{24,28},{28,24},{1,5},{5... | collective-permute-start | bytes 7077896 | tf_op jit(solution)/shard_map/ppermute | solution.py:76
  773.5 251.8 %reduce-scatter.9.cloned.1.call-start = ((), (), s32[]{:S(2)}) async-start(), calls=%async_computation.19 | async-start | bytes 3932160 | tf_op jit(solution)/shard_map/reduce_scatter | solution.py:689
  883.6 35.4 %collective-permute-start.101 = (bf16[384,1536]{1,0:T(8,128)(2,1)}, bf16[384,1536]{1,0:T(8,128)(2,1)}, u32[]{:S(2)}, u32[]{:S(2)}) collective-permute-start(bf16[384,1536]{1,0:T(8,128)(2,1)} %pad_maximum_fusion.44), channel_id=1, source_target_pairs={{0,8},{4,12},{8,0},{12,4},{16,24},{20,28},{24,16},{28,20},{1,9},{5... | collective-permute-start | bytes 3538952 | tf_op jit(solution)/shard_map/ppermute | solution.py:73
  887.4 31.7 %collective-permute-start.100 = (bf16[384,1536]{1,0:T(8,128)(2,1)}, bf16[384,1536]{1,0:T(8,128)(2,1)}, u32[]{:S(2)}, u32[]{:S(2)}) collective-permute-start(bf16[384,1536]{1,0:T(8,128)(2,1)} %pad_maximum_fusion.43), channel_id=1, source_target_pairs={{0,16},{4,20},{8,24},{12,28},{16,0},{20,4},{24,8},{28,12},{1,17},{... | collective-permute-start | bytes 3538952 | tf_op jit(solution)/shard_map/ppermute | solution.py:73
  888.4 247.1 %reduce-scatter.15.cloned.1.call-start = ((), (), s32[]{:S(2)}) async-start(), calls=%async_computation.22 | async-start | bytes 1474560 | tf_op jit(solution)/shard_map/reduce_scatter | solution.py:689
  990.3 321.7 %reduce-scatter.17.cloned.1.call-start = ((), (), s32[]{:S(2)}) async-start(), calls=%async_computation.23 | async-start | bytes 5898240 | tf_op jit(solution)/shard_map/reduce_scatter | solution.py:689
  1027.0 35.0 %collective-permute-start.114 = (bf16[192,1536]{1,0:T(8,128)(2,1)}, bf16[192,1536]{1,0:T(8,128)(2,1)S(1)}, u32[]{:S(2)}, u32[]{:S(2)}) collective-permute-start(bf16[192,1536]{1,0:T(8,128)(2,1)} %get-tuple-element.578), channel_id=1, source_target_pairs={{0,16},{4,20},{8,24},{12,28},{16,0},{20,4},{24,8},{28,12},{1,17},{... | collective-permute-start | bytes 1769480 | tf_op jit(solution)/shard_map/ppermute | solution.py:73
  1028.0 33.9 %collective-permute-start.115 = (bf16[192,1536]{1,0:T(8,128)(2,1)}, bf16[192,1536]{1,0:T(8,128)(2,1)S(1)}, u32[]{:S(2)}, u32[]{:S(2)}) collective-permute-start(bf16[192,1536]{1,0:T(8,128)(2,1)} %get-tuple-element.579), channel_id=1, source_target_pairs={{0,8},{4,12},{8,0},{12,4},{16,24},{20,28},{24,16},{28,20},{1,9},{5... | collective-permute-start | bytes 1769480 | tf_op jit(solution)/shard_map/ppermute | solution.py:73
  1076.7 118.3 %collective-permute-start.138 = (bf16[3,768,384]{2,1,0:T(8,128)(2,1)}, bf16[3,768,384]{2,1,0:T(8,128)(2,1)}, u32[]{:S(2)}, u32[]{:S(2)}) collective-permute-start(bf16[3,768,384]{2,1,0:T(8,128)(2,1)} %get-tuple-element.584), channel_id=1, source_target_pairs={{0,4},{4,0},{8,12},{12,8},{16,20},{20,16},{24,28},{28,24},{1,5},{5... | collective-permute-start | bytes 5308424 | tf_op jit(solution)/shard_map/ppermute | solution.py:76
  1076.7 55.9 %collective-permute-start.139 = (bf16[3,768,128]{2,1,0:T(8,128)(2,1)}, bf16[3,768,128]{2,1,0:T(8,128)(2,1)}, u32[]{:S(2)}, u32[]{:S(2)}) collective-permute-start(bf16[3,768,128]{2,1,0:T(8,128)(2,1)} %get-tuple-element.593), channel_id=1, source_target_pairs={{0,4},{4,0},{8,12},{12,8},{16,20},{20,16},{24,28},{28,24},{1,5},{5... | collective-permute-start | bytes 1769480 | tf_op jit(solution)/shard_map/ppermute | solution.py:76
  1081.1 42.7 %collective-permute-start.120 = (bf16[128,1536]{1,0:T(8,128)(2,1)}, bf16[128,1536]{1,0:T(8,128)(2,1)}, u32[]{:S(2)}, u32[]{:S(2)}) collective-permute-start(bf16[128,1536]{1,0:T(8,128)(2,1)} %get-tuple-element.597), channel_id=1, source_target_pairs={{0,16},{4,20},{8,24},{12,28},{16,0},{20,4},{24,8},{28,12},{1,17},{... | collective-permute-start | bytes 1179656 | tf_op jit(solution)/shard_map/ppermute | solution.py:73
  1090.9 34.2 %collective-permute-start.118 = (bf16[128,1536]{1,0:T(8,128)(2,1)S(1)}, bf16[128,1536]{1,0:T(8,128)(2,1)}, u32[]{:S(2)}, u32[]{:S(2)}) collective-permute-start(bf16[128,1536]{1,0:T(8,128)(2,1)S(1)} %get-tuple-element.595), channel_id=1, source_target_pairs={{0,8},{4,12},{8,0},{12,4},{16,24},{20,28},{24,16},{28,20},{1,9},{5... | collective-permute-start | bytes 1179656 | tf_op jit(solution)/shard_map/ppermute | solution.py:73
  1095.2 80.3 %collective-permute-start.141 = (bf16[384,1536]{1,0:T(8,128)(2,1)}, bf16[384,1536]{1,0:T(8,128)(2,1)}, u32[]{:S(2)}, u32[]{:S(2)}) collective-permute-start(bf16[384,1536]{1,0:T(8,128)(2,1)} %pad_maximum_fusion.46), channel_id=1, source_target_pairs={{0,8},{4,12},{8,0},{12,4},{16,24},{20,28},{24,16},{28,20},{1,9},{5... | collective-permute-start | bytes 3538952 | tf_op jit(solution)/shard_map/ppermute | solution.py:73
  1116.3 200.7 %reduce-scatter.13.cloned.1.call-start = ((), (), s32[]{:S(2)}) async-start(), calls=%async_computation.21 | async-start | bytes 1474560 | tf_op jit(solution)/shard_map/reduce_scatter | solution.py:689
  1132.7 42.8 %collective-permute-start.140 = (bf16[384,1536]{1,0:T(8,128)(2,1)}, bf16[384,1536]{1,0:T(8,128)(2,1)}, u32[]{:S(2)}, u32[]{:S(2)}) collective-permute-start(bf16[384,1536]{1,0:T(8,128)(2,1)} %pad_maximum_fusion.45), channel_id=1, source_target_pairs={{0,16},{4,20},{8,24},{12,28},{16,0},{20,4},{24,8},{28,12},{1,17},{... | collective-permute-start | bytes 3538952 | tf_op jit(solution)/shard_map/ppermute | solution.py:73
  1142.5 28.5 %collective-permute-start.131 = (bf16[4,24576]{1,0:T(4,128)(2,1)S(1)}, bf16[4,24576]{1,0:T(4,128)(2,1)S(1)}, u32[]{:S(2)}, u32[]{:S(2)}) collective-permute-start(bf16[4,24576]{1,0:T(4,128)(2,1)S(1)} %slice.872), channel_id=1, source_target_pairs={{0,16},{4,20},{8,24},{12,28},{16,0},{20,4},{24,8},{28,12},{1,17},{... | collective-permute-start | bytes 589832 | tf_op jit(solution)/shard_map/ppermute | solution.py:73
  1144.1 28.5 %collective-permute-start.132 = (bf16[4,24576]{1,0:T(4,128)(2,1)S(1)}, bf16[4,24576]{1,0:T(4,128)(2,1)S(1)}, u32[]{:S(2)}, u32[]{:S(2)}) collective-permute-start(bf16[4,24576]{1,0:T(4,128)(2,1)S(1)} %slice.873), channel_id=1, source_target_pairs={{0,8},{4,12},{8,0},{12,4},{16,24},{20,28},{24,16},{28,20},{1,9},{5... | collective-permute-start | bytes 589832 | tf_op jit(solution)/shard_map/ppermute | solution.py:73
  1171.0 45.3 %collective-permute-start.121 = (bf16[256,1536]{1,0:T(8,128)(2,1)}, bf16[256,1536]{1,0:T(8,128)(2,1)}, u32[]{:S(2)}, u32[]{:S(2)}) collective-permute-start(bf16[256,1536]{1,0:T(8,128)(2,1)} %pad_maximum_fusion.67), channel_id=1, source_target_pairs={{0,8},{4,12},{8,0},{12,4},{16,24},{20,28},{24,16},{28,20},{1,9},{5... | collective-permute-start | bytes 2359304 | tf_op jit(solution)/shard_map/ppermute | solution.py:73
  1172.5 43.8 %collective-permute-start.119 = (bf16[256,1536]{1,0:T(8,128)(2,1)}, bf16[256,1536]{1,0:T(8,128)(2,1)}, u32[]{:S(2)}, u32[]{:S(2)}) collective-permute-start(bf16[256,1536]{1,0:T(8,128)(2,1)} %pad_maximum_fusion.66), channel_id=1, source_target_pairs={{0,16},{4,20},{8,24},{12,28},{16,0},{20,4},{24,8},{28,12},{1,17},{... | collective-permute-start | bytes 2359304 | tf_op jit(solution)/shard_map/ppermute | solution.py:73
  1182.8 137.1 %reduce-scatter.11.cloned.1.call-start = ((), (), s32[]{:S(2)}) async-start(), calls=%async_computation.20 | async-start | bytes 3932160 | tf_op jit(solution)/shard_map/reduce_scatter | solution.py:689
  1232.7 62.0 %all-to-all-start.6 = ((bf16[4,192,1280]{2,1,0:T(8,128)(2,1)}), bf16[4,192,1280]{2,1,0:T(8,128)(2,1)}, u32[]{:S(2)}, u32[]{:S(2)}) async-start(bf16[4,192,1280]{2,1,0:T(8,128)(2,1)} %pad_maximum_fusion.34), calls=%async_computation.8 | async-start | bytes 3932160 | tf_op jit(solution)/shard_map/all_to_all | solution.py:79
  1266.1 28.6 %collective-permute-start.122 = (bf16[64,1536]{1,0:T(8,128)(2,1)S(1)}, bf16[64,1536]{1,0:T(8,128)(2,1)S(1)}, u32[]{:S(2)}, u32[]{:S(2)}) collective-permute-start(bf16[64,1536]{1,0:T(8,128)(2,1)S(1)} %get-tuple-element.852), channel_id=1, source_target_pairs={{0,1},{1,0},{2,3},{3,2},{4,5},{5,4},{6,7},{7,6},{8,9},{9,8},{10,11... | collective-permute-start | bytes 589832 | tf_op jit(solution)/shard_map/ppermute | solution.py:161
  (415 other events, 3944.9 us)
Sparse Core Ops, SparseCore 0:
  67.8 71.4 all-gather.16
  141.4 33.4 all-gather.18
  177.0 49.3 all-gather.20
  228.3 49.2 all-gather.22
  352.3 64.9 all-gather.24
  419.3 29.0 all-gather.26
  490.4 49.5 all-gather.28
  542.2 49.2 all-gather.30
  773.6 92.2 reduce-scatter.6
  888.5 71.7 reduce-scatter.8
  990.4 41.0 reduce-scatter.14
  1033.7 85.2 reduce-scatter.16
  1182.9 28.3 reduce-scatter.12
  1213.5 64.5 reduce-scatter.10

commit v3 on v2

--- a/solution.py
+++ b/solution.py
@@ -867,7 +867,7 @@
             next_near = grid.gather_begin(cross_columns(grid, after(cross_full, full_one)))
             k["attn_low"], next_near = meet(k["attn_low"], next_near)
             w_cross[n] = cross_weights(grid, grid.gather_end(next_near), 2)
-        up_full = hidden_gathered(hidden_moved[n], 0, full_one)
+        up_full = hidden_gathered(hidden_moved[n], 0, full_one if n == 0 else hidden_moved[n])
         down_full = hidden_gathered(hidden_moved[n], 1, k["qkv"])
         top, rest = rows_terms(grid, k["attn_low"], w_self[n], (3,))
         fill = []
@@ -888,6 +888,8 @@
         residual = residual + product_nt(k["cross_low"], w_cross[n][1])
         k["normed_three"], k["inv_three"], low_three = norm_forward(residual, gains[n, 2], shifts[n, 2])
         if n < last:
+            w_down = with_other(grid, after(down_full, before_cross))
+            w_down, low_three = meet(w_down, low_three)
             sent = by_matrix(grid.plane_a2a(after(self_parts[n + 1], before_cross)))
             low_three, sent = meet(low_three, sent)
             self_full[n + 1] = lax.all_gather(sent, "col", axis=0)
@@ -899,7 +901,9 @@
             hidden_moved[n + 1] = grid.plane_a2a(after(hidden_parts[n + 1], low_three))
             k["full_three"], hidden_moved[n + 1] = meet(k["full_three"], hidden_moved[n + 1])
         k["hidden_low"], k["hidden_slope"] = columns_product(k["full_three"], w_up, (0,), "gelu")
-        w_hidden[n] = (w_up, with_other(grid, after(down_full, k["hidden_low"])))
+        if n == last:
+            w_down = with_other(grid, after(down_full, k["hidden_low"]))
+        w_hidden[n] = (w_up, w_down)
         if n < last:
             top, rest = rows_terms(grid, k["hidden_low"], w_hidden[n][1], (0,))
             gradient = own_first(grid, after(gradient, rest)) if n == 0 else gradient
@@ -922,7 +926,8 @@
         if n < last:
             sent, slots = meet(gradient.astype(BF), self_slots_grad)
             self_sums[n + 1] = col_sum(slots)
-            dy_three, hidden_sums[n + 1] = meet(flat(grid.gather(sent)), hidden_sums[n + 1])
+            cross_terms_late = cross_terms(grid, cross_core_sum(grid, cross_lows, sent), rows, width)
+            dy_three, cross_terms_late = meet(flat(grid.gather(sent)), cross_terms_late)
         if n == last:
             late_top, late_rest = rows_terms(grid, k["hidden_low"], w_down, (0,))
             late_state = grid.scatter_begin(late_top)
@@ -931,10 +936,7 @@
         top, rest = rows_terms(grid, d_pre, w_up, (0,))
         state = grid.scatter_begin(top)
         if n < last:
-            own, _ = grid.scatter_end(tied(cross_state, dy_three), cross_last)
-            own = cross_blocks(grid, own, rows, width)
-            (state, rest), own = meet((state, rest), own)
-            cross_late = own
+            (state, rest), cross_state = meet((state, rest), grid.scatter_begin(cross_terms_late[0]))
         hidden_pairs = [
             weight_grads(after(k["full_three"], state), d_pre),
             weight_grads(after(dy_three, state), k["hidden_low"]),
@@ -944,6 +946,8 @@
         grad_normed, hidden_pairs = grid.scatter_end(state, rest, hidden_pairs)
         grad_res, gain_three, shift_three = norm_backward(grad_normed, k["normed_three"], k["inv_three"], gains[n, 2])
         gradient = gradient + grad_res
+        if n < last:
+            gradient, hidden_sums[n + 1] = meet(gradient, hidden_sums[n + 1])
         before_cross = gradient
         if n == last:
             late_sum, _ = grid.scatter_end(tied(late_state, gradient), late_rest)
@@ -955,69 +959,69 @@
         grad_res, gain_two, shift_two = norm_backward(grad_normed, k["normed_two"], k["inv_two"], gains[n, 1])
         gradient = gradient + grad_res
         sent = gradient.astype(BF)
-        cross_lows = [
-            product_tn(after(k["low_two"], sent), d_cquery).astype(BF),
-            product_tn(after(dy_two, sent), k["cross_low"]).astype(BF),
-        ]
-        cross_halves = cross_core_sum(grid, cross_lows, sent)
-        cross_top, cross_rest = cross_terms(grid, cross_halves, rows, width)
-        fill = [cross_top]
         if n == last:
             sent, late_sum = meet(sent, late_sum)
-            output = own_last(grid, (before_last + late_sum).astype(BF))
-            fill += [output, hidden_grad_slots(grid, hidden_pairs, sent)]
+            fill = own_last(grid, (before_last + late_sum).astype(BF))
         else:
             sent, hidden_slots_grad = meet(sent, hidden_grad_slots(grid, hidden_pairs, grad_normed))
             hidden_sums[n] = col_sum(hidden_slots_grad)
-            cross_sums[n + 1] = col_sum(after(cross_late, hidden_slots_grad))
-            fill.append(self_sums[n + 1])
+            fill = ()
         dy_one, fill = meet(flat(grid.gather(sent)), fill)
-        cross_top = fill[0]
         if n == last:
-            output = grid.tokens_out_begin(fill[1])
-            hidden_sums[n] = col_sum(fill[2])
-        else:
-            self_sums[n + 1] = fill[1]
+            output = grid.tokens_out_begin(fill)
         d_attn = columns_product(dy_one, w_self[n], (3,))
         d_qkv = self_attention_grad(grid, k["qkv"], d_attn, k["sums_self"])
-        cross_state, cross_last = grid.scatter_begin(after(cross_top, dy_one)), cross_rest
         if n == 0:
             text_state, text_rest = text_begin(grid, after(jnp.concatenate(text_grads, axis=1), dy_one))
-            d_qkv, text_state = meet(d_qkv, text_state)
+            d_qkv, (text_state, self_sums[1:]) = meet(d_qkv, (text_state, self_sums[1:]))
         if n == last:
             d_qkv, output = meet(d_qkv, output)
             output = grid.tokens_out_end(output)
-        d_qkv, cross_state = meet(d_qkv, cross_state)
+
+        def cross_products(token):
+            return [
+                product_tn(after(k["low_two"], token), d_cquery).astype(BF),
+                product_tn(after(dy_two, token), k["cross_low"]).astype(BF),
+            ]
+
         if n > 0:
             top, rest = rows_terms(grid, d_qkv, w_self[n], (0, 1, 2))
             state = grid.scatter_begin(top)
             qkv_pair = weight_grads(after(k["full_one"], state), d_qkv)
             out_pair = weight_grads(after(dy_one, state), k["attn_low"])
-            fill = [qkv_pair, out_pair, output]
+            fill = [qkv_pair, out_pair, output, hidden_grad_slots(grid, hidden_pairs, state), cross_products(state)]
         else:
             qkv_pair = weight_grads(k["full_one"], d_qkv)
             out_pair = weight_grads(dy_one, after(k["attn_low"], d_qkv))
             text_mine = grid.scatter_end(text_state, text_rest)[0].astype(BF)
-            out_pair, text_mine = meet(out_pair, text_mine)
+            own, _ = grid.scatter_end(tied(cross_state, dy_one), cross_terms_late[1])
+            out_pair, (text_mine, own) = meet(out_pair, (text_mine, cross_blocks(grid, own, rows, width)))
+            cross_sums[n + 1] = own
             top = rows_top(grid, after(d_qkv, [qkv_pair, out_pair]), w_self[n], (0, 1, 2))
             state = grid.scatter_begin(top)
             top, slots = meet(top, self_grad_slots(grid, [qkv_pair, out_pair], out_pair))
             self_sums[0] = col_sum(slots)
-            rest = rows_rest(grid, after(d_qkv, top), w_self[n], (0, 1, 2))
-            own, _ = grid.scatter_end(tied(cross_state, rest), cross_last)
-            cross_sums[n] = col_sum(after(cross_blocks(grid, own, rows, width), self_sums[0]))
-            fill = []
+            rest = rows_rest(grid, after(d_qkv, slots), w_self[n], (0, 1, 2))
+            fill = cross_terms(grid, cross_core_sum(grid, cross_products(state), state), rows, width)
         grad_normed, fill = grid.scatter_end(state, rest, fill)
+        if n == 0:
+            cross_state, cross_last = grid.scatter_begin(fill[0]), fill[1]
         if n > 0:
-            qkv_pair, out_pair, output = fill
+            qkv_pair, out_pair, output, hidden_slots_grad, cross_lows = fill
+            hidden_sums[n] = col_sum(hidden_slots_grad)
             self_slots_grad = self_grad_slots(grid, [qkv_pair, out_pair], grad_normed)
         grad_res, gain_one, shift_one = norm_backward(grad_normed, k["normed_one"], k["inv_one"], gains[n, 0])
         gradient = gradient + grad_res
         norms[n] = jnp.stack([gain_one, gain_two, gain_three, shift_one, shift_two, shift_three])
 
-    cross_out_grads = [value.astype(F32) for value in cross_sums]
-    input_grad = grid.tokens_out_begin(own_last(grid, gradient.astype(BF)))
-    text_full = text_backward(grid, after(text_mine, rest), width)
+    gradient, cross_state = meet(gradient.astype(BF), cross_state)
+    input_grad = grid.tokens_out_begin(own_last(grid, gradient))
+    text_full = text_backward(grid, after(text_mine, grad_normed), width)
+    own, _ = grid.scatter_end(cross_state, cross_last)
+    text_full, cross_sums[0] = meet(text_full, cross_blocks(grid, own, rows, width))
+    cross_all, self_sums[0] = meet(jnp.concatenate(cross_sums, axis=1), self_sums[0])
+    cross_all = col_sum(cross_all).astype(F32)
+    cross_out_grads = [cross_all[2 * n : 2 * n + 2] for n in range(LAYERS)]
     text_weights = [[product_tn(text_cols, text_full[:, 2 * n + side]) for side in range(2)] for n in range(LAYERS)]
     text_part = 0.0
     for n in range(LAYERS):
@@ -1028,7 +1032,7 @@
     widths = [value.shape[1] for value in early]
     moved = jnp.concatenate([value.reshape(grid.T, rows, value.shape[1]) for value in early], axis=2)
     moved = grid.plane_a2a(after(moved, grad_normed))
-    input_grad, moved = meet(input_grad, moved)
+    input_grad, (moved, hidden_sums[0]) = meet(input_grad, (moved, hidden_sums[0]))
     input_grad = grid.tokens_out_end(input_grad).astype(F32)
     parts = [moved[:, :, sum(widths[:m]) : sum(widths[: m + 1])] for m in range(len(early))]
     first = [grid.plane_a2a(value[0].reshape(grid.T, rows, value[0].shape[1])) for value in (hidden_sums, self_sums)]

time: 1370 us -> 1320 us (0.964)
  waiting for transfers between devices: 420 us -> 374 us
    ppermute x2, waiting for transfers between devices: 21.2 us -> 1.32 us  [total(): lax.ppermute(value, 'col', [(c, c ^ 1 << d) for c in range(self.C)])]
    all_gather x1, waiting for transfers between devices: 19.5 us -> 0.02 us  [shards(): self_full[n + 1] = lax.all_gather(sent, 'col', axis=0)]
    all_to_all x2, starting transfers between devices: 20.9 us -> 6.77 us  [col_a2a(): return lax.all_to_all(value, 'col', 0, 0, tiled=True)]
    unnamed x598 -> x594, local copies, waits for them, and re-layouts: 47.8 us -> 55.7 us
  transfers between devices with their start and end apart: 168 -> 167, of which waited for: 63 -> 65; matrix products, arithmetic and copies ran while one was open for 24% -> 25% of each run, Pallas kernels for 23% -> 24%
where the time goes in v3:
time: 1320 us; the launch traced here: 1300 us
  waiting for transfers between devices  374 us (28%)
  Pallas kernels  311 us (24%)
  starting transfers between devices  205 us (16%)
  local copies, waits for them, and re-layouts  201 us (15%)
  other arithmetic  161 us (12%)
  matrix products  33.7 us (3%)
  between operations  18.7 us (1%)
    ppermute x101, waiting for transfers between devices, swap(): return lax.ppermute(value, 'row', [(r, r ^ 2 * d) for r in range(self.R)])  280 us
    ppermute x101, starting transfers between devices, swap(): return lax.ppermute(value, 'row', [(r, r ^ 2 * d) for r in range(self.R)])  110 us
    pallas_call x16, Pallas kernels, rows_product(): pl.pallas_call(functools.partial(rows_kernel, (0,) if len(mats) == 1 else...  80 us
    pallas_call x8, Pallas kernels, weight_grads(): pl.pallas_call(functools.partial(grads_kernel, len(pieces)), grid=(blocks...  69.5 us
    pallas_call x8, Pallas kernels, columns_product(): pl.pallas_call(functools.partial(columns_kernel, (0,) if len(mats) == 1 e...  65.3 us
    unnamed x594, local copies, waits for them, and re-layouts  55.7 us
    all_to_all x7, waiting for transfers between devices, plane_a2a(): lax.all_to_all(value, 'row', 0, 0, tiled=True, axis_index_groups=self.gro...  37.2 us
    pallas_call x2, Pallas kernels, self_attention_grad(): pl.pallas_call(functools.partial(self_backward_kernel, grid, width), grid...  34.8 us
  transfers between devices with their start and end apart: 167, of which 65 were waited for; matrix products, arithmetic and copies ran while one was open for 25% of the time, Pallas kernels for 24%

profile of v3, /device:TPU:0, one launch (start us, length us, event | category | flops | bytes accessed | tf_op | source)
XLA Modules:
  0.0 1304.2 jit_solution(3081322836060192631)
XLA Ops:
  22.9 12.9 collective-permute-done.1
  42.4 8.3 collective-permute-done.3
  50.7 15.0 %collective-permute-done.4 = bf16[64,3072]{1,0:T(8,128)(2,1)S(1)} collective-permute-done((bf16[64,3072]{1,0:T(8,128)(2,1)}, bf16[64,3072]{1,0:T(8,128)(2,1)S(1)}, u32[]{:S(2)}, u32[]{:S(2)}) %collective-permute-start.4) | collective-permute-done | bytes 393248 | tf_op jit(solution)/shard_map/ppermute | solution.py:161
  85.3 6.8 all-to-all-done.1
  92.1 8.9 collective-permute-start.10
  148.1 6.7 collective-permute-start.13
  172.1 6.8 columns_plain.4.x_ref
  185.9 12.6 self_attention.2
  229.3 8.5 collective-permute-done.23
  254.6 11.5 collective-permute-done.22
  275.4 10.0 all-to-all-done.4
  337.6 7.1 collective-permute-done.33.refs_3_
  344.8 12.1 columns_gelu.2
  362.7 8.4 rows.19
  378.4 11.9 collective-permute-done.39
  401.2 16.5 %collective-permute-done.40.refs_1_ = bf16[256,1536]{1,0:T(8,128)(2,1)S(1)} collective-permute-done((bf16[256,1536]{1,0:T(8,128)(2,1)S(1)}, bf16[256,1536]{1,0:T(8,128)(2,1)S(1)}, u32[]{:S(2)}, u32[]{:S(2)}) %collective-permute-start.40) | collective-permute-done | bytes 786464 | tf_op jit(solution)/shard_map/ppermute | solution.py:73
  436.1 7.2 columns_plain.5.x_ref
  443.4 12.6 self_attention.3
  500.8 11.5 collective-permute-done.50
  538.5 17.3 %collective-permute-done.58.refs_1_ = bf16[256,1536]{1,0:T(8,128)(2,1)S(1)} collective-permute-done((bf16[256,1536]{1,0:T(8,128)(2,1)S(1)}, bf16[256,1536]{1,0:T(8,128)(2,1)S(1)}, u32[]{:S(2)}, u32[]{:S(2)}) %collective-permute-start.58) | collective-permute-done | bytes 786464 | tf_op jit(solution)/shard_map/ppermute | solution.py:73
  558.5 8.1 collective-permute-done.60.refs_3_
  567.4 10.4 columns_gelu.3
  594.1 8.4 rows.23
  606.1 10.9 columns_slope.2.act_ref.refs_5_
  622.9 8.5 rows.25
  637.9 10.9 weight_grads.9
  650.3 10.4 weight_grads.8
  689.5 14.2 %collective-permute-done.72.refs_1_ = bf16[256,1536]{1,0:T(8,128)(2,1)S(1)} collective-permute-done((bf16[256,1536]{1,0:T(8,128)(2,1)S(1)}, bf16[256,1536]{1,0:T(8,128)(2,1)S(1)}, u32[]{:S(2)}, u32[]{:S(2)}) %collective-permute-start.72) | collective-permute-done | bytes 786464 | tf_op jit(solution)/shard_map/ppermute | solution.py:73
  727.9 17.6 %self_attention_grad.2.act_ref.refs_5_ = bf16[3,1024,384]{2,1,0:T(8,128)(2,1)S(1)} custom-call(s32[2]{0:T(128)S(1)} %pad_add_fusion.at_ref, bf16[3,1024,384]{2,1,0:T(8,128)(2,1)S(1)} %copy-done.127, bf16[3,1024,128]{2,1,0:T(8,128)(2,1)S(1)} %columns_plain.6.da_ref, f32[3,8,1024]{2,1,0:T(8,128)S(1)} %copy-done.131), custom_call_target="tpu_custom_call" | custom-call | flops 9663676416 | bytes 6291456 | tf_op jit(solution)/shard_map/self_attention_grad/pallas_call | solution.py:353
  752.4 6.9 rows.27
  762.4 7.1 collective-permute-done.79
  784.7 8.6 weight_grads.10
  836.5 7.4 collective-permute-done.90.refs_1_
  857.4 9.7 columns_slope.3.act_ref.refs_5_
  873.8 8.4 rows.29
  886.7 10.6 weight_grads.13
  897.3 11.3 weight_grads.12
  918.4 6.5 cross_attention_grad.3
  941.5 17.0 %collective-permute-done.104.refs_1_ = bf16[256,1536]{1,0:T(8,128)(2,1)S(1)} collective-permute-done((bf16[256,1536]{1,0:T(8,128)(2,1)S(1)}, bf16[256,1536]{1,0:T(8,128)(2,1)S(1)}, u32[]{:S(2)}, u32[]{:S(2)}) %collective-permute-start.104) | collective-permute-done | bytes 786464 | tf_op jit(solution)/shard_map/ppermute | solution.py:73
  960.9 7.6 collective-permute-done.106.refs_3_
  981.0 17.2 %self_attention_grad.3.refs_5_.act_ref = bf16[3,1024,384]{2,1,0:T(8,128)(2,1)S(1)} custom-call(s32[2]{0:T(128)S(1)} %pad_add_fusion.at_ref, bf16[3,1024,384]{2,1,0:T(8,128)(2,1)S(1)} %copy-done.125, bf16[3,1024,128]{2,1,0:T(8,128)(2,1)S(1)} %columns_plain.7.da_ref, f32[3,8,1024]{2,1,0:T(8,128)S(1)} %copy-done.129), custom_call_target="tpu_custom_call" | custom-call | flops 9663676416 | bytes 6291456 | tf_op jit(solution)/shard_map/self_attention_grad/pallas_call | solution.py:353
  1007.7 8.5 weight_grads.14
  1044.7 8.7 collective-permute-done.116
  1070.2 7.2 rows.31
  1088.1 9.4 collective-permute-done.119
  1144.0 22.1 %collective-permute-done.134 = bf16[4,24576]{1,0:T(4,128)(2,1)S(1)} collective-permute-done((bf16[4,24576]{1,0:T(4,128)(2,1)S(1)}, bf16[4,24576]{1,0:T(4,128)(2,1)S(1)}, u32[]{:S(2)}, u32[]{:S(2)}) %collective-permute-start.134) | collective-permute-done | bytes 196640 | tf_op jit(solution)/shard_map/ppermute | solution.py:73
  1235.9 8.4 all-to-all-done.6
  1278.7 9.3 all-to-all-done.11
  (1314 shorter events, 781.4 us)
Async XLA Ops:
  22.9 141.5 %all-gather.17.cloned.1.call-start = ((), (), s32[]{:S(2)}) async-start(), calls=%async_computation.22 | async-start | bytes 3932160 | tf_op jit(solution)/shard_map/all_gather | solution.py:836
  38.4 27.4 %collective-permute-start.4 = (bf16[64,3072]{1,0:T(8,128)(2,1)}, bf16[64,3072]{1,0:T(8,128)(2,1)S(1)}, u32[]{:S(2)}, u32[]{:S(2)}) collective-permute-start(bf16[64,3072]{1,0:T(8,128)(2,1)} %get-tuple-element.842), channel_id=1, source_target_pairs={{0,2},{1,3},{2,0},{3,1},{4,6},{5,7},{6,4},{7,5},{8,10},{9,11},{10,... | collective-permute-start | bytes 1179656 | tf_op jit(solution)/shard_map/ppermute | solution.py:161
  78.2 36.0 %collective-permute-start.6 = (bf16[256,1536]{1,0:T(8,128)(2,1)S(1)}, bf16[256,1536]{1,0:T(8,128)(2,1)S(1)}, u32[]{:S(2)}, u32[]{:S(2)}) collective-permute-start(bf16[256,1536]{1,0:T(8,128)(2,1)S(1)} %fusion.27.refs_0_), channel_id=1, source_target_pairs={{0,8},{4,12},{8,0},{12,4},{16,24},{20,28},{24,16},{28,20},{1,9},{5... | collective-permute-start | bytes 2359304 | tf_op jit(solution)/shard_map/ppermute | solution.py:73
  78.9 35.3 %collective-permute-start.7 = (bf16[256,1536]{1,0:T(8,128)(2,1)S(1)}, bf16[256,1536]{1,0:T(8,128)(2,1)S(1)}, u32[]{:S(2)}, u32[]{:S(2)}) collective-permute-start(bf16[256,1536]{1,0:T(8,128)(2,1)S(1)} %fusion.27.refs_0_), channel_id=1, source_target_pairs={{0,16},{4,20},{8,24},{12,28},{16,0},{20,4},{24,8},{28,12},{1,17},{... | collective-permute-start | bytes 2359304 | tf_op jit(solution)/shard_map/ppermute | solution.py:73
  116.1 26.0 %all-to-all-start.2 = ((bf16[8,64,1536]{2,1,0:T(8,128)(2,1)}), bf16[8,64,1536]{2,1,0:T(8,128)(2,1)}, u32[]{:S(2)}, u32[]{:S(2)}) async-start(bf16[8,64,1536]{2,1,0:T(8,128)(2,1)} %bitcast.446), calls=%async_computation.2 | async-start | bytes 3145728 | tf_op jit(solution)/shard_map/all_to_all | solution.py:82
  120.6 59.8 %all-gather.19.cloned.1.call-start = ((), (), s32[]{:S(2)}) async-start(), calls=%async_computation.23 | async-start | bytes 1474560 | tf_op jit(solution)/shard_map/all_gather | solution.py:859
  145.6 123.7 %all-gather.23.cloned.1.call-start = ((), (), s32[]{:S(2)}) async-start(), calls=%async_computation.25 | async-start | bytes 2949120 | tf_op jit(solution)/shard_map/all_gather | solution.py:677
  168.9 118.6 %all-gather.21.cloned.1.call-start = ((), (), s32[]{:S(2)}) async-start(), calls=%async_computation.24 | async-start | bytes 2949120 | tf_op jit(solution)/shard_map/all_gather | solution.py:677
  182.7 29.1 %collective-permute-start.17 = (bf16[384,1536]{1,0:T(8,128)(2,1)S(1)}, bf16[384,1536]{1,0:T(8,128)(2,1)}, u32[]{:S(2)}, u32[]{:S(2)}) collective-permute-start(bf16[384,1536]{1,0:T(8,128)(2,1)S(1)} %bitcast.449), channel_id=1, source_target_pairs={{0,8},{4,12},{8,0},{12,4},{16,24},{20,28},{24,16},{28,20},{1,9},{5... | collective-permute-start | bytes 3538952 | tf_op jit(solution)/shard_map/ppermute | solution.py:73
  184.5 29.0 %collective-permute-start.18 = (bf16[384,1536]{1,0:T(8,128)(2,1)S(1)}, bf16[384,1536]{1,0:T(8,128)(2,1)}, u32[]{:S(2)}, u32[]{:S(2)}) collective-permute-start(bf16[384,1536]{1,0:T(8,128)(2,1)S(1)} %bitcast.450), channel_id=1, source_target_pairs={{0,16},{4,20},{8,24},{12,28},{16,0},{20,4},{24,8},{28,12},{1,17},{... | collective-permute-start | bytes 3538952 | tf_op jit(solution)/shard_map/ppermute | solution.py:73
  201.0 43.9 %collective-permute-start.21 = (bf16[128,1536]{1,0:T(8,128)(2,1)S(1)}, bf16[128,1536]{1,0:T(8,128)(2,1)}, u32[]{:S(2)}, u32[]{:S(2)}) collective-permute-start(bf16[128,1536]{1,0:T(8,128)(2,1)S(1)} %get-tuple-element.342), channel_id=1, source_target_pairs={{0,16},{4,20},{8,24},{12,28},{16,0},{20,4},{24,8},{28,12},{1,17},{... | collective-permute-start | bytes 1179656 | tf_op jit(solution)/shard_map/ppermute | solution.py:73
  217.8 30.1 %collective-permute-start.19 = (bf16[128,1536]{1,0:T(8,128)(2,1)S(1)}, bf16[128,1536]{1,0:T(8,128)(2,1)S(1)}, u32[]{:S(2)}, u32[]{:S(2)}) collective-permute-start(bf16[128,1536]{1,0:T(8,128)(2,1)S(1)} %get-tuple-element.343), channel_id=1, source_target_pairs={{0,8},{4,12},{8,0},{12,4},{16,24},{20,28},{24,16},{28,20},{1,9},{5... | collective-permute-start | bytes 1179656 | tf_op jit(solution)/shard_map/ppermute | solution.py:73
  243.9 43.7 %collective-permute-start.25 = (bf16[2,768,1536]{2,1,0:T(8,128)(2,1)}, bf16[2,768,1536]{2,1,0:T(8,128)(2,1)}, u32[]{:S(2)}, u32[]{:S(2)}) collective-permute-start(bf16[2,768,1536]{2,1,0:T(8,128)(2,1)} %bitcast.53), channel_id=1, source_target_pairs={{0,4},{4,0},{8,12},{12,8},{16,20},{20,16},{24,28},{28,24},{1,5},{5... | collective-permute-start | bytes 14155784 | tf_op jit(solution)/shard_map/ppermute | solution.py:76
  269.3 75.5 %collective-permute-start.35 = (bf16[4,1,768,384]{3,2,1,0:T(8,128)(2,1)}, bf16[4,1,768,384]{3,2,1,0:T(8,128)(2,1)}, u32[]{:S(2)}, u32[]{:S(2)}) collective-permute-start(bf16[4,1,768,384]{3,2,1,0:T(8,128)(2,1)} %bitcast.415), channel_id=1, source_target_pairs={{0,4},{4,0},{8,12},{12,8},{16,20},{20,16},{24,28},{28,24},{1,5},{5... | collective-permute-start | bytes 7077896 | tf_op jit(solution)/shard_map/ppermute | solution.py:76
  273.7 121.3 %all-gather.25.cloned.1.call-start = ((), (), s32[]{:S(2)}) async-start(), calls=%async_computation.26 | async-start | bytes 3932160 | tf_op jit(solution)/shard_map/all_gather | solution.py:895
  304.2 27.1 %collective-permute-start.32 = (bf16[256,1536]{1,0:T(8,128)(2,1)}, bf16[256,1536]{1,0:T(8,128)(2,1)}, u32[]{:S(2)}, u32[]{:S(2)}) collective-permute-start(bf16[256,1536]{1,0:T(8,128)(2,1)} %add_convert_fusion.16.refs_0_), channel_id=1, source_target_pairs={{0,16},{4,20},{8,24},{12,28},{16,0},{20,4},{24,8},{28,12},{1,17},{... | collective-permute-start | bytes 2359304 | tf_op jit(solution)/shard_map/ppermute | solution.py:73
  317.4 105.6 %all-gather.27.cloned.1.call-start = ((), (), s32[]{:S(2)}) async-start(), calls=%async_computation.27 | async-start | bytes 1474560 | tf_op jit(solution)/shard_map/all_gather | solution.py:896
  376.1 141.6 %all-gather.29.cloned.1.call-start = ((), (), s32[]{:S(2)}) async-start(), calls=%async_computation.28 | async-start | bytes 2949120 | tf_op jit(solution)/shard_map/all_gather | solution.py:677
  397.1 38.9 %collective-permute-start.44 = (bf16[3,4,768,128]{3,2,1,0:T(8,128)(2,1)S(1)}, bf16[3,4,768,128]{3,2,1,0:T(8,128)(2,1)}, u32[]{:S(2)}, u32[]{:S(2)}) collective-permute-start(bf16[3,4,768,128]{3,2,1,0:T(8,128)(2,1)S(1)} %pad_maximum_fusion.33.refs_5_.own_ref), channel_id=1, source_target_pairs={{0,4},{4,0},{8,12},{12,8},{16,20},{20,16},{24,28},{28,24},{1,5},{5... | collective-permute-start | bytes 7077896 | tf_op jit(solution)/shard_map/ppermute | solution.py:76
  434.6 26.0 %collective-permute-start.46 = (bf16[384,1536]{1,0:T(8,128)(2,1)S(1)}, bf16[384,1536]{1,0:T(8,128)(2,1)S(1)}, u32[]{:S(2)}, u32[]{:S(2)}) collective-permute-start(bf16[384,1536]{1,0:T(8,128)(2,1)S(1)} %bitcast.453), channel_id=1, source_target_pairs={{0,16},{4,20},{8,24},{12,28},{16,0},{20,4},{24,8},{28,12},{1,17},{... | collective-permute-start | bytes 3538952 | tf_op jit(solution)/shard_map/ppermute | solution.py:73
  465.4 114.9 %all-gather.31.cloned.1.call-start = ((), (), s32[]{:S(2)}) async-start(), calls=%async_computation.29 | async-start | bytes 2949120 | tf_op jit(solution)/shard_map/all_gather | solution.py:677
  479.1 40.8 %collective-permute-start.53 = (bf16[2,768,1536]{2,1,0:T(8,128)(2,1)}, bf16[2,768,1536]{2,1,0:T(8,128)(2,1)}, u32[]{:S(2)}, u32[]{:S(2)}) collective-permute-start(bf16[2,768,1536]{2,1,0:T(8,128)(2,1)} %bitcast.87), channel_id=1, source_target_pairs={{0,4},{4,0},{8,12},{12,8},{16,20},{20,16},{24,28},{28,24},{1,5},{5... | collective-permute-start | bytes 14155784 | tf_op jit(solution)/shard_map/ppermute | solution.py:76
  495.6 416.9 %reduce-scatter.6.cloned.1.call-start = ((), (), s32[]{:S(2)}) async-start(), calls=%async_computation.17 | async-start | bytes 5898240 | tf_op jit(solution)/shard_map/reduce_scatter | solution.py:689
  517.6 40.8 %collective-permute-start.62 = (bf16[4,1,768,384]{3,2,1,0:T(8,128)(2,1)}, bf16[4,1,768,384]{3,2,1,0:T(8,128)(2,1)S(1)}, u32[]{:S(2)}, u32[]{:S(2)}) collective-permute-start(bf16[4,1,768,384]{3,2,1,0:T(8,128)(2,1)} %bitcast.423), channel_id=1, source_target_pairs={{0,4},{4,0},{8,12},{12,8},{16,20},{20,16},{24,28},{28,24},{1,5},{5... | collective-permute-start | bytes 7077896 | tf_op jit(solution)/shard_map/ppermute | solution.py:76
  592.0 41.7 %collective-permute-start.68 = (bf16[128,1536]{1,0:T(8,128)(2,1)}, bf16[128,1536]{1,0:T(8,128)(2,1)S(1)}, u32[]{:S(2)}, u32[]{:S(2)}) collective-permute-start(bf16[128,1536]{1,0:T(8,128)(2,1)} %get-tuple-element.421), channel_id=1, source_target_pairs={{0,16},{4,20},{8,24},{12,28},{16,0},{20,4},{24,8},{28,12},{1,17},{... | collective-permute-start | bytes 1179656 | tf_op jit(solution)/shard_map/ppermute | solution.py:73
  593.1 40.7 %collective-permute-start.69 = (bf16[128,1536]{1,0:T(8,128)(2,1)}, bf16[128,1536]{1,0:T(8,128)(2,1)S(1)}, u32[]{:S(2)}, u32[]{:S(2)}) collective-permute-start(bf16[128,1536]{1,0:T(8,128)(2,1)} %get-tuple-element.422), channel_id=1, source_target_pairs={{0,8},{4,12},{8,0},{12,4},{16,24},{20,28},{24,16},{28,20},{1,9},{5... | collective-permute-start | bytes 1179656 | tf_op jit(solution)/shard_map/ppermute | solution.py:73
  634.9 25.8 %collective-permute-start.67 = (bf16[256,1536]{1,0:T(8,128)(2,1)}, bf16[256,1536]{1,0:T(8,128)(2,1)}, u32[]{:S(2)}, u32[]{:S(2)}) collective-permute-start(bf16[256,1536]{1,0:T(8,128)(2,1)} %pad_maximum_fusion.57), channel_id=1, source_target_pairs={{0,8},{4,12},{8,0},{12,4},{16,24},{20,28},{24,16},{28,20},{1,9},{5... | collective-permute-start | bytes 2359304 | tf_op jit(solution)/shard_map/ppermute | solution.py:73
  689.0 73.5 %collective-permute-start.86 = (bf16[4,768,384]{2,1,0:T(8,128)(2,1)}, bf16[4,768,384]{2,1,0:T(8,128)(2,1)}, u32[]{:S(2)}, u32[]{:S(2)}) collective-permute-start(bf16[4,768,384]{2,1,0:T(8,128)(2,1)} %get-tuple-element.499), channel_id=1, source_target_pairs={{0,4},{4,0},{8,12},{12,8},{16,20},{20,16},{24,28},{28,24},{1,5},{5... | collective-permute-start | bytes 7077896 | tf_op jit(solution)/shard_map/ppermute | solution.py:76
  689.0 81.4 %collective-permute-start.87 = (bf16[4,768,384]{2,1,0:T(8,128)(2,1)}, bf16[4,768,384]{2,1,0:T(8,128)(2,1)}, u32[]{:S(2)}, u32[]{:S(2)}) collective-permute-start(bf16[4,768,384]{2,1,0:T(8,128)(2,1)} %get-tuple-element.502), channel_id=1, source_target_pairs={{0,4},{4,0},{8,12},{12,8},{16,20},{20,16},{24,28},{28,24},{1,5},{5... | collective-permute-start | bytes 7077896 | tf_op jit(solution)/shard_map/ppermute | solution.py:76
  716.2 29.3 %collective-permute-start.76 = (bf16[64,1536]{1,0:T(8,128)(2,1)S(1)}, bf16[64,1536]{1,0:T(8,128)(2,1)S(1)}, u32[]{:S(2)}, u32[]{:S(2)}) collective-permute-start(bf16[64,1536]{1,0:T(8,128)(2,1)S(1)} %get-tuple-element.894), channel_id=1, source_target_pairs={{0,1},{1,0},{2,3},{3,2},{4,5},{5,4},{6,7},{7,6},{8,9},{9,8},{10,11... | collective-permute-start | bytes 589832 | tf_op jit(solution)/shard_map/ppermute | solution.py:161
  771.4 35.5 %collective-permute-start.82 = (bf16[256,1536]{1,0:T(8,128)(2,1)}, bf16[256,1536]{1,0:T(8,128)(2,1)}, u32[]{:S(2)}, u32[]{:S(2)}) collective-permute-start(bf16[256,1536]{1,0:T(8,128)(2,1)} %pad_maximum_fusion.61), channel_id=1, source_target_pairs={{0,8},{4,12},{8,0},{12,4},{16,24},{20,28},{24,16},{28,20},{1,9},{5... | collective-permute-start | bytes 2359304 | tf_op jit(solution)/shard_map/ppermute | solution.py:73
  773.2 33.7 %collective-permute-start.80 = (bf16[256,1536]{1,0:T(8,128)(2,1)}, bf16[256,1536]{1,0:T(8,128)(2,1)}, u32[]{:S(2)}, u32[]{:S(2)}) collective-permute-start(bf16[256,1536]{1,0:T(8,128)(2,1)} %pad_maximum_fusion.60), channel_id=1, source_target_pairs={{0,16},{4,20},{8,24},{12,28},{16,0},{20,4},{24,8},{28,12},{1,17},{... | collective-permute-start | bytes 2359304 | tf_op jit(solution)/shard_map/ppermute | solution.py:73
  806.9 192.6 %reduce-scatter.8.cloned.1.call-start = ((), (), s32[]{:S(2)}) async-start(), calls=%async_computation.18 | async-start | bytes 3932160 | tf_op jit(solution)/shard_map/reduce_scatter | solution.py:689
  855.5 26.8 %collective-permute-start.98 = (bf16[192,1536]{1,0:T(8,128)(2,1)}, bf16[192,1536]{1,0:T(8,128)(2,1)S(1)}, u32[]{:S(2)}, u32[]{:S(2)}) collective-permute-start(bf16[192,1536]{1,0:T(8,128)(2,1)} %get-tuple-element.533), channel_id=1, source_target_pairs={{0,16},{4,20},{8,24},{12,28},{16,0},{20,4},{24,8},{28,12},{1,17},{... | collective-permute-start | bytes 1769480 | tf_op jit(solution)/shard_map/ppermute | solution.py:73
  856.3 25.9 %collective-permute-start.99 = (bf16[192,1536]{1,0:T(8,128)(2,1)}, bf16[192,1536]{1,0:T(8,128)(2,1)S(1)}, u32[]{:S(2)}, u32[]{:S(2)}) collective-permute-start(bf16[192,1536]{1,0:T(8,128)(2,1)} %get-tuple-element.534), channel_id=1, source_target_pairs={{0,8},{4,12},{8,0},{12,4},{16,24},{20,28},{24,16},{28,20},{1,9},{5... | collective-permute-start | bytes 1769480 | tf_op jit(solution)/shard_map/ppermute | solution.py:73
  873.8 358.6 %reduce-scatter.12.cloned.1.call-start = ((), (), s32[]{:S(2)}) async-start(), calls=%async_computation.20 | async-start | bytes 3932160 | tf_op jit(solution)/shard_map/reduce_scatter | solution.py:689
  970.4 29.2 %collective-permute-start.108 = (bf16[8,6144]{1,0:T(8,128)(2,1)}, bf16[8,6144]{1,0:T(8,128)(2,1)}, u32[]{:S(2)}, u32[]{:S(2)}) collective-permute-start(bf16[8,6144]{1,0:T(8,128)(2,1)} %get-tuple-element.883), channel_id=1, source_target_pairs={{0,16},{4,20},{8,24},{12,28},{16,0},{20,4},{24,8},{28,12},{1,17},{... | collective-permute-start | bytes 294920 | tf_op jit(solution)/shard_map/ppermute | solution.py:73
  971.1 28.5 %collective-permute-start.109 = (bf16[8,6144]{1,0:T(8,128)(2,1)}, bf16[8,6144]{1,0:T(8,128)(2,1)}, u32[]{:S(2)}, u32[]{:S(2)}) collective-permute-start(bf16[8,6144]{1,0:T(8,128)(2,1)} %get-tuple-element.882), channel_id=1, source_target_pairs={{0,8},{4,12},{8,0},{12,4},{16,24},{20,28},{24,16},{28,20},{1,9},{5... | collective-permute-start | bytes 294920 | tf_op jit(solution)/shard_map/ppermute | solution.py:73
  973.4 50.2 %collective-permute-start.113 = (bf16[384,1536]{1,0:T(8,128)(2,1)}, bf16[384,1536]{1,0:T(8,128)(2,1)}, u32[]{:S(2)}, u32[]{:S(2)}) collective-permute-start(bf16[384,1536]{1,0:T(8,128)(2,1)} %pad_maximum_fusion.45), channel_id=1, source_target_pairs={{0,8},{4,12},{8,0},{12,4},{16,24},{20,28},{24,16},{28,20},{1,9},{5... | collective-permute-start | bytes 3538952 | tf_op jit(solution)/shard_map/ppermute | solution.py:73
  975.7 47.9 %collective-permute-start.112 = (bf16[384,1536]{1,0:T(8,128)(2,1)}, bf16[384,1536]{1,0:T(8,128)(2,1)}, u32[]{:S(2)}, u32[]{:S(2)}) collective-permute-start(bf16[384,1536]{1,0:T(8,128)(2,1)} %pad_maximum_fusion.44), channel_id=1, source_target_pairs={{0,16},{4,20},{8,24},{12,28},{16,0},{20,4},{24,8},{28,12},{1,17},{... | collective-permute-start | bytes 3538952 | tf_op jit(solution)/shard_map/ppermute | solution.py:73
  1041.4 206.5 %reduce-scatter.10.cloned.1.call-start = ((), (), s32[]{:S(2)}) async-start(), calls=%async_computation.19 | async-start | bytes 5898240 | tf_op jit(solution)/shard_map/reduce_scatter | solution.py:689
  1113.7 71.2 %collective-permute-start.137 = (f32[12,1536]{1,0:T(8,128)}, f32[12,1536]{1,0:T(8,128)}, u32[]{:S(2)}, u32[]{:S(2)}) collective-permute-start(f32[12,1536]{1,0:T(8,128)} %reorder.11), channel_id=1, source_target_pairs={{0,4},{4,0},{8,12},{12,8},{16,20},{20,16},{24,28},{28,24},{1,5},{5... | collective-permute-start | bytes 221192 | tf_op jit(solution)/shard_map/ppermute | solution.py:189
  1129.8 40.5 %collective-permute-start.136 = (bf16[384,1536]{1,0:T(8,128)(2,1)}, bf16[384,1536]{1,0:T(8,128)(2,1)}, u32[]{:S(2)}, u32[]{:S(2)}) collective-permute-start(bf16[384,1536]{1,0:T(8,128)(2,1)} %pad_maximum_fusion.47), channel_id=1, source_target_pairs={{0,8},{4,12},{8,0},{12,4},{16,24},{20,28},{24,16},{28,20},{1,9},{5... | collective-permute-start | bytes 3538952 | tf_op jit(solution)/shard_map/ppermute | solution.py:73
  1139.1 27.0 %collective-permute-start.134 = (bf16[4,24576]{1,0:T(4,128)(2,1)S(1)}, bf16[4,24576]{1,0:T(4,128)(2,1)S(1)}, u32[]{:S(2)}, u32[]{:S(2)}) collective-permute-start(bf16[4,24576]{1,0:T(4,128)(2,1)S(1)} %slice.881), channel_id=1, source_target_pairs={{0,8},{4,12},{8,0},{12,4},{16,24},{20,28},{24,16},{28,20},{1,9},{5... | collective-permute-start | bytes 589832 | tf_op jit(solution)/shard_map/ppermute | solution.py:73
  1140.7 29.5 %collective-permute-start.135 = (bf16[384,1536]{1,0:T(8,128)(2,1)}, bf16[384,1536]{1,0:T(8,128)(2,1)}, u32[]{:S(2)}, u32[]{:S(2)}) collective-permute-start(bf16[384,1536]{1,0:T(8,128)(2,1)} %pad_maximum_fusion.46), channel_id=1, source_target_pairs={{0,16},{4,20},{8,24},{12,28},{16,0},{20,4},{24,8},{28,12},{1,17},{... | collective-permute-start | bytes 3538952 | tf_op jit(solution)/shard_map/ppermute | solution.py:73
  1215.5 28.8 %all-to-all-start.6 = ((bf16[4,192,1280]{2,1,0:T(8,128)(2,1)}), bf16[4,192,1280]{2,1,0:T(8,128)(2,1)}, u32[]{:S(2)}, u32[]{:S(2)}) async-start(bf16[4,192,1280]{2,1,0:T(8,128)(2,1)} %pad_maximum_fusion.35), calls=%async_computation.8 | async-start | bytes 3932160 | tf_op jit(solution)/shard_map/all_to_all | solution.py:79
  1220.0 74.5 %reduce-scatter.14.cloned.1.call-start = ((), (), s32[]{:S(2)}) async-start(), calls=%async_computation.21 | async-start | bytes 2949120 | tf_op jit(solution)/shard_map/reduce_scatter | solution.py:689
  1244.4 26.5 %all-to-all-start.10 = ((bf16[4,192,512]{2,1,0:T(8,128)(2,1)}), bf16[4,192,512]{2,1,0:T(8,128)(2,1)S(1)}, u32[]{:S(2)}, u32[]{:S(2)}) async-start(bf16[4,192,512]{2,1,0:T(8,128)(2,1)} %bitcast.171), calls=%async_computation.14 | async-start | bytes 1572864 | tf_op jit(solution)/shard_map/all_to_all | solution.py:79
  (412 other events, 3978.8 us)
Sparse Core Ops, SparseCore 0:
  67.8 71.4 all-gather.16
  141.4 33.4 all-gather.18
  177.0 49.3 all-gather.22
  228.3 49.2 all-gather.20
  302.9 64.7 all-gather.24
  376.2 31.7 all-gather.26
  465.5 51.6 all-gather.28
  519.3 49.2 all-gather.30
  807.1 83.6 reduce-scatter.5
  893.0 60.7 reduce-scatter.7
  1041.5 58.5 reduce-scatter.11
  1102.3 86.5 reduce-scatter.9
  1234.4 46.6 reduce-scatter.13

commit v4 on v3

--- a/solution.py
+++ b/solution.py
@@ -989,7 +989,7 @@
             state = grid.scatter_begin(top)
             qkv_pair = weight_grads(after(k["full_one"], state), d_qkv)
             out_pair = weight_grads(after(dy_one, state), k["attn_low"])
-            fill = [qkv_pair, out_pair, output, hidden_grad_slots(grid, hidden_pairs, state), cross_products(state)]
+            fill = [qkv_pair, out_pair, output, hidden_grad_slots(grid, hidden_pairs, state)]
         else:
             qkv_pair = weight_grads(k["full_one"], d_qkv)
             out_pair = weight_grads(dy_one, after(k["attn_low"], d_qkv))
@@ -1007,7 +1007,8 @@
         if n == 0:
             cross_state, cross_last = grid.scatter_begin(fill[0]), fill[1]
         if n > 0:
-            qkv_pair, out_pair, output, hidden_slots_grad, cross_lows = fill
+            qkv_pair, out_pair, output, hidden_slots_grad = fill
+            cross_lows = cross_products(grad_normed)
             hidden_sums[n] = col_sum(hidden_slots_grad)
             self_slots_grad = self_grad_slots(grid, [qkv_pair, out_pair], grad_normed)
         grad_res, gain_one, shift_one = norm_backward(grad_normed, k["normed_one"], k["inv_one"], gains[n, 0])
@@ -1027,7 +1028,6 @@
     for n in range(LAYERS):
         for side, mats in enumerate((cross_key, cross_value)):
             text_part = text_part + product_nt(text_full[:, 2 * n + side], mats[n])
-    text_grad = text_out(grid, text_part)
     early = [hidden_sums[n] for n in range(1, LAYERS)] + [self_sums[n] for n in range(1, LAYERS)]
     widths = [value.shape[1] for value in early]
     moved = jnp.concatenate([value.reshape(grid.T, rows, value.shape[1]) for value in early], axis=2)
@@ -1036,6 +1036,8 @@
     input_grad = grid.tokens_out_end(input_grad).astype(F32)
     parts = [moved[:, :, sum(widths[:m]) : sum(widths[: m + 1])] for m in range(len(early))]
     first = [grid.plane_a2a(value[0].reshape(grid.T, rows, value[0].shape[1])) for value in (hidden_sums, self_sums)]
+    text_part, first = meet(text_part, first)
+    text_grad = text_out(grid, text_part)
     hidden_out = [hidden_grad_blocks(grid, part, 2) for part in [first[0]] + parts[: LAYERS - 1]]
     self_out_grads = [self_grad_blocks(grid, part, units) for part in [first[1]] + parts[LAYERS - 1 :]]
     totals = grid.total(own_last(grid, jnp.concatenate(norms, axis=0))).reshape(LAYERS, 6, -1)

time: 1320 us -> 1310 us (level)
  no operation moved by 1% of the time
where the time goes in v4:
time: 1310 us; the launch traced here: 1300 us
  waiting for transfers between devices  381 us (29%)
  Pallas kernels  310 us (24%)
  starting transfers between devices  204 us (16%)
  local copies, waits for them, and re-layouts  189 us (14%)
  other arithmetic  171 us (13%)
  matrix products  28.9 us (2%)
  between operations  18.8 us (1%)
    ppermute x101, waiting for transfers between devices, swap(): return lax.ppermute(value, 'row', [(r, r ^ 2 * d) for r in range(self.R)])  290 us
    ppermute x101, starting transfers between devices, swap(): return lax.ppermute(value, 'row', [(r, r ^ 2 * d) for r in range(self.R)])  108 us
    pallas_call x16, Pallas kernels, rows_product(): pl.pallas_call(functools.partial(rows_kernel, (0,) if len(mats) == 1 else...  80.5 us
    pallas_call x8, Pallas kernels, weight_grads(): pl.pallas_call(functools.partial(grads_kernel, len(pieces)), grid=(blocks...  68.6 us
    pallas_call x8, Pallas kernels, columns_product(): pl.pallas_call(functools.partial(columns_kernel, (0,) if len(mats) == 1 e...  64.7 us
    unnamed x594, local copies, waits for them, and re-layouts  47.2 us
    pallas_call x2, Pallas kernels, self_attention_grad(): pl.pallas_call(functools.partial(self_backward_kernel, grid, width), grid...  34.6 us
    all_to_all x7, waiting for transfers between devices, plane_a2a(): lax.all_to_all(value, 'row', 0, 0, tiled=True, axis_index_groups=self.gro...  28.6 us
  transfers between devices with their start and end apart: 167, of which 65 were waited for; matrix products, arithmetic and copies ran while one was open for 25% of the time, Pallas kernels for 24%

profile of v4, /device:TPU:0, one launch (start us, length us, event | category | flops | bytes accessed | tf_op | source)
XLA Modules:
  0.0 1302.0 jit_solution(11809838145948295749)
XLA Ops:
  22.9 12.9 collective-permute-done.1
  42.4 8.3 collective-permute-done.3
  50.7 15.0 %collective-permute-done.4 = bf16[64,3072]{1,0:T(8,128)(2,1)S(1)} collective-permute-done((bf16[64,3072]{1,0:T(8,128)(2,1)}, bf16[64,3072]{1,0:T(8,128)(2,1)S(1)}, u32[]{:S(2)}, u32[]{:S(2)}) %collective-permute-start.4) | collective-permute-done | bytes 393248 | tf_op jit(solution)/shard_map/ppermute | solution.py:161
  85.3 6.8 all-to-all-done.1
  92.1 8.9 collective-permute-start.10
  148.1 6.6 collective-permute-start.13
  172.2 6.8 columns_plain.4.x_ref
  186.0 12.6 self_attention.2
  229.4 8.5 collective-permute-done.23
  255.0 11.5 collective-permute-done.22
  275.9 10.0 all-to-all-done.4
  312.4 11.6 collective-permute-done.31.refs_1_
  338.1 7.1 collective-permute-done.33.refs_3_
  345.3 11.8 columns_gelu.2
  362.9 8.4 rows.19
  378.6 11.9 collective-permute-done.39
  403.3 17.2 %collective-permute-done.40.refs_1_ = bf16[256,1536]{1,0:T(8,128)(2,1)S(1)} collective-permute-done((bf16[256,1536]{1,0:T(8,128)(2,1)S(1)}, bf16[256,1536]{1,0:T(8,128)(2,1)S(1)}, u32[]{:S(2)}, u32[]{:S(2)}) %collective-permute-start.40) | collective-permute-done | bytes 786464 | tf_op jit(solution)/shard_map/ppermute | solution.py:73
  439.8 7.3 columns_plain.5.x_ref
  447.1 12.6 self_attention.3
  469.1 7.3 collective-permute-done.51
  505.0 11.7 collective-permute-done.50
  543.0 17.9 %collective-permute-done.58.refs_1_ = bf16[256,1536]{1,0:T(8,128)(2,1)S(1)} collective-permute-done((bf16[256,1536]{1,0:T(8,128)(2,1)S(1)}, bf16[256,1536]{1,0:T(8,128)(2,1)S(1)}, u32[]{:S(2)}, u32[]{:S(2)}) %collective-permute-start.58) | collective-permute-done | bytes 786464 | tf_op jit(solution)/shard_map/ppermute | solution.py:73
  563.0 8.8 collective-permute-done.60.refs_3_
  572.6 10.5 columns_gelu.3
  599.1 8.4 rows.23
  611.1 10.4 columns_slope.2.act_ref.refs_5_
  627.5 8.5 rows.25
  642.5 10.6 weight_grads.9
  654.6 10.6 weight_grads.8
  694.2 14.2 %collective-permute-done.72.refs_1_ = bf16[256,1536]{1,0:T(8,128)(2,1)S(1)} collective-permute-done((bf16[256,1536]{1,0:T(8,128)(2,1)S(1)}, bf16[256,1536]{1,0:T(8,128)(2,1)S(1)}, u32[]{:S(2)}, u32[]{:S(2)}) %collective-permute-start.72) | collective-permute-done | bytes 786464 | tf_op jit(solution)/shard_map/ppermute | solution.py:73
  732.9 17.4 %self_attention_grad.2.act_ref.refs_5_ = bf16[3,1024,384]{2,1,0:T(8,128)(2,1)S(1)} custom-call(s32[2]{0:T(128)S(1)} %pad_add_fusion.at_ref, bf16[3,1024,384]{2,1,0:T(8,128)(2,1)S(1)} %copy-done.121, bf16[3,1024,128]{2,1,0:T(8,128)(2,1)S(1)} %columns_plain.6.da_ref, f32[3,8,1024]{2,1,0:T(8,128)S(1)} %copy-done.125), custom_call_target="tpu_custom_call" | custom-call | flops 9663676416 | bytes 6291456 | tf_op jit(solution)/shard_map/self_attention_grad/pallas_call | solution.py:353
  757.1 6.9 rows.27
  767.2 7.2 collective-permute-done.79
  796.7 8.6 weight_grads.10
  838.2 8.2 collective-permute-done.90.refs_1_
  860.0 9.7 columns_slope.3.act_ref.refs_5_
  876.7 8.4 rows.29
  889.8 10.1 weight_grads.13
  899.9 11.2 weight_grads.12
  943.9 17.1 %collective-permute-done.104.refs_1_ = bf16[256,1536]{1,0:T(8,128)(2,1)S(1)} collective-permute-done((bf16[256,1536]{1,0:T(8,128)(2,1)S(1)}, bf16[256,1536]{1,0:T(8,128)(2,1)S(1)}, u32[]{:S(2)}, u32[]{:S(2)}) %collective-permute-start.104) | collective-permute-done | bytes 786464 | tf_op jit(solution)/shard_map/ppermute | solution.py:73
  963.3 7.7 collective-permute-done.106.refs_3_
  983.4 17.2 %self_attention_grad.3.refs_5_.act_ref = bf16[3,1024,384]{2,1,0:T(8,128)(2,1)S(1)} custom-call(s32[2]{0:T(128)S(1)} %pad_add_fusion.at_ref, bf16[3,1024,384]{2,1,0:T(8,128)(2,1)S(1)} %copy-done.119, bf16[3,1024,128]{2,1,0:T(8,128)(2,1)S(1)} %columns_plain.7.da_ref, f32[3,8,1024]{2,1,0:T(8,128)S(1)} %copy-done.123), custom_call_target="tpu_custom_call" | custom-call | flops 9663676416 | bytes 6291456 | tf_op jit(solution)/shard_map/self_attention_grad/pallas_call | solution.py:353
  1011.3 8.6 weight_grads.14
  1064.4 7.0 rows.31
  1082.8 9.8 collective-permute-done.119
  1157.4 15.2 %collective-permute-done.131 = bf16[8,24576]{1,0:T(8,128)(2,1)S(1)} collective-permute-done((bf16[8,24576]{1,0:T(8,128)(2,1)}, bf16[8,24576]{1,0:T(8,128)(2,1)S(1)}, u32[]{:S(2)}, u32[]{:S(2)}) %collective-permute-start.131) | collective-permute-done | bytes 393248 | tf_op jit(solution)/shard_map/ppermute | solution.py:73
  1180.5 21.2 %collective-permute-done.133 = bf16[4,24576]{1,0:T(4,128)(2,1)S(1)} collective-permute-done((bf16[4,24576]{1,0:T(4,128)(2,1)S(1)}, bf16[4,24576]{1,0:T(4,128)(2,1)S(1)}, u32[]{:S(2)}, u32[]{:S(2)}) %collective-permute-start.133) | collective-permute-done | bytes 196640 | tf_op jit(solution)/shard_map/ppermute | solution.py:73
  1255.6 7.3 all-to-all-done.8
  (1312 shorter events, 769.7 us)
Async XLA Ops:
  22.9 141.5 %all-gather.17.cloned.1.call-start = ((), (), s32[]{:S(2)}) async-start(), calls=%async_computation.22 | async-start | bytes 3932160 | tf_op jit(solution)/shard_map/all_gather | solution.py:836
  38.4 27.4 %collective-permute-start.4 = (bf16[64,3072]{1,0:T(8,128)(2,1)}, bf16[64,3072]{1,0:T(8,128)(2,1)S(1)}, u32[]{:S(2)}, u32[]{:S(2)}) collective-permute-start(bf16[64,3072]{1,0:T(8,128)(2,1)} %get-tuple-element.844), channel_id=1, source_target_pairs={{0,2},{1,3},{2,0},{3,1},{4,6},{5,7},{6,4},{7,5},{8,10},{9,11},{10,... | collective-permute-start | bytes 1179656 | tf_op jit(solution)/shard_map/ppermute | solution.py:161
  78.2 36.1 %collective-permute-start.6 = (bf16[256,1536]{1,0:T(8,128)(2,1)S(1)}, bf16[256,1536]{1,0:T(8,128)(2,1)S(1)}, u32[]{:S(2)}, u32[]{:S(2)}) collective-permute-start(bf16[256,1536]{1,0:T(8,128)(2,1)S(1)} %fusion.27.refs_0_), channel_id=1, source_target_pairs={{0,8},{4,12},{8,0},{12,4},{16,24},{20,28},{24,16},{28,20},{1,9},{5... | collective-permute-start | bytes 2359304 | tf_op jit(solution)/shard_map/ppermute | solution.py:73
  79.0 35.3 %collective-permute-start.7 = (bf16[256,1536]{1,0:T(8,128)(2,1)S(1)}, bf16[256,1536]{1,0:T(8,128)(2,1)S(1)}, u32[]{:S(2)}, u32[]{:S(2)}) collective-permute-start(bf16[256,1536]{1,0:T(8,128)(2,1)S(1)} %fusion.27.refs_0_), channel_id=1, source_target_pairs={{0,16},{4,20},{8,24},{12,28},{16,0},{20,4},{24,8},{28,12},{1,17},{... | collective-permute-start | bytes 2359304 | tf_op jit(solution)/shard_map/ppermute | solution.py:73
  120.6 59.8 %all-gather.19.cloned.1.call-start = ((), (), s32[]{:S(2)}) async-start(), calls=%async_computation.23 | async-start | bytes 1474560 | tf_op jit(solution)/shard_map/all_gather | solution.py:859
  145.7 124.1 %all-gather.23.cloned.1.call-start = ((), (), s32[]{:S(2)}) async-start(), calls=%async_computation.25 | async-start | bytes 2949120 | tf_op jit(solution)/shard_map/all_gather | solution.py:677
  168.9 119.1 %all-gather.21.cloned.1.call-start = ((), (), s32[]{:S(2)}) async-start(), calls=%async_computation.24 | async-start | bytes 2949120 | tf_op jit(solution)/shard_map/all_gather | solution.py:677
  182.8 29.1 %collective-permute-start.17 = (bf16[384,1536]{1,0:T(8,128)(2,1)S(1)}, bf16[384,1536]{1,0:T(8,128)(2,1)}, u32[]{:S(2)}, u32[]{:S(2)}) collective-permute-start(bf16[384,1536]{1,0:T(8,128)(2,1)S(1)} %bitcast.445), channel_id=1, source_target_pairs={{0,8},{4,12},{8,0},{12,4},{16,24},{20,28},{24,16},{28,20},{1,9},{5... | collective-permute-start | bytes 3538952 | tf_op jit(solution)/shard_map/ppermute | solution.py:73
  184.6 29.0 %collective-permute-start.18 = (bf16[384,1536]{1,0:T(8,128)(2,1)S(1)}, bf16[384,1536]{1,0:T(8,128)(2,1)}, u32[]{:S(2)}, u32[]{:S(2)}) collective-permute-start(bf16[384,1536]{1,0:T(8,128)(2,1)S(1)} %bitcast.446), channel_id=1, source_target_pairs={{0,16},{4,20},{8,24},{12,28},{16,0},{20,4},{24,8},{28,12},{1,17},{... | collective-permute-start | bytes 3538952 | tf_op jit(solution)/shard_map/ppermute | solution.py:73
  201.1 44.3 %collective-permute-start.21 = (bf16[128,1536]{1,0:T(8,128)(2,1)S(1)}, bf16[128,1536]{1,0:T(8,128)(2,1)}, u32[]{:S(2)}, u32[]{:S(2)}) collective-permute-start(bf16[128,1536]{1,0:T(8,128)(2,1)S(1)} %get-tuple-element.343), channel_id=1, source_target_pairs={{0,16},{4,20},{8,24},{12,28},{16,0},{20,4},{24,8},{28,12},{1,17},{... | collective-permute-start | bytes 1179656 | tf_op jit(solution)/shard_map/ppermute | solution.py:73
  217.9 30.4 %collective-permute-start.19 = (bf16[128,1536]{1,0:T(8,128)(2,1)S(1)}, bf16[128,1536]{1,0:T(8,128)(2,1)S(1)}, u32[]{:S(2)}, u32[]{:S(2)}) collective-permute-start(bf16[128,1536]{1,0:T(8,128)(2,1)S(1)} %get-tuple-element.344), channel_id=1, source_target_pairs={{0,8},{4,12},{8,0},{12,4},{16,24},{20,28},{24,16},{28,20},{1,9},{5... | collective-permute-start | bytes 1179656 | tf_op jit(solution)/shard_map/ppermute | solution.py:73
  244.3 43.7 %collective-permute-start.25 = (bf16[2,768,1536]{2,1,0:T(8,128)(2,1)}, bf16[2,768,1536]{2,1,0:T(8,128)(2,1)}, u32[]{:S(2)}, u32[]{:S(2)}) collective-permute-start(bf16[2,768,1536]{2,1,0:T(8,128)(2,1)} %bitcast.53), channel_id=1, source_target_pairs={{0,4},{4,0},{8,12},{12,8},{16,20},{20,16},{24,28},{28,24},{1,5},{5... | collective-permute-start | bytes 14155784 | tf_op jit(solution)/shard_map/ppermute | solution.py:76
  269.7 75.5 %collective-permute-start.35 = (bf16[4,1,768,384]{3,2,1,0:T(8,128)(2,1)}, bf16[4,1,768,384]{3,2,1,0:T(8,128)(2,1)}, u32[]{:S(2)}, u32[]{:S(2)}) collective-permute-start(bf16[4,1,768,384]{3,2,1,0:T(8,128)(2,1)} %bitcast.415), channel_id=1, source_target_pairs={{0,4},{4,0},{8,12},{12,8},{16,20},{20,16},{24,28},{28,24},{1,5},{5... | collective-permute-start | bytes 7077896 | tf_op jit(solution)/shard_map/ppermute | solution.py:76
  274.2 122.4 %all-gather.25.cloned.1.call-start = ((), (), s32[]{:S(2)}) async-start(), calls=%async_computation.26 | async-start | bytes 3932160 | tf_op jit(solution)/shard_map/all_gather | solution.py:895
  307.9 30.2 %all-to-all-start.5 = ((bf16[4,2,192,384]{3,2,1,0:T(8,128)(2,1)}), bf16[4,2,192,384]{3,2,1,0:T(8,128)(2,1)}, u32[]{:S(2)}, u32[]{:S(2)}) async-start(bf16[4,2,192,384]{3,2,1,0:T(8,128)(2,1)} %copy.131), calls=%async_computation.5 | async-start | bytes 2359296 | tf_op jit(solution)/shard_map/all_to_all | solution.py:79
  312.4 113.5 %all-gather.27.cloned.1.call-start = ((), (), s32[]{:S(2)}) async-start(), calls=%async_computation.27 | async-start | bytes 1474560 | tf_op jit(solution)/shard_map/all_gather | solution.py:896
  376.2 146.3 %all-gather.29.cloned.1.call-start = ((), (), s32[]{:S(2)}) async-start(), calls=%async_computation.28 | async-start | bytes 2949120 | tf_op jit(solution)/shard_map/all_gather | solution.py:677
  398.6 41.1 %collective-permute-start.44 = (bf16[3,4,768,128]{3,2,1,0:T(8,128)(2,1)S(1)}, bf16[3,4,768,128]{3,2,1,0:T(8,128)(2,1)}, u32[]{:S(2)}, u32[]{:S(2)}) collective-permute-start(bf16[3,4,768,128]{3,2,1,0:T(8,128)(2,1)S(1)} %pad_maximum_fusion.33.refs_5_.own_ref), channel_id=1, source_target_pairs={{0,4},{4,0},{8,12},{12,8},{16,20},{20,16},{24,28},{28,24},{1,5},{5... | collective-permute-start | bytes 7077896 | tf_op jit(solution)/shard_map/ppermute | solution.py:76
  469.0 116.4 %all-gather.31.cloned.1.call-start = ((), (), s32[]{:S(2)}) async-start(), calls=%async_computation.29 | async-start | bytes 2949120 | tf_op jit(solution)/shard_map/all_gather | solution.py:677
  483.6 41.3 %collective-permute-start.53 = (bf16[2,768,1536]{2,1,0:T(8,128)(2,1)}, bf16[2,768,1536]{2,1,0:T(8,128)(2,1)}, u32[]{:S(2)}, u32[]{:S(2)}) collective-permute-start(bf16[2,768,1536]{2,1,0:T(8,128)(2,1)} %bitcast.87), channel_id=1, source_target_pairs={{0,4},{4,0},{8,12},{12,8},{16,20},{20,16},{24,28},{28,24},{1,5},{5... | collective-permute-start | bytes 14155784 | tf_op jit(solution)/shard_map/ppermute | solution.py:76
  500.0 415.1 %reduce-scatter.6.cloned.1.call-start = ((), (), s32[]{:S(2)}) async-start(), calls=%async_computation.17 | async-start | bytes 5898240 | tf_op jit(solution)/shard_map/reduce_scatter | solution.py:689
  522.6 40.4 %collective-permute-start.62 = (bf16[4,1,768,384]{3,2,1,0:T(8,128)(2,1)}, bf16[4,1,768,384]{3,2,1,0:T(8,128)(2,1)S(1)}, u32[]{:S(2)}, u32[]{:S(2)}) collective-permute-start(bf16[4,1,768,384]{3,2,1,0:T(8,128)(2,1)} %bitcast.423), channel_id=1, source_target_pairs={{0,4},{4,0},{8,12},{12,8},{16,20},{20,16},{24,28},{28,24},{1,5},{5... | collective-permute-start | bytes 7077896 | tf_op jit(solution)/shard_map/ppermute | solution.py:76
  597.2 41.1 %collective-permute-start.68 = (bf16[128,1536]{1,0:T(8,128)(2,1)}, bf16[128,1536]{1,0:T(8,128)(2,1)S(1)}, u32[]{:S(2)}, u32[]{:S(2)}) collective-permute-start(bf16[128,1536]{1,0:T(8,128)(2,1)} %get-tuple-element.422), channel_id=1, source_target_pairs={{0,16},{4,20},{8,24},{12,28},{16,0},{20,4},{24,8},{28,12},{1,17},{... | collective-permute-start | bytes 1179656 | tf_op jit(solution)/shard_map/ppermute | solution.py:73
  598.3 40.0 %collective-permute-start.69 = (bf16[128,1536]{1,0:T(8,128)(2,1)}, bf16[128,1536]{1,0:T(8,128)(2,1)S(1)}, u32[]{:S(2)}, u32[]{:S(2)}) collective-permute-start(bf16[128,1536]{1,0:T(8,128)(2,1)} %get-tuple-element.423), channel_id=1, source_target_pairs={{0,8},{4,12},{8,0},{12,4},{16,24},{20,28},{24,16},{28,20},{1,9},{5... | collective-permute-start | bytes 1179656 | tf_op jit(solution)/shard_map/ppermute | solution.py:73
  693.7 73.6 %collective-permute-start.86 = (bf16[4,768,384]{2,1,0:T(8,128)(2,1)}, bf16[4,768,384]{2,1,0:T(8,128)(2,1)}, u32[]{:S(2)}, u32[]{:S(2)}) collective-permute-start(bf16[4,768,384]{2,1,0:T(8,128)(2,1)} %get-tuple-element.500), channel_id=1, source_target_pairs={{0,4},{4,0},{8,12},{12,8},{16,20},{20,16},{24,28},{28,24},{1,5},{5... | collective-permute-start | bytes 7077896 | tf_op jit(solution)/shard_map/ppermute | solution.py:76
  693.7 81.5 %collective-permute-start.87 = (bf16[4,768,384]{2,1,0:T(8,128)(2,1)}, bf16[4,768,384]{2,1,0:T(8,128)(2,1)}, u32[]{:S(2)}, u32[]{:S(2)}) collective-permute-start(bf16[4,768,384]{2,1,0:T(8,128)(2,1)} %get-tuple-element.503), channel_id=1, source_target_pairs={{0,4},{4,0},{8,12},{12,8},{16,20},{20,16},{24,28},{28,24},{1,5},{5... | collective-permute-start | bytes 7077896 | tf_op jit(solution)/shard_map/ppermute | solution.py:76
  721.4 28.9 %collective-permute-start.76 = (bf16[64,1536]{1,0:T(8,128)(2,1)S(1)}, bf16[64,1536]{1,0:T(8,128)(2,1)S(1)}, u32[]{:S(2)}, u32[]{:S(2)}) collective-permute-start(bf16[64,1536]{1,0:T(8,128)(2,1)S(1)} %get-tuple-element.896), channel_id=1, source_target_pairs={{0,1},{1,0},{2,3},{3,2},{4,5},{5,4},{6,7},{7,6},{8,9},{9,8},{10,11... | collective-permute-start | bytes 589832 | tf_op jit(solution)/shard_map/ppermute | solution.py:161
  776.2 29.0 %collective-permute-start.82 = (bf16[256,1536]{1,0:T(8,128)(2,1)}, bf16[256,1536]{1,0:T(8,128)(2,1)}, u32[]{:S(2)}, u32[]{:S(2)}) collective-permute-start(bf16[256,1536]{1,0:T(8,128)(2,1)} %pad_maximum_fusion.61), channel_id=1, source_target_pairs={{0,8},{4,12},{8,0},{12,4},{16,24},{20,28},{24,16},{28,20},{1,9},{5... | collective-permute-start | bytes 2359304 | tf_op jit(solution)/shard_map/ppermute | solution.py:73
  778.1 27.1 %collective-permute-start.80 = (bf16[256,1536]{1,0:T(8,128)(2,1)}, bf16[256,1536]{1,0:T(8,128)(2,1)}, u32[]{:S(2)}, u32[]{:S(2)}) collective-permute-start(bf16[256,1536]{1,0:T(8,128)(2,1)} %pad_maximum_fusion.60), channel_id=1, source_target_pairs={{0,16},{4,20},{8,24},{12,28},{16,0},{20,4},{24,8},{28,12},{1,17},{... | collective-permute-start | bytes 2359304 | tf_op jit(solution)/shard_map/ppermute | solution.py:73
  805.3 196.7 %reduce-scatter.8.cloned.1.call-start = ((), (), s32[]{:S(2)}) async-start(), calls=%async_computation.18 | async-start | bytes 3932160 | tf_op jit(solution)/shard_map/reduce_scatter | solution.py:689
  857.9 27.2 %collective-permute-start.98 = (bf16[192,1536]{1,0:T(8,128)(2,1)}, bf16[192,1536]{1,0:T(8,128)(2,1)S(1)}, u32[]{:S(2)}, u32[]{:S(2)}) collective-permute-start(bf16[192,1536]{1,0:T(8,128)(2,1)} %get-tuple-element.532), channel_id=1, source_target_pairs={{0,16},{4,20},{8,24},{12,28},{16,0},{20,4},{24,8},{28,12},{1,17},{... | collective-permute-start | bytes 1769480 | tf_op jit(solution)/shard_map/ppermute | solution.py:73
  876.3 349.5 %reduce-scatter.12.cloned.1.call-start = ((), (), s32[]{:S(2)}) async-start(), calls=%async_computation.20 | async-start | bytes 3932160 | tf_op jit(solution)/shard_map/reduce_scatter | solution.py:689
  973.2 53.9 %collective-permute-start.113 = (bf16[384,1536]{1,0:T(8,128)(2,1)}, bf16[384,1536]{1,0:T(8,128)(2,1)}, u32[]{:S(2)}, u32[]{:S(2)}) collective-permute-start(bf16[384,1536]{1,0:T(8,128)(2,1)} %pad_maximum_fusion.45), channel_id=1, source_target_pairs={{0,8},{4,12},{8,0},{12,4},{16,24},{20,28},{24,16},{28,20},{1,9},{5... | collective-permute-start | bytes 3538952 | tf_op jit(solution)/shard_map/ppermute | solution.py:73
  975.3 51.8 %collective-permute-start.112 = (bf16[384,1536]{1,0:T(8,128)(2,1)}, bf16[384,1536]{1,0:T(8,128)(2,1)}, u32[]{:S(2)}, u32[]{:S(2)}) collective-permute-start(bf16[384,1536]{1,0:T(8,128)(2,1)} %pad_maximum_fusion.44), channel_id=1, source_target_pairs={{0,16},{4,20},{8,24},{12,28},{16,0},{20,4},{24,8},{28,12},{1,17},{... | collective-permute-start | bytes 3538952 | tf_op jit(solution)/shard_map/ppermute | solution.py:73
  1046.4 184.8 %reduce-scatter.10.cloned.1.call-start = ((), (), s32[]{:S(2)}) async-start(), calls=%async_computation.19 | async-start | bytes 5898240 | tf_op jit(solution)/shard_map/reduce_scatter | solution.py:689
  1119.0 28.5 %collective-permute-start.122 = (bf16[192,1536]{1,0:T(8,128)(2,1)}, bf16[192,1536]{1,0:T(8,128)(2,1)}, u32[]{:S(2)}, u32[]{:S(2)}) collective-permute-start(bf16[192,1536]{1,0:T(8,128)(2,1)} %get-tuple-element.614), channel_id=1, source_target_pairs={{0,16},{4,20},{8,24},{12,28},{16,0},{20,4},{24,8},{28,12},{1,17},{... | collective-permute-start | bytes 1769480 | tf_op jit(solution)/shard_map/ppermute | solution.py:73
  1120.1 27.5 %collective-permute-start.123 = (bf16[192,1536]{1,0:T(8,128)(2,1)}, bf16[192,1536]{1,0:T(8,128)(2,1)}, u32[]{:S(2)}, u32[]{:S(2)}) collective-permute-start(bf16[192,1536]{1,0:T(8,128)(2,1)} %get-tuple-element.615), channel_id=1, source_target_pairs={{0,8},{4,12},{8,0},{12,4},{16,24},{20,28},{24,16},{28,20},{1,9},{5... | collective-permute-start | bytes 1769480 | tf_op jit(solution)/shard_map/ppermute | solution.py:73
  1135.0 92.7 %all-to-all-start.6 = ((bf16[4,192,1280]{2,1,0:T(8,128)(2,1)}), bf16[4,192,1280]{2,1,0:T(8,128)(2,1)}, u32[]{:S(2)}, u32[]{:S(2)}) async-start(bf16[4,192,1280]{2,1,0:T(8,128)(2,1)} %pad_maximum_fusion.35), calls=%async_computation.8 | async-start | bytes 3932160 | tf_op jit(solution)/shard_map/all_to_all | solution.py:79
  1139.4 152.9 %reduce-scatter.14.cloned.1.call-start = ((), (), s32[]{:S(2)}) async-start(), calls=%async_computation.21 | async-start | bytes 2949120 | tf_op jit(solution)/shard_map/reduce_scatter | solution.py:689
  1144.8 27.8 %collective-permute-start.131 = (bf16[8,24576]{1,0:T(8,128)(2,1)}, bf16[8,24576]{1,0:T(8,128)(2,1)S(1)}, u32[]{:S(2)}, u32[]{:S(2)}) collective-permute-start(bf16[8,24576]{1,0:T(8,128)(2,1)} %reshape.753), channel_id=1, source_target_pairs={{0,8},{4,12},{8,0},{12,4},{16,24},{20,28},{24,16},{28,20},{1,9},{5... | collective-permute-start | bytes 1179656 | tf_op jit(solution)/shard_map/ppermute | solution.py:73
  1146.0 28.2 %collective-permute-start.132 = (bf16[8,24576]{1,0:T(8,128)(2,1)}, bf16[8,24576]{1,0:T(8,128)(2,1)}, u32[]{:S(2)}, u32[]{:S(2)}) collective-permute-start(bf16[8,24576]{1,0:T(8,128)(2,1)} %reshape.753), channel_id=1, source_target_pairs={{0,16},{4,20},{8,24},{12,28},{16,0},{20,4},{24,8},{28,12},{1,17},{... | collective-permute-start | bytes 1179656 | tf_op jit(solution)/shard_map/ppermute | solution.py:73
  1151.2 59.4 %collective-permute-start.136 = (bf16[384,1536]{1,0:T(8,128)(2,1)}, bf16[384,1536]{1,0:T(8,128)(2,1)}, u32[]{:S(2)}, u32[]{:S(2)}) collective-permute-start(bf16[384,1536]{1,0:T(8,128)(2,1)} %pad_maximum_fusion.47), channel_id=1, source_target_pairs={{0,8},{4,12},{8,0},{12,4},{16,24},{20,28},{24,16},{28,20},{1,9},{5... | collective-permute-start | bytes 3538952 | tf_op jit(solution)/shard_map/ppermute | solution.py:73
  1154.2 56.4 %collective-permute-start.135 = (bf16[384,1536]{1,0:T(8,128)(2,1)}, bf16[384,1536]{1,0:T(8,128)(2,1)}, u32[]{:S(2)}, u32[]{:S(2)}) collective-permute-start(bf16[384,1536]{1,0:T(8,128)(2,1)} %pad_maximum_fusion.46), channel_id=1, source_target_pairs={{0,16},{4,20},{8,24},{12,28},{16,0},{20,4},{24,8},{28,12},{1,17},{... | collective-permute-start | bytes 3538952 | tf_op jit(solution)/shard_map/ppermute | solution.py:73
  1172.7 29.0 %collective-permute-start.133 = (bf16[4,24576]{1,0:T(4,128)(2,1)S(1)}, bf16[4,24576]{1,0:T(4,128)(2,1)S(1)}, u32[]{:S(2)}, u32[]{:S(2)}) collective-permute-start(bf16[4,24576]{1,0:T(4,128)(2,1)S(1)} %slice.884), channel_id=1, source_target_pairs={{0,16},{4,20},{8,24},{12,28},{16,0},{20,4},{24,8},{28,12},{1,17},{... | collective-permute-start | bytes 589832 | tf_op jit(solution)/shard_map/ppermute | solution.py:73
  1175.3 27.3 %collective-permute-start.134 = (bf16[4,24576]{1,0:T(4,128)(2,1)S(1)}, bf16[4,24576]{1,0:T(4,128)(2,1)S(1)}, u32[]{:S(2)}, u32[]{:S(2)}) collective-permute-start(bf16[4,24576]{1,0:T(4,128)(2,1)S(1)} %slice.885), channel_id=1, source_target_pairs={{0,8},{4,12},{8,0},{12,4},{16,24},{20,28},{24,16},{28,20},{1,9},{5... | collective-permute-start | bytes 589832 | tf_op jit(solution)/shard_map/ppermute | solution.py:73
  1178.0 53.2 %collective-permute-start.124 = (bf16[64,1536]{1,0:T(8,128)(2,1)}, bf16[64,1536]{1,0:T(8,128)(2,1)}, u32[]{:S(2)}, u32[]{:S(2)}) collective-permute-start(bf16[64,1536]{1,0:T(8,128)(2,1)} %get-tuple-element.880), channel_id=1, source_target_pairs={{0,1},{1,0},{2,3},{3,2},{4,5},{5,4},{6,7},{7,6},{8,9},{9,8},{10,11... | collective-permute-start | bytes 589832 | tf_op jit(solution)/shard_map/ppermute | solution.py:161
  1201.7 29.6 %collective-permute-start.125 = (bf16[64,1536]{1,0:T(8,128)(2,1)}, bf16[64,1536]{1,0:T(8,128)(2,1)}, u32[]{:S(2)}, u32[]{:S(2)}) collective-permute-start(bf16[64,1536]{1,0:T(8,128)(2,1)} %get-tuple-element.879), channel_id=1, source_target_pairs={{0,2},{1,3},{2,0},{3,1},{4,6},{5,7},{6,4},{7,5},{8,10},{9,11},{10,... | collective-permute-start | bytes 589832 | tf_op jit(solution)/shard_map/ppermute | solution.py:161
  1202.6 28.6 %collective-permute-start.126 = (bf16[64,1536]{1,0:T(8,128)(2,1)}, bf16[64,1536]{1,0:T(8,128)(2,1)}, u32[]{:S(2)}, u32[]{:S(2)}) collective-permute-start(bf16[64,1536]{1,0:T(8,128)(2,1)} %get-tuple-element.878), channel_id=1, source_target_pairs={{0,3},{1,2},{2,1},{3,0},{4,7},{5,6},{6,5},{7,4},{8,11},{9,10},{10,... | collective-permute-start | bytes 589832 | tf_op jit(solution)/shard_map/ppermute | solution.py:161
  (412 other events, 3975.1 us)
Sparse Core Ops, SparseCore 0:
  67.8 71.4 all-gather.16
  141.4 33.4 all-gather.18
  177.0 49.3 all-gather.22
  228.3 49.2 all-gather.20
  303.3 64.7 all-gather.24
  376.4 31.7 all-gather.26
  469.2 51.7 all-gather.28
  523.1 49.2 all-gather.30
  805.4 83.2 reduce-scatter.5
  890.9 60.7 reduce-scatter.7
  1046.6 58.4 reduce-scatter.11
  1107.2 96.0 reduce-scatter.9
  1227.8 45.2 reduce-scatter.13

commit v5 on v4

--- a/solution.py
+++ b/solution.py
@@ -234,12 +234,21 @@
         target[pl.ds(goal, small), :] = block[pl.ds(start, small), :]
 
 
-def causal_block(scores_t, size):
-    keys = lax.broadcasted_iota(jnp.int32, (size, size), 0)
-    asks = lax.broadcasted_iota(jnp.int32, (size, size), 1)
-    last = scores_t.shape[0] - size
-    edge = jnp.where(keys <= asks, scores_t[last:], NEG)
-    return edge if last == 0 else jnp.concatenate([scores_t[:last], edge], axis=0)
+def causal_spans(low, high):
+    return ([(0, low, False)] if low else []) + [(low, high, True)]
+
+
+def causal_scores(keys, asks, masked):
+    scores = dot_nt(keys, asks)
+    if not masked:
+        return scores
+    key_ids = lax.broadcasted_iota(jnp.int32, scores.shape, 0)
+    ask_ids = lax.broadcasted_iota(jnp.int32, scores.shape, 1)
+    return jnp.where(key_ids <= ask_ids, scores, NEG)
+
+
+def summed(terms):
+    return functools.reduce(lambda left, right: left + right, terms)
 
 
 def dot_nt(left, right):
@@ -269,11 +278,15 @@
         outs = []
         for h in heads:
             asks = clip[low:high, lanes(0, h)] * BF(SCALE)
-            scores = causal_block(dot_nt(keys[h][:high], asks), size)
-            top = jnp.max(scores, axis=0, keepdims=True)
-            weight = jnp.exp(scores - top)
-            total = jnp.sum(weight, axis=0, keepdims=True)
-            outs.append(dot_nn(values_t[h][:, :high], weight.astype(BF)) / total)
+            spans = causal_spans(low, high)
+            scores = [causal_scores(keys[h][start:end], asks, masked) for start, end, masked in spans]
+            top = functools.reduce(jnp.maximum, [jnp.max(part, axis=0, keepdims=True) for part in scores])
+            weights = [jnp.exp(part - top) for part in scores]
+            total = summed([jnp.sum(part, axis=0, keepdims=True) for part in weights])
+            out = summed(
+                [dot_nn(values_t[h][:, start:end], part.astype(BF)) for (start, end, _), part in zip(spans, weights)]
+            )
+            outs.append(out / total)
             sums_ref[h : h + 1, low:high] = top + jnp.log(total)
         both = outs[0] if len(outs) == 1 else jnp.concatenate(outs, axis=0)
         block[...] = both.T.astype(BF)
@@ -298,20 +311,24 @@
         for h in heads:
             asks = clip[low:high, lanes(0, h)] * BF(SCALE)
             da = da_clip[low:high, lanes(0, h)]
-            scores = causal_block(dot_nt(keys[h][:high], asks), size)
-            probs = jnp.exp(scores - sums_ref[h : h + 1, low:high])
-            d_probs = dot_nt(values[h][:high], da)
-            inner = jnp.sum(probs * d_probs, axis=0, keepdims=True)
-            d_scores = (probs * (d_probs - inner)).astype(BF)
-            dk = dot_nn(d_scores, asks)
-            dv = dot_nn(probs.astype(BF), da)
-            if k == grid.C - 1:
-                acc[:, lanes(0, h)] = dk
-                acc[:, lanes(1, h)] = dv
-            else:
-                acc[:high, lanes(0, h)] += dk
-                acc[:high, lanes(1, h)] += dv
-            dq.append(dot_nn(keys_t[h][:, :high], d_scores) * SCALE)
+            spans = causal_spans(low, high)
+            sums = sums_ref[h : h + 1, low:high]
+            probs = [jnp.exp(causal_scores(keys[h][start:end], asks, masked) - sums) for start, end, masked in spans]
+            d_probs = [dot_nt(values[h][start:end], da) for start, end, _ in spans]
+            inner = summed([jnp.sum(p * d, axis=0, keepdims=True) for p, d in zip(probs, d_probs)])
+            terms = []
+            for (start, end, _), p, d in zip(spans, probs, d_probs):
+                d_scores = (p * (d - inner)).astype(BF)
+                dk = dot_nn(d_scores, asks)
+                dv = dot_nn(p.astype(BF), da)
+                if k == grid.C - 1:
+                    acc[start:end, lanes(0, h)] = dk
+                    acc[start:end, lanes(1, h)] = dv
+                else:
+                    acc[start:end, lanes(0, h)] += dk
+                    acc[start:end, lanes(1, h)] += dv
+                terms.append(dot_nn(keys_t[h][:, start:end], d_scores))
+            dq.append(summed(terms) * SCALE)
         both = dq[0] if len(dq) == 1 else jnp.concatenate(dq, axis=0)
         block[:, :width] = both.T.astype(BF)
         block[:, width:] = acc[low:high, :].astype(BF)

time: 1310 us -> 1310 us (level)
  transfers between devices with their start and end apart: 167 -> 167, of which waited for: 65 -> 64; matrix products, arithmetic and copies ran while one was open for 25% -> 25% of each run, Pallas kernels for 24% -> 23%
where the time goes in v5:
time: 1310 us; the launch traced here: 1300 us
  waiting for transfers between devices  384 us (29%)
  Pallas kernels  305 us (23%)
  starting transfers between devices  205 us (16%)
  local copies, waits for them, and re-layouts  189 us (14%)
  other arithmetic  170 us (13%)
  matrix products  29 us (2%)
  between operations  18.8 us (1%)
    ppermute x101, waiting for transfers between devices, swap(): return lax.ppermute(value, 'row', [(r, r ^ 2 * d) for r in range(self.R)])  293 us
    ppermute x101, starting transfers between devices, swap(): return lax.ppermute(value, 'row', [(r, r ^ 2 * d) for r in range(self.R)])  108 us
    pallas_call x16, Pallas kernels, rows_product(): pl.pallas_call(functools.partial(rows_kernel, (0,) if len(mats) == 1 else...  80.4 us
    pallas_call x8, Pallas kernels, weight_grads(): pl.pallas_call(functools.partial(grads_kernel, len(pieces)), grid=(blocks...  68.5 us
    pallas_call x8, Pallas kernels, columns_product(): pl.pallas_call(functools.partial(columns_kernel, (0,) if len(mats) == 1 e...  64.5 us
    unnamed x594, local copies, waits for them, and re-layouts  47.1 us
    pallas_call x2, Pallas kernels, self_attention_grad(): pl.pallas_call(functools.partial(self_backward_kernel, grid, width), grid...  34.4 us
    all_to_all x7, waiting for transfers between devices, plane_a2a(): lax.all_to_all(value, 'row', 0, 0, tiled=True, axis_index_groups=self.gro...  28.2 us
  transfers between devices with their start and end apart: 167, of which 64 were waited for; matrix products, arithmetic and copies ran while one was open for 25% of the time, Pallas kernels for 23%

profile of v5, /device:TPU:0, one launch (start us, length us, event | category | flops | bytes accessed | tf_op | source)
XLA Modules:
  0.0 1300.4 jit_solution(14269123854279671890)
XLA Ops:
  22.9 12.9 collective-permute-done.1
  42.4 8.3 collective-permute-done.3
  50.7 15.0 %collective-permute-done.4 = bf16[64,3072]{1,0:T(8,128)(2,1)S(1)} collective-permute-done((bf16[64,3072]{1,0:T(8,128)(2,1)}, bf16[64,3072]{1,0:T(8,128)(2,1)S(1)}, u32[]{:S(2)}, u32[]{:S(2)}) %collective-permute-start.4) | collective-permute-done | bytes 393248 | tf_op jit(solution)/shard_map/ppermute | solution.py:161
  85.3 6.8 all-to-all-done.1
  92.1 8.9 collective-permute-start.10
  148.1 6.6 collective-permute-start.13
  171.9 7.0 columns_plain.4.x_ref
  185.9 10.4 self_attention.2
  229.3 8.7 collective-permute-done.23
  254.5 11.5 collective-permute-done.22
  275.8 9.6 all-to-all-done.4
  311.9 11.6 collective-permute-done.31.refs_1_
  337.6 7.1 collective-permute-done.33.refs_3_
  344.8 11.7 columns_gelu.2
  362.3 8.4 rows.19
  378.1 11.8 collective-permute-done.39
  402.7 17.2 %collective-permute-done.40.refs_1_ = bf16[256,1536]{1,0:T(8,128)(2,1)S(1)} collective-permute-done((bf16[256,1536]{1,0:T(8,128)(2,1)S(1)}, bf16[256,1536]{1,0:T(8,128)(2,1)S(1)}, u32[]{:S(2)}, u32[]{:S(2)}) %collective-permute-start.40) | collective-permute-done | bytes 786464 | tf_op jit(solution)/shard_map/ppermute | solution.py:73
  439.1 7.1 columns_plain.5.x_ref
  446.2 10.4 self_attention.3
  468.5 7.3 collective-permute-done.51
  504.9 11.3 collective-permute-done.50
  542.0 17.9 %collective-permute-done.58.refs_1_ = bf16[256,1536]{1,0:T(8,128)(2,1)S(1)} collective-permute-done((bf16[256,1536]{1,0:T(8,128)(2,1)S(1)}, bf16[256,1536]{1,0:T(8,128)(2,1)S(1)}, u32[]{:S(2)}, u32[]{:S(2)}) %collective-permute-start.58) | collective-permute-done | bytes 786464 | tf_op jit(solution)/shard_map/ppermute | solution.py:73
  562.0 8.6 collective-permute-done.60.refs_3_
  571.6 10.5 columns_gelu.3
  598.1 8.4 rows.23
  610.1 10.4 columns_slope.2.act_ref.refs_5_
  626.5 8.5 rows.25
  641.5 10.6 weight_grads.9
  653.6 10.6 weight_grads.8
  693.0 14.5 %collective-permute-done.72.refs_1_ = bf16[256,1536]{1,0:T(8,128)(2,1)S(1)} collective-permute-done((bf16[256,1536]{1,0:T(8,128)(2,1)S(1)}, bf16[256,1536]{1,0:T(8,128)(2,1)S(1)}, u32[]{:S(2)}, u32[]{:S(2)}) %collective-permute-start.72) | collective-permute-done | bytes 786464 | tf_op jit(solution)/shard_map/ppermute | solution.py:73
  731.5 17.3 %self_attention_grad.2.act_ref.refs_5_ = bf16[3,1024,384]{2,1,0:T(8,128)(2,1)S(1)} custom-call(s32[2]{0:T(128)S(1)} %pad_add_fusion.at_ref, bf16[3,1024,384]{2,1,0:T(8,128)(2,1)S(1)} %copy-done.121, bf16[3,1024,128]{2,1,0:T(8,128)(2,1)S(1)} %columns_plain.6.da_ref, f32[3,8,1024]{2,1,0:T(8,128)S(1)} %copy-done.125), custom_call_target="tpu_custom_call" | custom-call | flops 9663676416 | bytes 6291456 | tf_op jit(solution)/shard_map/self_attention_grad/pallas_call | solution.py:370
  755.6 6.9 rows.27
  766.1 7.2 collective-permute-done.79
  795.0 8.6 weight_grads.10
  836.4 8.3 collective-permute-done.90.refs_1_
  858.6 9.7 columns_slope.3.act_ref.refs_5_
  875.3 8.4 rows.29
  888.3 10.1 weight_grads.13
  898.5 11.2 weight_grads.12
  942.5 17.0 %collective-permute-done.104.refs_1_ = bf16[256,1536]{1,0:T(8,128)(2,1)S(1)} collective-permute-done((bf16[256,1536]{1,0:T(8,128)(2,1)S(1)}, bf16[256,1536]{1,0:T(8,128)(2,1)S(1)}, u32[]{:S(2)}, u32[]{:S(2)}) %collective-permute-start.104) | collective-permute-done | bytes 786464 | tf_op jit(solution)/shard_map/ppermute | solution.py:73
  961.9 7.6 collective-permute-done.106.refs_3_
  981.6 17.1 %self_attention_grad.3.refs_5_.act_ref = bf16[3,1024,384]{2,1,0:T(8,128)(2,1)S(1)} custom-call(s32[2]{0:T(128)S(1)} %pad_add_fusion.at_ref, bf16[3,1024,384]{2,1,0:T(8,128)(2,1)S(1)} %copy-done.119, bf16[3,1024,128]{2,1,0:T(8,128)(2,1)S(1)} %columns_plain.7.da_ref, f32[3,8,1024]{2,1,0:T(8,128)S(1)} %copy-done.123), custom_call_target="tpu_custom_call" | custom-call | flops 9663676416 | bytes 6291456 | tf_op jit(solution)/shard_map/self_attention_grad/pallas_call | solution.py:370
  1009.8 8.6 weight_grads.14
  1062.6 6.9 rows.31
  1081.1 9.8 collective-permute-done.119
  1155.8 15.1 %collective-permute-done.131 = bf16[8,24576]{1,0:T(8,128)(2,1)S(1)} collective-permute-done((bf16[8,24576]{1,0:T(8,128)(2,1)}, bf16[8,24576]{1,0:T(8,128)(2,1)S(1)}, u32[]{:S(2)}, u32[]{:S(2)}) %collective-permute-start.131) | collective-permute-done | bytes 393248 | tf_op jit(solution)/shard_map/ppermute | solution.py:73
  1178.9 21.2 %collective-permute-done.133 = bf16[4,24576]{1,0:T(4,128)(2,1)S(1)} collective-permute-done((bf16[4,24576]{1,0:T(4,128)(2,1)S(1)}, bf16[4,24576]{1,0:T(4,128)(2,1)S(1)}, u32[]{:S(2)}, u32[]{:S(2)}) %collective-permute-start.133) | collective-permute-done | bytes 196640 | tf_op jit(solution)/shard_map/ppermute | solution.py:73
  1253.9 7.3 all-to-all-done.8
  (1312 shorter events, 773.8 us)
Async XLA Ops:
  22.9 141.5 %all-gather.17.cloned.1.call-start = ((), (), s32[]{:S(2)}) async-start(), calls=%async_computation.22 | async-start | bytes 3932160 | tf_op jit(solution)/shard_map/all_gather | solution.py:853
  38.4 27.4 %collective-permute-start.4 = (bf16[64,3072]{1,0:T(8,128)(2,1)}, bf16[64,3072]{1,0:T(8,128)(2,1)S(1)}, u32[]{:S(2)}, u32[]{:S(2)}) collective-permute-start(bf16[64,3072]{1,0:T(8,128)(2,1)} %get-tuple-element.844), channel_id=1, source_target_pairs={{0,2},{1,3},{2,0},{3,1},{4,6},{5,7},{6,4},{7,5},{8,10},{9,11},{10,... | collective-permute-start | bytes 1179656 | tf_op jit(solution)/shard_map/ppermute | solution.py:161
  78.2 36.1 %collective-permute-start.6 = (bf16[256,1536]{1,0:T(8,128)(2,1)S(1)}, bf16[256,1536]{1,0:T(8,128)(2,1)S(1)}, u32[]{:S(2)}, u32[]{:S(2)}) collective-permute-start(bf16[256,1536]{1,0:T(8,128)(2,1)S(1)} %fusion.27.refs_0_), channel_id=1, source_target_pairs={{0,8},{4,12},{8,0},{12,4},{16,24},{20,28},{24,16},{28,20},{1,9},{5... | collective-permute-start | bytes 2359304 | tf_op jit(solution)/shard_map/ppermute | solution.py:73
  79.0 35.3 %collective-permute-start.7 = (bf16[256,1536]{1,0:T(8,128)(2,1)S(1)}, bf16[256,1536]{1,0:T(8,128)(2,1)S(1)}, u32[]{:S(2)}, u32[]{:S(2)}) collective-permute-start(bf16[256,1536]{1,0:T(8,128)(2,1)S(1)} %fusion.27.refs_0_), channel_id=1, source_target_pairs={{0,16},{4,20},{8,24},{12,28},{16,0},{20,4},{24,8},{28,12},{1,17},{... | collective-permute-start | bytes 2359304 | tf_op jit(solution)/shard_map/ppermute | solution.py:73
  120.6 59.7 %all-gather.19.cloned.1.call-start = ((), (), s32[]{:S(2)}) async-start(), calls=%async_computation.23 | async-start | bytes 1474560 | tf_op jit(solution)/shard_map/all_gather | solution.py:876
  145.7 123.6 %all-gather.23.cloned.1.call-start = ((), (), s32[]{:S(2)}) async-start(), calls=%async_computation.25 | async-start | bytes 2949120 | tf_op jit(solution)/shard_map/all_gather | solution.py:694
  168.9 118.6 %all-gather.21.cloned.1.call-start = ((), (), s32[]{:S(2)}) async-start(), calls=%async_computation.24 | async-start | bytes 2949120 | tf_op jit(solution)/shard_map/all_gather | solution.py:694
  182.7 29.1 %collective-permute-start.17 = (bf16[384,1536]{1,0:T(8,128)(2,1)S(1)}, bf16[384,1536]{1,0:T(8,128)(2,1)}, u32[]{:S(2)}, u32[]{:S(2)}) collective-permute-start(bf16[384,1536]{1,0:T(8,128)(2,1)S(1)} %bitcast.445), channel_id=1, source_target_pairs={{0,8},{4,12},{8,0},{12,4},{16,24},{20,28},{24,16},{28,20},{1,9},{5... | collective-permute-start | bytes 3538952 | tf_op jit(solution)/shard_map/ppermute | solution.py:73
  184.5 29.0 %collective-permute-start.18 = (bf16[384,1536]{1,0:T(8,128)(2,1)S(1)}, bf16[384,1536]{1,0:T(8,128)(2,1)}, u32[]{:S(2)}, u32[]{:S(2)}) collective-permute-start(bf16[384,1536]{1,0:T(8,128)(2,1)S(1)} %bitcast.446), channel_id=1, source_target_pairs={{0,16},{4,20},{8,24},{12,28},{16,0},{20,4},{24,8},{28,12},{1,17},{... | collective-permute-start | bytes 3538952 | tf_op jit(solution)/shard_map/ppermute | solution.py:73
  198.7 46.1 %collective-permute-start.21 = (bf16[128,1536]{1,0:T(8,128)(2,1)S(1)}, bf16[128,1536]{1,0:T(8,128)(2,1)}, u32[]{:S(2)}, u32[]{:S(2)}) collective-permute-start(bf16[128,1536]{1,0:T(8,128)(2,1)S(1)} %get-tuple-element.343), channel_id=1, source_target_pairs={{0,16},{4,20},{8,24},{12,28},{16,0},{20,4},{24,8},{28,12},{1,17},{... | collective-permute-start | bytes 1179656 | tf_op jit(solution)/shard_map/ppermute | solution.py:73
  217.7 30.1 %collective-permute-start.19 = (bf16[128,1536]{1,0:T(8,128)(2,1)S(1)}, bf16[128,1536]{1,0:T(8,128)(2,1)S(1)}, u32[]{:S(2)}, u32[]{:S(2)}) collective-permute-start(bf16[128,1536]{1,0:T(8,128)(2,1)S(1)} %get-tuple-element.344), channel_id=1, source_target_pairs={{0,8},{4,12},{8,0},{12,4},{16,24},{20,28},{24,16},{28,20},{1,9},{5... | collective-permute-start | bytes 1179656 | tf_op jit(solution)/shard_map/ppermute | solution.py:73
  243.8 43.7 %collective-permute-start.25 = (bf16[2,768,1536]{2,1,0:T(8,128)(2,1)}, bf16[2,768,1536]{2,1,0:T(8,128)(2,1)}, u32[]{:S(2)}, u32[]{:S(2)}) collective-permute-start(bf16[2,768,1536]{2,1,0:T(8,128)(2,1)} %bitcast.53), channel_id=1, source_target_pairs={{0,4},{4,0},{8,12},{12,8},{16,20},{20,16},{24,28},{28,24},{1,5},{5... | collective-permute-start | bytes 14155784 | tf_op jit(solution)/shard_map/ppermute | solution.py:76
  269.2 75.5 %collective-permute-start.35 = (bf16[4,1,768,384]{3,2,1,0:T(8,128)(2,1)}, bf16[4,1,768,384]{3,2,1,0:T(8,128)(2,1)}, u32[]{:S(2)}, u32[]{:S(2)}) collective-permute-start(bf16[4,1,768,384]{3,2,1,0:T(8,128)(2,1)} %bitcast.415), channel_id=1, source_target_pairs={{0,4},{4,0},{8,12},{12,8},{16,20},{20,16},{24,28},{28,24},{1,5},{5... | collective-permute-start | bytes 7077896 | tf_op jit(solution)/shard_map/ppermute | solution.py:76
  273.7 122.2 %all-gather.25.cloned.1.call-start = ((), (), s32[]{:S(2)}) async-start(), calls=%async_computation.26 | async-start | bytes 3932160 | tf_op jit(solution)/shard_map/all_gather | solution.py:912
  304.2 27.1 %collective-permute-start.32 = (bf16[256,1536]{1,0:T(8,128)(2,1)}, bf16[256,1536]{1,0:T(8,128)(2,1)}, u32[]{:S(2)}, u32[]{:S(2)}) collective-permute-start(bf16[256,1536]{1,0:T(8,128)(2,1)} %add_convert_fusion.16.refs_0_), channel_id=1, source_target_pairs={{0,16},{4,20},{8,24},{12,28},{16,0},{20,4},{24,8},{28,12},{1,17},{... | collective-permute-start | bytes 2359304 | tf_op jit(solution)/shard_map/ppermute | solution.py:73
  307.4 30.2 %all-to-all-start.5 = ((bf16[4,2,192,384]{3,2,1,0:T(8,128)(2,1)}), bf16[4,2,192,384]{3,2,1,0:T(8,128)(2,1)}, u32[]{:S(2)}, u32[]{:S(2)}) async-start(bf16[4,2,192,384]{3,2,1,0:T(8,128)(2,1)} %copy.131), calls=%async_computation.5 | async-start | bytes 2359296 | tf_op jit(solution)/shard_map/all_to_all | solution.py:79
  311.9 113.4 %all-gather.27.cloned.1.call-start = ((), (), s32[]{:S(2)}) async-start(), calls=%async_computation.27 | async-start | bytes 1474560 | tf_op jit(solution)/shard_map/all_gather | solution.py:913
  375.6 146.4 %all-gather.29.cloned.1.call-start = ((), (), s32[]{:S(2)}) async-start(), calls=%async_computation.28 | async-start | bytes 2949120 | tf_op jit(solution)/shard_map/all_gather | solution.py:694
  398.0 41.1 %collective-permute-start.44 = (bf16[3,4,768,128]{3,2,1,0:T(8,128)(2,1)S(1)}, bf16[3,4,768,128]{3,2,1,0:T(8,128)(2,1)}, u32[]{:S(2)}, u32[]{:S(2)}) collective-permute-start(bf16[3,4,768,128]{3,2,1,0:T(8,128)(2,1)S(1)} %pad_maximum_fusion.33.refs_5_.own_ref), channel_id=1, source_target_pairs={{0,4},{4,0},{8,12},{12,8},{16,20},{20,16},{24,28},{28,24},{1,5},{5... | collective-permute-start | bytes 7077896 | tf_op jit(solution)/shard_map/ppermute | solution.py:76
  468.4 116.0 %all-gather.31.cloned.1.call-start = ((), (), s32[]{:S(2)}) async-start(), calls=%async_computation.29 | async-start | bytes 2949120 | tf_op jit(solution)/shard_map/all_gather | solution.py:694
  483.0 41.2 %collective-permute-start.53 = (bf16[2,768,1536]{2,1,0:T(8,128)(2,1)}, bf16[2,768,1536]{2,1,0:T(8,128)(2,1)}, u32[]{:S(2)}, u32[]{:S(2)}) collective-permute-start(bf16[2,768,1536]{2,1,0:T(8,128)(2,1)} %bitcast.87), channel_id=1, source_target_pairs={{0,4},{4,0},{8,12},{12,8},{16,20},{20,16},{24,28},{28,24},{1,5},{5... | collective-permute-start | bytes 14155784 | tf_op jit(solution)/shard_map/ppermute | solution.py:76
  499.5 414.2 %reduce-scatter.6.cloned.1.call-start = ((), (), s32[]{:S(2)}) async-start(), calls=%async_computation.17 | async-start | bytes 5898240 | tf_op jit(solution)/shard_map/reduce_scatter | solution.py:706
  521.9 40.1 %collective-permute-start.62 = (bf16[4,1,768,384]{3,2,1,0:T(8,128)(2,1)}, bf16[4,1,768,384]{3,2,1,0:T(8,128)(2,1)S(1)}, u32[]{:S(2)}, u32[]{:S(2)}) collective-permute-start(bf16[4,1,768,384]{3,2,1,0:T(8,128)(2,1)} %bitcast.423), channel_id=1, source_target_pairs={{0,4},{4,0},{8,12},{12,8},{16,20},{20,16},{24,28},{28,24},{1,5},{5... | collective-permute-start | bytes 7077896 | tf_op jit(solution)/shard_map/ppermute | solution.py:76
  596.2 41.1 %collective-permute-start.68 = (bf16[128,1536]{1,0:T(8,128)(2,1)}, bf16[128,1536]{1,0:T(8,128)(2,1)S(1)}, u32[]{:S(2)}, u32[]{:S(2)}) collective-permute-start(bf16[128,1536]{1,0:T(8,128)(2,1)} %get-tuple-element.422), channel_id=1, source_target_pairs={{0,16},{4,20},{8,24},{12,28},{16,0},{20,4},{24,8},{28,12},{1,17},{... | collective-permute-start | bytes 1179656 | tf_op jit(solution)/shard_map/ppermute | solution.py:73
  597.2 40.2 %collective-permute-start.69 = (bf16[128,1536]{1,0:T(8,128)(2,1)}, bf16[128,1536]{1,0:T(8,128)(2,1)S(1)}, u32[]{:S(2)}, u32[]{:S(2)}) collective-permute-start(bf16[128,1536]{1,0:T(8,128)(2,1)} %get-tuple-element.423), channel_id=1, source_target_pairs={{0,8},{4,12},{8,0},{12,4},{16,24},{20,28},{24,16},{28,20},{1,9},{5... | collective-permute-start | bytes 1179656 | tf_op jit(solution)/shard_map/ppermute | solution.py:73
  692.5 73.6 %collective-permute-start.86 = (bf16[4,768,384]{2,1,0:T(8,128)(2,1)}, bf16[4,768,384]{2,1,0:T(8,128)(2,1)}, u32[]{:S(2)}, u32[]{:S(2)}) collective-permute-start(bf16[4,768,384]{2,1,0:T(8,128)(2,1)} %get-tuple-element.500), channel_id=1, source_target_pairs={{0,4},{4,0},{8,12},{12,8},{16,20},{20,16},{24,28},{28,24},{1,5},{5... | collective-permute-start | bytes 7077896 | tf_op jit(solution)/shard_map/ppermute | solution.py:76
  692.5 80.8 %collective-permute-start.87 = (bf16[4,768,384]{2,1,0:T(8,128)(2,1)}, bf16[4,768,384]{2,1,0:T(8,128)(2,1)}, u32[]{:S(2)}, u32[]{:S(2)}) collective-permute-start(bf16[4,768,384]{2,1,0:T(8,128)(2,1)} %get-tuple-element.503), channel_id=1, source_target_pairs={{0,4},{4,0},{8,12},{12,8},{16,20},{20,16},{24,28},{28,24},{1,5},{5... | collective-permute-start | bytes 7077896 | tf_op jit(solution)/shard_map/ppermute | solution.py:76
  720.1 28.7 %collective-permute-start.76 = (bf16[64,1536]{1,0:T(8,128)(2,1)S(1)}, bf16[64,1536]{1,0:T(8,128)(2,1)S(1)}, u32[]{:S(2)}, u32[]{:S(2)}) collective-permute-start(bf16[64,1536]{1,0:T(8,128)(2,1)S(1)} %get-tuple-element.896), channel_id=1, source_target_pairs={{0,1},{1,0},{2,3},{3,2},{4,5},{5,4},{6,7},{7,6},{8,9},{9,8},{10,11... | collective-permute-start | bytes 589832 | tf_op jit(solution)/shard_map/ppermute | solution.py:161
  774.4 29.1 %collective-permute-start.82 = (bf16[256,1536]{1,0:T(8,128)(2,1)}, bf16[256,1536]{1,0:T(8,128)(2,1)}, u32[]{:S(2)}, u32[]{:S(2)}) collective-permute-start(bf16[256,1536]{1,0:T(8,128)(2,1)} %pad_maximum_fusion.61), channel_id=1, source_target_pairs={{0,8},{4,12},{8,0},{12,4},{16,24},{20,28},{24,16},{28,20},{1,9},{5... | collective-permute-start | bytes 2359304 | tf_op jit(solution)/shard_map/ppermute | solution.py:73
  803.6 196.5 %reduce-scatter.8.cloned.1.call-start = ((), (), s32[]{:S(2)}) async-start(), calls=%async_computation.18 | async-start | bytes 3932160 | tf_op jit(solution)/shard_map/reduce_scatter | solution.py:706
  856.5 27.2 %collective-permute-start.98 = (bf16[192,1536]{1,0:T(8,128)(2,1)}, bf16[192,1536]{1,0:T(8,128)(2,1)S(1)}, u32[]{:S(2)}, u32[]{:S(2)}) collective-permute-start(bf16[192,1536]{1,0:T(8,128)(2,1)} %get-tuple-element.532), channel_id=1, source_target_pairs={{0,16},{4,20},{8,24},{12,28},{16,0},{20,4},{24,8},{28,12},{1,17},{... | collective-permute-start | bytes 1769480 | tf_op jit(solution)/shard_map/ppermute | solution.py:73
  874.9 349.2 %reduce-scatter.12.cloned.1.call-start = ((), (), s32[]{:S(2)}) async-start(), calls=%async_computation.20 | async-start | bytes 3932160 | tf_op jit(solution)/shard_map/reduce_scatter | solution.py:706
  971.4 54.2 %collective-permute-start.113 = (bf16[384,1536]{1,0:T(8,128)(2,1)}, bf16[384,1536]{1,0:T(8,128)(2,1)}, u32[]{:S(2)}, u32[]{:S(2)}) collective-permute-start(bf16[384,1536]{1,0:T(8,128)(2,1)} %pad_maximum_fusion.45), channel_id=1, source_target_pairs={{0,8},{4,12},{8,0},{12,4},{16,24},{20,28},{24,16},{28,20},{1,9},{5... | collective-permute-start | bytes 3538952 | tf_op jit(solution)/shard_map/ppermute | solution.py:73
  973.9 51.7 %collective-permute-start.112 = (bf16[384,1536]{1,0:T(8,128)(2,1)}, bf16[384,1536]{1,0:T(8,128)(2,1)}, u32[]{:S(2)}, u32[]{:S(2)}) collective-permute-start(bf16[384,1536]{1,0:T(8,128)(2,1)} %pad_maximum_fusion.44), channel_id=1, source_target_pairs={{0,16},{4,20},{8,24},{12,28},{16,0},{20,4},{24,8},{28,12},{1,17},{... | collective-permute-start | bytes 3538952 | tf_op jit(solution)/shard_map/ppermute | solution.py:73
  1045.1 184.6 %reduce-scatter.10.cloned.1.call-start = ((), (), s32[]{:S(2)}) async-start(), calls=%async_computation.19 | async-start | bytes 5898240 | tf_op jit(solution)/shard_map/reduce_scatter | solution.py:706
  1117.4 28.5 %collective-permute-start.122 = (bf16[192,1536]{1,0:T(8,128)(2,1)}, bf16[192,1536]{1,0:T(8,128)(2,1)}, u32[]{:S(2)}, u32[]{:S(2)}) collective-permute-start(bf16[192,1536]{1,0:T(8,128)(2,1)} %get-tuple-element.614), channel_id=1, source_target_pairs={{0,16},{4,20},{8,24},{12,28},{16,0},{20,4},{24,8},{28,12},{1,17},{... | collective-permute-start | bytes 1769480 | tf_op jit(solution)/shard_map/ppermute | solution.py:73
  1118.5 27.4 %collective-permute-start.123 = (bf16[192,1536]{1,0:T(8,128)(2,1)}, bf16[192,1536]{1,0:T(8,128)(2,1)}, u32[]{:S(2)}, u32[]{:S(2)}) collective-permute-start(bf16[192,1536]{1,0:T(8,128)(2,1)} %get-tuple-element.615), channel_id=1, source_target_pairs={{0,8},{4,12},{8,0},{12,4},{16,24},{20,28},{24,16},{28,20},{1,9},{5... | collective-permute-start | bytes 1769480 | tf_op jit(solution)/shard_map/ppermute | solution.py:73
  1133.3 92.7 %all-to-all-start.6 = ((bf16[4,192,1280]{2,1,0:T(8,128)(2,1)}), bf16[4,192,1280]{2,1,0:T(8,128)(2,1)}, u32[]{:S(2)}, u32[]{:S(2)}) async-start(bf16[4,192,1280]{2,1,0:T(8,128)(2,1)} %pad_maximum_fusion.35), calls=%async_computation.8 | async-start | bytes 3932160 | tf_op jit(solution)/shard_map/all_to_all | solution.py:79
  1137.8 152.9 %reduce-scatter.14.cloned.1.call-start = ((), (), s32[]{:S(2)}) async-start(), calls=%async_computation.21 | async-start | bytes 2949120 | tf_op jit(solution)/shard_map/reduce_scatter | solution.py:706
  1143.2 27.8 %collective-permute-start.131 = (bf16[8,24576]{1,0:T(8,128)(2,1)}, bf16[8,24576]{1,0:T(8,128)(2,1)S(1)}, u32[]{:S(2)}, u32[]{:S(2)}) collective-permute-start(bf16[8,24576]{1,0:T(8,128)(2,1)} %reshape.753), channel_id=1, source_target_pairs={{0,8},{4,12},{8,0},{12,4},{16,24},{20,28},{24,16},{28,20},{1,9},{5... | collective-permute-start | bytes 1179656 | tf_op jit(solution)/shard_map/ppermute | solution.py:73
  1144.2 28.3 %collective-permute-start.132 = (bf16[8,24576]{1,0:T(8,128)(2,1)}, bf16[8,24576]{1,0:T(8,128)(2,1)}, u32[]{:S(2)}, u32[]{:S(2)}) collective-permute-start(bf16[8,24576]{1,0:T(8,128)(2,1)} %reshape.753), channel_id=1, source_target_pairs={{0,16},{4,20},{8,24},{12,28},{16,0},{20,4},{24,8},{28,12},{1,17},{... | collective-permute-start | bytes 1179656 | tf_op jit(solution)/shard_map/ppermute | solution.py:73
  1149.6 59.4 %collective-permute-start.136 = (bf16[384,1536]{1,0:T(8,128)(2,1)}, bf16[384,1536]{1,0:T(8,128)(2,1)}, u32[]{:S(2)}, u32[]{:S(2)}) collective-permute-start(bf16[384,1536]{1,0:T(8,128)(2,1)} %pad_maximum_fusion.47), channel_id=1, source_target_pairs={{0,8},{4,12},{8,0},{12,4},{16,24},{20,28},{24,16},{28,20},{1,9},{5... | collective-permute-start | bytes 3538952 | tf_op jit(solution)/shard_map/ppermute | solution.py:73
  1152.7 56.3 %collective-permute-start.135 = (bf16[384,1536]{1,0:T(8,128)(2,1)}, bf16[384,1536]{1,0:T(8,128)(2,1)}, u32[]{:S(2)}, u32[]{:S(2)}) collective-permute-start(bf16[384,1536]{1,0:T(8,128)(2,1)} %pad_maximum_fusion.46), channel_id=1, source_target_pairs={{0,16},{4,20},{8,24},{12,28},{16,0},{20,4},{24,8},{28,12},{1,17},{... | collective-permute-start | bytes 3538952 | tf_op jit(solution)/shard_map/ppermute | solution.py:73
  1171.0 29.0 %collective-permute-start.133 = (bf16[4,24576]{1,0:T(4,128)(2,1)S(1)}, bf16[4,24576]{1,0:T(4,128)(2,1)S(1)}, u32[]{:S(2)}, u32[]{:S(2)}) collective-permute-start(bf16[4,24576]{1,0:T(4,128)(2,1)S(1)} %slice.884), channel_id=1, source_target_pairs={{0,16},{4,20},{8,24},{12,28},{16,0},{20,4},{24,8},{28,12},{1,17},{... | collective-permute-start | bytes 589832 | tf_op jit(solution)/shard_map/ppermute | solution.py:73
  1173.6 27.5 %collective-permute-start.134 = (bf16[4,24576]{1,0:T(4,128)(2,1)S(1)}, bf16[4,24576]{1,0:T(4,128)(2,1)S(1)}, u32[]{:S(2)}, u32[]{:S(2)}) collective-permute-start(bf16[4,24576]{1,0:T(4,128)(2,1)S(1)} %slice.885), channel_id=1, source_target_pairs={{0,8},{4,12},{8,0},{12,4},{16,24},{20,28},{24,16},{28,20},{1,9},{5... | collective-permute-start | bytes 589832 | tf_op jit(solution)/shard_map/ppermute | solution.py:73
  1176.4 53.2 %collective-permute-start.124 = (bf16[64,1536]{1,0:T(8,128)(2,1)}, bf16[64,1536]{1,0:T(8,128)(2,1)}, u32[]{:S(2)}, u32[]{:S(2)}) collective-permute-start(bf16[64,1536]{1,0:T(8,128)(2,1)} %get-tuple-element.880), channel_id=1, source_target_pairs={{0,1},{1,0},{2,3},{3,2},{4,5},{5,4},{6,7},{7,6},{8,9},{9,8},{10,11... | collective-permute-start | bytes 589832 | tf_op jit(solution)/shard_map/ppermute | solution.py:161
  1200.0 29.6 %collective-permute-start.125 = (bf16[64,1536]{1,0:T(8,128)(2,1)}, bf16[64,1536]{1,0:T(8,128)(2,1)}, u32[]{:S(2)}, u32[]{:S(2)}) collective-permute-start(bf16[64,1536]{1,0:T(8,128)(2,1)} %get-tuple-element.879), channel_id=1, source_target_pairs={{0,2},{1,3},{2,0},{3,1},{4,6},{5,7},{6,4},{7,5},{8,10},{9,11},{10,... | collective-permute-start | bytes 589832 | tf_op jit(solution)/shard_map/ppermute | solution.py:161
  1201.1 28.5 %collective-permute-start.126 = (bf16[64,1536]{1,0:T(8,128)(2,1)}, bf16[64,1536]{1,0:T(8,128)(2,1)}, u32[]{:S(2)}, u32[]{:S(2)}) collective-permute-start(bf16[64,1536]{1,0:T(8,128)(2,1)} %get-tuple-element.878), channel_id=1, source_target_pairs={{0,3},{1,2},{2,1},{3,0},{4,7},{5,6},{6,5},{7,4},{8,11},{9,10},{10,... | collective-permute-start | bytes 589832 | tf_op jit(solution)/shard_map/ppermute | solution.py:161
  (412 other events, 3978.0 us)
Sparse Core Ops, SparseCore 0:
  67.8 71.4 all-gather.16
  141.4 33.4 all-gather.18
  177.0 49.3 all-gather.22
  228.3 49.2 all-gather.20
  302.8 64.6 all-gather.24
  375.7 31.5 all-gather.26
  468.5 51.5 all-gather.28
  522.2 49.2 all-gather.30
  803.7 83.1 reduce-scatter.5
  889.1 60.7 reduce-scatter.7
  1045.2 58.4 reduce-scatter.11
  1105.8 95.8 reduce-scatter.9
  1226.2 45.2 reduce-scatter.13
